TPU v7x, 256 devices: a whole 4x4x8 slice. The times are simulated.
256 devices in a mesh: demo: 32 (over z, x), fsdp: 2 (over y_hi), sketch: 4 (over y_lo, core).
Axes of the slice: x: 4, y: 4 (y_hi: 2, y_lo: 2; y = y_hi * 2 + y_lo), z: 8, core: 2. Of those that a mesh axis runs over, the one named last changes fastest.
Arguments:
- activations: bfloat16 [128, 512, 8192], P('demo', 'sketch', 'fsdp'), may hold values from -6 to 6
- cotangents: bfloat16 [128, 512, 8192], P('demo', 'sketch', 'fsdp'), may hold values from -6 to 6
- lengths: int32 [128], P('demo'), may hold values from 64 to 512, as said below
- lowrank_contract_matrix: bfloat16 [8192, 128], P('fsdp', 'demo'), may hold values from -0.0625 to 0.0625
- lowrank_expand_matrix: bfloat16 [8192, 128], P('fsdp', 'demo'), may hold values from -0.0625 to 0.0625
- input_feature_sketch: bfloat16 [8192, 64], P('fsdp', 'demo'), may hold values from -0.0625 to 0.0625
- latent_random_map_contracting: bfloat16 [128, 128], replicated, may hold values from -0.5 to 0.5
- latent_random_map_expanding: bfloat16 [128, 64], replicated, may hold values from -0.5 to 0.5
- output_feature_sketch: bfloat16 [8192, 128], P('fsdp', 'demo'), may hold values from -0.0625 to 0.0625
- queries: bfloat16 [4096, 8192], P('demo', 'sketch'), may hold values from -6 to 6
Outputs:
- scores: float32 [128, 4096], P('sketch', 'demo')
Inputs may be any that keep to these rules, and one draw needn't show every extreme that they name: `lengths`: positions from a demonstration's length on are padding; at least one demonstration uses all 512 positions.
All inputs are finite; a program needn't handle non-finite values.
Results may differ from a plain program's by a relative error of at most 0.0057.
Values may be sent and summed in bfloat16 or wider, within the bound.
No kernel may reach another device: no remote copies, remote signals or barrier semaphores. Data moves between devices by JAX's collectives and lax.ppermute only.
A program may use at most 64 MiB of HBM per device.

v0:
```python
import math

import jax
import jax.numpy as jnp
from jax import lax
from jax.sharding import PartitionSpec as P

PROBE_ROWS = 64
PROBE_COLUMNS = 128
K = 8192


def combine_maps(
    down_cols,
    up_cols,
    left_cols,
    right_cols,
    latent_random_map_contracting,
    latent_random_map_expanding,
):
    reduced_left_factor = jnp.dot(
        down_cols, latent_random_map_expanding, preferred_element_type=jnp.float32
    ).astype(jnp.bfloat16)
    reduced_right_factor = jnp.dot(
        up_cols, latent_random_map_contracting, preferred_element_type=jnp.float32
    ).astype(jnp.bfloat16)
    left_map = jnp.concatenate([left_cols, reduced_left_factor], axis=1)
    right_map = jnp.concatenate([reduced_right_factor, right_cols], axis=1)
    return (left_map, right_map)


def shards(
    activations,
    cotangents,
    lengths,
    lowrank_contract_matrix,
    lowrank_expand_matrix,
    input_feature_sketch,
    latent_random_map_contracting,
    latent_random_map_expanding,
    output_feature_sketch,
    queries,
):
    demo_count, tok_local, feat_half = activations.shape
    out_half = cotangents.shape[2]
    sketch_index = lax.axis_index("sketch")
    sketch_count = lax.axis_size("sketch")
    down_cols, up_cols, left_cols, right_cols = (
        lax.all_gather(lowrank_contract_matrix, "demo", axis=1, tiled=True),
        lax.all_gather(lowrank_expand_matrix, "demo", axis=1, tiled=True),
        lax.all_gather(input_feature_sketch, "demo", axis=1, tiled=True),
        lax.all_gather(output_feature_sketch, "demo", axis=1, tiled=True),
    )
    left_map, right_map = combine_maps(
        down_cols,
        up_cols,
        left_cols,
        right_cols,
        latent_random_map_contracting,
        latent_random_map_expanding,
    )
    tok_rows = demo_count * tok_local
    left_part = jnp.dot(
        activations.reshape(tok_rows, feat_half), left_map, preferred_element_type=jnp.float32
    )
    left_part = left_part.reshape(demo_count, tok_local, 2 * PROBE_ROWS)
    right_part = jnp.dot(
        cotangents.reshape(tok_rows, out_half), right_map, preferred_element_type=jnp.float32
    )
    positions = sketch_index * tok_local + jnp.arange(tok_local, dtype=jnp.int32)
    padding = (positions[None, :] < lengths[:, None]).astype(jnp.float32)
    right_part = right_part.reshape(demo_count, tok_local, 2 * PROBE_COLUMNS) * padding[:, :, None]
    left_sum, right_sum = lax.psum((left_part, right_part), "fsdp")
    kept = left_sum.shape[1]
    left_rows = left_sum.astype(jnp.bfloat16).reshape(demo_count, kept, 2, PROBE_ROWS)
    right_rows = right_sum.astype(jnp.bfloat16).reshape(demo_count, kept, 2, PROBE_COLUMNS)
    partial_value = jnp.einsum(
        "ntpa,ntpb->nab", left_rows, right_rows, preferred_element_type=jnp.float32
    )
    partial_value = partial_value.reshape(demo_count, K)
    summed = lax.psum_scatter(partial_value, "sketch", scatter_dimension=1, tiled=True)
    demo_sketch = summed.astype(jnp.bfloat16)
    every_demo = lax.all_gather(demo_sketch, "demo", axis=0, tiled=True)
    inner_part = lax.dot_general(
        every_demo, queries, (((1,), (1,)), ((), ())), preferred_element_type=jnp.float32
    )
    every_f = every_demo.astype(jnp.float32)
    demo_squares = jnp.sum(every_f * every_f, axis=1)
    query_f = queries.astype(jnp.float32)
    query_squares = jnp.sum(query_f * query_f, axis=1)
    query_tile = jnp.broadcast_to(query_squares[None, :], (sketch_count, query_squares.shape[0]))
    inner, demo_total, query_total = (
        lax.psum_scatter(inner_part, "sketch", scatter_dimension=0, tiled=True),
        lax.psum_scatter(demo_squares, "sketch", scatter_dimension=0, tiled=True),
        lax.psum_scatter(query_tile, "sketch", scatter_dimension=0, tiled=True),
    )
    demo_norm = jnp.sqrt(demo_total + 1e-06)
    query_norm = jnp.sqrt(query_total[0] + 1e-06)
    return math.sqrt(K) * inner / (demo_norm[:, None] * query_norm[None, :])


def solution(mesh):
    placed = (
        P("demo", "sketch", "fsdp"),
        P("demo", "sketch", "fsdp"),
        P("demo"),
        P("fsdp", "demo"),
        P("fsdp", "demo"),
        P("fsdp", "demo"),
        P(),
        P(),
        P("fsdp", "demo"),
        P("demo", "sketch"),
    )
    return jax.shard_map(
        shards, mesh=mesh, in_specs=placed, out_specs=P("sketch", "demo"), check_vma=False
    )
```

profile of v0, /device:TPU:1, one launch (start us, length us, event | category | flops | bytes accessed | tf_op | source)
XLA Modules:
  0.0 398.2 jit_solution(10282851625283697972)
XLA Ops:
  6.5 0.7 all-gather.11.cloned.1.call-update
  7.3 0.7 all-gather.13.cloned.1.call-update
  8.1 0.7 all-gather.9.cloned.1.call-update
  8.8 43.8 %all-gather = bf16[32,2,4096]{2,1,0:T(2,128)(2,1)S(1)} all-gather(bf16[1,2,4096]{2,1,0:T(2,128)(2,1)} %bitcast.60), channel_id=1, replica_groups=mesh['demo'=32,'fsdp'=2,'sketch'=4] {'demo'}, dimensions={0}, use_global_device_ids=true | all-gather | bytes 540672 | tf_op jit(solution)/shard_map/all_gather | solution.py:51
  52.6 0.2 reshape.64
  52.8 0.7 compare_convert_fusion
  53.5 32.1 %all-gather.11.cloned.1.call-done = bf16[32,4,4096]{2,1,0:T(4,128)(2,1)} async-done(((bf16[1,4,4096]{2,1,0:T(4,128)(2,1)}), bf16[32,4,4096]{2,1,0:T(4,128)(2,1)}) %all-gather.11.cloned.1.call-update) | async-done | bytes 1048592 | tf_op jit(solution)/shard_map/all_gather | solution.py:50
  85.6 1.3 reshape.68
  86.9 75.1 %all-gather.13.cloned.1.call-done = bf16[32,4,4096]{2,1,0:T(4,128)(2,1)} async-done(((bf16[1,4,4096]{2,1,0:T(4,128)(2,1)}), bf16[32,4,4096]{2,1,0:T(4,128)(2,1)}) %all-gather.13.cloned.1.call-update) | async-done | bytes 1048592 | tf_op jit(solution)/shard_map/all_gather | solution.py:52
  162.0 1.3 reshape.70
  163.3 0.5 convolution_convert_fusion
  163.8 3.5 fusion.4
  167.4 71.1 %all-gather.9.cloned.1.call-done = bf16[32,4,4096]{2,1,0:T(4,128)(2,1)} async-done(((bf16[1,4,4096]{2,1,0:T(4,128)(2,1)}), bf16[32,4,4096]{2,1,0:T(4,128)(2,1)}) %all-gather.9.cloned.1.call-update) | async-done | bytes 1048592 | tf_op jit(solution)/shard_map/all_gather | solution.py:49
  238.4 1.3 reshape.66
  239.8 0.3 convolution_convert_fusion.1
  240.1 3.7 convolution_bitcast_fusion
  243.8 0.1 reshape.57
  243.9 20.4 %all-reduce.5 = (bf16[4,128,128]{1,0,2:T(4,128)(2,1)S(1)}, bf16[4,128,256]{1,2,0:T(8,128)(2,1)S(1)}) all-reduce(f32[4,128,128]{1,0,2:T(4,128)S(1)} %reshape.57, f32[4,128,256]{1,2,0:T(8,128)S(1)} %bitcast_multiply_fusion), channel_id=1, replica_groups=mesh['demo'=32,'fsdp'=2,'sketch'=4] {'fsdp'}, use_global_device_ids=true, to_apply=%region_0.0 | all-reduce | flops 196608 | bytes 1179648 | tf_op jit(solution)/shard_map/psum | solution.py:73
  264.3 0.2 convolution_bitcast_fusion.1
  264.5 2.6 copy.22
  267.2 0.6 dynamic-slice
  268.5 0.2 multiply_reduce_fusion
  268.7 50.9 %reduce-scatter.7.cloned.1.call-done = f32[2048,4]{1,0:T(8,128)} async-done(((f32[8192,4]{1,0:T(8,128)}), f32[2048,4]{1,0:T(8,128)}) %reduce-scatter.7.cloned.1.call-update) | async-done | bytes 32784
  319.5 1.6 copy.21
  321.1 38.5 %all-gather.4 = bf16[32,4,2048]{2,1,0:T(4,128)(2,1)S(1)} all-gather(bf16[1,4,2048]{2,1,0:T(4,128)(2,1)S(1)} %bitcast.56), channel_id=1, replica_groups=mesh['demo'=32,'fsdp'=2,'sketch'=4] {'demo'}, dimensions={0}, use_global_device_ids=true | all-gather | bytes 540672 | tf_op jit(solution)/shard_map/all_gather | solution.py:83
  359.6 0.1 reshape.72
  359.7 0.2 multiply_reduce_fusion.1
  359.9 0.9 fusion.15
  360.8 17.2 %all-reduce.2 = (f32[4,128]{1,0:T(4,128)S(1)}, f32[128]{0:T(128)S(1)}) all-reduce(f32[4,128]{1,0:T(4,128)S(1)} %broadcast_in_dim.2, f32[128]{0:T(128)S(1)} %multiply_reduce_fusion.1), channel_id=5, replica_groups=mesh['demo'=32,'fsdp'=2,'sketch'=4] {'sketch'}, use_global_device_ids=true, to_apply=%region_7.0.clone | all-reduce | flops 640 | bytes 5120
  378.1 0.7 fusion.12
  378.8 11.5 %reduce-scatter.5.cloned.1.call-done = f32[32,128]{1,0:T(8,128)} async-done(((f32[128,128]{1,0:T(8,128)}), f32[32,128]{1,0:T(8,128)}) %reduce-scatter.5.cloned.1.call-update) | async-done | bytes 16400 | tf_op jit(solution)/shard_map/reduce_scatter | solution.py:93
  390.3 1.4 multiply_divide_fusion
  (20 shorter events, 0.4 us)
Async XLA Ops:
  6.5 156.8 %copy-start = (bf16[128,128]{1,0:T(8,128)(2,1)S(1)}, bf16[128,128]{1,0:T(8,128)(2,1)}, u32[]{:S(2)}) copy-start(bf16[128,128]{1,0:T(8,128)(2,1)} %param.16) | copy-start | bytes 98308
  6.5 79.0 %all-gather.11.cloned.1.call-start = ((), (), s32[]{:S(2)}) async-start(), calls=%async_computation.4 | async-start | bytes 1081344 | tf_op jit(solution)/shard_map/all_gather | solution.py:50
  7.3 154.7 %all-gather.13.cloned.1.call-start = ((), (), s32[]{:S(2)}) async-start(), calls=%async_computation.5 | async-start | bytes 1081344 | tf_op jit(solution)/shard_map/all_gather | solution.py:52
  8.0 230.4 %all-gather.9.cloned.1.call-start = ((), (), s32[]{:S(2)}) async-start(), calls=%async_computation.3 | async-start | bytes 1081344 | tf_op jit(solution)/shard_map/all_gather | solution.py:49
  8.7 310.8 %reduce-scatter.7.cloned.1.call-start = ((), (), s32[]{:S(2)}) async-start(), calls=%async_computation.6 | async-start | bytes 5242880
  163.8 75.9 %copy-start.2 = (bf16[128,64]{0,1:T(8,128)(2,1)S(1)}, bf16[128,64]{0,1:T(8,128)(2,1)}, u32[]{:S(2)}) copy-start(bf16[128,64]{0,1:T(8,128)(2,1)} %param.17) | copy-start | bytes 49156
  264.5 2.7 copy-start.3
  264.5 4.0 copy-start.1
  267.2 123.1 %reduce-scatter.5.cloned.1.call-start = ((), (), s32[]{:S(2)}) async-start(), calls=%async_computation.2 | async-start | bytes 81920 | tf_op jit(solution)/shard_map/reduce_scatter | solution.py:93
Sparse Core Ops, SparseCore 0:
  9.9 75.5 all-gather.10
  88.1 73.7 all-gather.12
  164.6 73.7 all-gather.8
  267.3 52.1 reduce-scatter.6
  361.0 29.2 reduce-scatter.4
where the time goes:
time: 399 us; the launch traced here: 398 us
  waiting for transfers between devices  243 us (61%)
  blocking collectives  120 us (30%)
  between operations  14 us (4%)
  local copies, waits for them, and re-layouts  9.24 us (2%)
  matrix products  9.08 us (2%)
    all_gather x1, waiting for transfers between devices, shards(): lax.all_gather(output_feature_sketch, 'demo', axis=1, tiled=True)  75.1 us
    all_gather x1, waiting for transfers between devices, shards(): lax.all_gather(lowrank_contract_matrix, 'demo', axis=1, tiled=True)  71.1 us
    unnamed x6, waiting for transfers between devices  53 us
    all_gather x1, blocking collectives, shards(): lax.all_gather(input_feature_sketch, 'demo', axis=1, tiled=True)  43.8 us
    all_gather x1, blocking collectives, shards(): every_demo = lax.all_gather(demo_sketch, 'demo', axis=0, tiled=True)  38.5 us
    all_gather x1, waiting for transfers between devices, shards(): lax.all_gather(lowrank_expand_matrix, 'demo', axis=1, tiled=True)  32.1 us
    psum x1, blocking collectives, shards(): left_sum, right_sum = lax.psum((left_part, right_part), 'fsdp')  20.4 us
    unnamed x1, blocking collectives  17.2 us
  transfers between devices with their start and end apart: 5, of which 5 were waited for; matrix products, arithmetic and copies ran while one was open for 2% of the time, Pallas kernels for 0%

commit v1 on v0

v1 whole, which is shorter than its diff:
```python
import math

import jax
import jax.numpy as jnp
from jax import lax
from jax.sharding import PartitionSpec as P

PROBE_ROWS = 64
PROBE_COLUMNS = 128
RANK = 128
K = 8192
AXES = ("demo", "fsdp", "sketch")
Z, X, F, S = 8, 4, 2, 4
ROWS = 16


def pairs(step):
    out = []
    for z in range(Z):
        for x in range(X):
            for f in range(F):
                for s in range(S):
                    z2, x2, f2, s2 = step(z, x, f, s)
                    source = ((z * X + x) * F + f) * S + s
                    target = (((z2 % Z) * X + x2 % X) * F + f2) * S + s2
                    out.append((source, target))
    return out


CORE = pairs(lambda z, x, f, s: (z, x, f, s ^ 1))
NEAR = pairs(lambda z, x, f, s: (z, x, f, s ^ 2))
FAR = pairs(lambda z, x, f, s: (z, x, f ^ 1, s))
FAR_NEAR = pairs(lambda z, x, f, s: (z, x, f ^ 1, s ^ 2))


def shift(dz, dx):
    return pairs(lambda z, x, f, s: (z + dz, x + dx, f, s))


def send(value, moves):
    return lax.ppermute(value, AXES, moves)


def pick(value, index):
    return lax.dynamic_index_in_dim(value, index, 0, keepdims=False)


def map_weights(contracting, expanding, z, x):
    weights = jnp.zeros((2 * PROBE_ROWS + 2 * PROBE_COLUMNS, Z * X, ROWS), jnp.bfloat16)
    weights = weights.at[PROBE_ROWS : 2 * PROBE_ROWS, :, 0:4].set(
        expanding.T.reshape(PROBE_ROWS, Z * X, 4)
    )
    weights = weights.at[2 * PROBE_ROWS : 2 * PROBE_ROWS + PROBE_COLUMNS, :, 4:8].set(
        contracting.T.reshape(PROBE_COLUMNS, Z * X, 4)
    )
    weights = weights.at[2 * PROBE_ROWS + PROBE_COLUMNS :, :, 8:12].set(
        jnp.eye(PROBE_COLUMNS, dtype=jnp.bfloat16).reshape(PROBE_COLUMNS, Z * X, 4)
    )
    weights = weights.at[:PROBE_ROWS, :, 12:14].set(
        jnp.eye(PROBE_ROWS, dtype=jnp.bfloat16).reshape(PROBE_ROWS, Z * X, 2)
    )
    weights = weights.reshape(-1, Z, X, ROWS)
    z_order = (z - jnp.arange(Z)) % Z
    x_order = (x - jnp.arange(X)) % X
    weights = jnp.take(jnp.take(weights, z_order, axis=1), x_order, axis=2)
    return weights.reshape(-1, Z * X * ROWS)


def gather_x(block):
    return jnp.stack([block] + [send(block, shift(0, k)) for k in range(1, X)])


def gather_z(block):
    got = {0: block}
    up = down = block
    for k in range(1, Z // 2 + 1):
        up = send(up, shift(1, 0))
        got[k] = up
        if k < Z // 2:
            down = send(down, shift(-1, 0))
            got[Z - k] = down
    return jnp.stack([got[k] for k in range(Z)])


def shards(
    activations,
    cotangents,
    lengths,
    lowrank_contract_matrix,
    lowrank_expand_matrix,
    input_feature_sketch,
    latent_random_map_contracting,
    latent_random_map_expanding,
    output_feature_sketch,
    queries,
):
    demo_count, tok_local, feat = activations.shape
    demo = lax.axis_index("demo")
    z, x = demo // X, demo % X
    f = lax.axis_index("fsdp")
    s = lax.axis_index("sketch")
    near, core = s // 2, s % 2

    block = jnp.concatenate(
        [
            lowrank_contract_matrix.T,
            lowrank_expand_matrix.T,
            output_feature_sketch.T,
            input_feature_sketch.T,
            jnp.zeros((2, feat), jnp.bfloat16),
        ],
        axis=0,
    )
    half = feat // 2
    block = lax.dynamic_slice_in_dim(block, core * half, half, axis=1)
    rows = gather_z(gather_x(block)).reshape(Z * X * ROWS, half)
    other = send(rows, CORE)
    first = jnp.where(core == 0, rows, other)
    second = jnp.where(core == 0, other, rows)
    weights = map_weights(
        latent_random_map_contracting, latent_random_map_expanding, z, x
    )
    maps = jnp.concatenate(
        [
            jnp.dot(weights, first, preferred_element_type=jnp.float32).astype(jnp.bfloat16),
            jnp.dot(weights, second, preferred_element_type=jnp.float32).astype(jnp.bfloat16),
        ],
        axis=1,
    )
    tok_rows = demo_count * tok_local
    contract_last = (((1,), (1,)), ((), ()))
    right = lax.dot_general(
        cotangents.reshape(tok_rows, feat),
        maps[2 * PROBE_ROWS :],
        contract_last,
        preferred_element_type=jnp.float32,
    ).reshape(F, demo_count // F, tok_local, 2 * PROBE_COLUMNS)
    left = lax.dot_general(
        activations.reshape(tok_rows, feat),
        maps[: 2 * PROBE_ROWS],
        contract_last,
        preferred_element_type=jnp.float32,
    ).reshape(F, demo_count // F, tok_local, 2 * PROBE_ROWS)

    right_sum = pick(right, f) + send(pick(right, 1 - f), FAR)
    left_sum = pick(left, f) + send(pick(left, 1 - f), FAR)
    positions = s * tok_local + jnp.arange(tok_local, dtype=jnp.int32)
    own_lengths = pick(lengths.reshape(F, demo_count // F), f)
    padding = (positions[None, :] < own_lengths[:, None]).astype(jnp.float32)
    right_sum = right_sum * padding[:, :, None]
    own = demo_count // F
    left_rows = left_sum.astype(jnp.bfloat16).reshape(own, tok_local, 2, PROBE_ROWS)
    right_rows = right_sum.astype(jnp.bfloat16).reshape(own, tok_local, 2, PROBE_COLUMNS)
    partial_value = jnp.einsum(
        "ntpa,ntpb->nab", left_rows, right_rows, preferred_element_type=jnp.float32
    )
    parts = partial_value.reshape(own, 2, 2, K // S).transpose(2, 1, 0, 3)
    parts = pick(parts, core) + send(pick(parts, 1 - core), CORE)
    part = pick(parts, near) + send(pick(parts, 1 - near), NEAR)
    demo_sketch = part.astype(jnp.bfloat16)

    every_demo = gather_z(gather_x(demo_sketch)).reshape(Z * X * own, K // S)
    inner = lax.dot_general(
        every_demo, queries, contract_last, preferred_element_type=jnp.float32
    )
    every_f = every_demo.astype(jnp.float32)
    demo_squares = jnp.sum(every_f * every_f, axis=1, keepdims=True)
    query_f = queries.astype(jnp.float32)
    query_squares = jnp.sum(query_f * query_f, axis=1)[None, :]
    query_squares = query_squares + send(query_squares, CORE)
    query_squares = query_squares + send(query_squares, NEAR)
    nq = queries.shape[0]
    both = jnp.concatenate([inner, jnp.broadcast_to(demo_squares, inner.shape)], axis=1)
    both = both.reshape(Z, X, own, 2 * nq)
    z_order = (z - jnp.arange(Z)) % Z
    x_order = (x - jnp.arange(X)) % X
    both = jnp.take(jnp.take(both, z_order, axis=0), x_order, axis=1)
    both = both.reshape(2, 2, (Z // S) * X * own, 2 * nq).transpose(1, 0, 2, 3)
    pair = pick(both, core) + send(pick(both, 1 - core), CORE)
    mine, theirs = pick(pair, near), pick(pair, 1 - near)
    here = mine + send(theirs, NEAR)
    there = send(mine, FAR) + send(theirs, FAR_NEAR)
    total = jnp.stack([jnp.where(f == 0, here, there), jnp.where(f == 0, there, here)])
    total = total.reshape(F, (Z // S) * X, own, 2 * nq).transpose(1, 0, 2, 3).reshape(-1, 2 * nq)
    demo_norm = jnp.sqrt(total[:, nq:] + 1e-06)
    query_norm = jnp.sqrt(query_squares + 1e-06)
    return math.sqrt(K) * total[:, :nq] / (demo_norm * query_norm)


def solution(mesh):
    placed = (
        P("demo", "sketch", "fsdp"),
        P("demo", "sketch", "fsdp"),
        P("demo"),
        P("fsdp", "demo"),
        P("fsdp", "demo"),
        P("fsdp", "demo"),
        P(),
        P(),
        P("fsdp", "demo"),
        P("demo", "sketch"),
    )
    return jax.shard_map(
        shards, mesh=mesh, in_specs=placed, out_specs=P("sketch", "demo"), check_vma=False
    )
```

time: 399 us -> 123 us (0.31)
  waiting for transfers between devices: 243 us -> 40.5 us
  blocking collectives: 120 us -> 0 us
  starting transfers between devices: 0.16 us -> 54 us
  between operations: 14 us -> 0.65 us
    all_gather x3 -> x0, waiting for transfers between devices: 178 us -> none  [the longest x1 75.1 us: shards(): lax.all_gather(output_feature_sketch, 'demo', axis=1, tiled=True)]
    all_gather x2 -> x0, blocking collectives: 82.2 us -> none  [the longest x1 43.8 us: shards(): lax.all_gather(input_feature_sketch, 'demo', axis=1, tiled=True)]
    ppermute x0 -> x31, starting transfers between devices: none -> 54 us  [send(): return lax.ppermute(value, AXES, moves)]
    unnamed x6 -> x0, waiting for transfers between devices: 53 us -> none
    ppermute x0 -> x31, waiting for transfers between devices: none -> 40.5 us  [send(): return lax.ppermute(value, AXES, moves)]
    psum x1 -> x0, blocking collectives: 20.4 us -> none  [shards(): left_sum, right_sum = lax.psum((left_part, right_part), 'fsdp')]
    unnamed x1 -> x0, blocking collectives: 17.2 us -> none
    reduce_scatter x1 -> x0, waiting for transfers between devices: 11.5 us -> none  [shards(): lax.psum_scatter(inner_part, 'sketch', scatter_dimension=0, tiled=True)]
  transfers between devices with their start and end apart: 5 -> 31, of which waited for: 5 -> 16; matrix products, arithmetic and copies ran while one was open for 2% -> 14% of each run, Pallas kernels for 0% -> 0%
where the time goes in v1:
time: 123 us
  starting transfers between devices  54 us (44%)
  waiting for transfers between devices  40.5 us (33%)
  local copies, waits for them, and re-layouts  12.1 us (10%)
  matrix products  9.27 us (8%)
  other arithmetic  6.39 us (5%)
    ppermute x31, starting transfers between devices, send(): return lax.ppermute(value, AXES, moves)  54 us
    ppermute x31, waiting for transfers between devices, send(): return lax.ppermute(value, AXES, moves)  40.5 us
    another operation x3, other arithmetic  4.26 us
    dot_general x1, matrix products, shards(): lax.dot_general(activations.reshape(tok_rows, feat), maps[:2 * PROBE_ROWS...  3.88 us
    unnamed x33, local copies, waits for them, and re-layouts  2.76 us
    dot_general x1, matrix products, shards(): jnp.dot(weights, first, preferred_element_type=jnp.float32)  2.62 us
    scatter x1, local copies, waits for them, and re-layouts, map_weights(): weights.at[:PROBE_ROWS, :, 12:14]  2.48 us
  transfers between devices with their start and end apart: 31, of which 16 were waited for; matrix products, arithmetic and copies ran while one was open for 14% of the time, Pallas kernels for 0%

profile of v1, /device:TPU:1, one launch (start us, length us, event | category | flops | bytes accessed | tf_op | source)
XLA Modules:
  0.0 122.9 jit_solution(6210055850774105249)
XLA Ops:
  0.0 1.6 %concatenate.21 = bf16[16,4096]{1,0:T(8,128)(2,1)S(1)} concatenate(bf16[4,4096]{1,0:T(4,128)(2,1)} %bitcast.159, bf16[4,4096]{1,0:T(4,128)(2,1)} %bitcast.160, bf16[4,4096]{1,0:T(4,128)(2,1)} %bitcast.161, bf16[2,4096]{1,0:T(2,128)(2,1)} %bitcast.168, bf16[2,4096]{1,0:T(2,128)(2,1)S(1)} %broadcast_in_dim.76), dimensions={0} | concatenate | bytes 262144 | tf_op jit(solution)/shard_map/concatenate | solution.py:104
  1.7 2.1 %collective-permute-start = (bf16[16,2048]{1,0:T(8,128)(2,1)S(1)}, bf16[16,2048]{1,0:T(8,128)(2,1)S(1)}, u32[]{:S(2)}, u32[]{:S(2)}) collective-permute-start(bf16[16,2048]{1,0:T(8,128)(2,1)S(1)} %constant_dynamic-slice_fusion.6), channel_id=1, source_target_pairs={{0,8},{1,9},{2,10},{3,11},{4,12},{5,13},{6,14},{7,15},{8,16},{9,17... | collective-permute-start | bytes 196616 | tf_op jit(solution)/shard_map/ppermute | solution.py:41
  3.8 2.5 %collective-permute-start.1 = (bf16[16,2048]{1,0:T(8,128)(2,1)S(1)}, bf16[16,2048]{1,0:T(8,128)(2,1)S(1)}, u32[]{:S(2)}, u32[]{:S(2)}) collective-permute-start(bf16[16,2048]{1,0:T(8,128)(2,1)S(1)} %constant_dynamic-slice_fusion.6), channel_id=1, source_target_pairs={{0,16},{1,17},{2,18},{3,19},{4,20},{5,21},{6,22},{7,23},{8,24},{9,... | collective-permute-start | bytes 196616 | tf_op jit(solution)/shard_map/ppermute | solution.py:41
  7.4 1.4 %collective-permute-done.1 = bf16[16,2048]{1,0:T(8,128)(2,1)S(1)} collective-permute-done((bf16[16,2048]{1,0:T(8,128)(2,1)S(1)}, bf16[16,2048]{1,0:T(8,128)(2,1)S(1)}, u32[]{:S(2)}, u32[]{:S(2)}) %collective-permute-start.1) | collective-permute-done | bytes 65568 | tf_op jit(solution)/shard_map/ppermute | solution.py:41
  9.7 2.0 %collective-permute-start.3 = (bf16[4,16,2048]{2,1,0:T(8,128)(2,1)S(1)}, bf16[4,16,2048]{2,1,0:T(8,128)(2,1)S(1)}, u32[]{:S(2)}, u32[]{:S(2)}) collective-permute-start(bf16[4,16,2048]{2,1,0:T(8,128)(2,1)S(1)} %pad_maximum_fusion.4), channel_id=1, source_target_pairs={{0,32},{1,33},{2,34},{3,35},{4,36},{5,37},{6,38},{7,39},{8,40},{9,... | collective-permute-start | bytes 786440 | tf_op jit(solution)/shard_map/ppermute | solution.py:41
  11.7 4.0 %collective-permute-start.7 = (bf16[4,16,2048]{2,1,0:T(8,128)(2,1)S(1)}, bf16[4,16,2048]{2,1,0:T(8,128)(2,1)S(1)}, u32[]{:S(2)}, u32[]{:S(2)}) collective-permute-start(bf16[4,16,2048]{2,1,0:T(8,128)(2,1)S(1)} %pad_maximum_fusion.4), channel_id=1, source_target_pairs={{0,224},{1,225},{2,226},{3,227},{4,228},{5,229},{6,230},{7,231},{8... | collective-permute-start | bytes 786440 | tf_op jit(solution)/shard_map/ppermute | solution.py:41
  16.4 4.0 %collective-permute-done.3 = bf16[4,16,2048]{2,1,0:T(8,128)(2,1)S(1)} collective-permute-done((bf16[4,16,2048]{2,1,0:T(8,128)(2,1)S(1)}, bf16[4,16,2048]{2,1,0:T(8,128)(2,1)S(1)}, u32[]{:S(2)}, u32[]{:S(2)}) %collective-permute-start.3) | collective-permute-done | bytes 262176 | tf_op jit(solution)/shard_map/ppermute | solution.py:41
  20.4 2.7 %collective-permute-start.8 = (bf16[4,16,2048]{2,1,0:T(8,128)(2,1)S(1)}, bf16[4,16,2048]{2,1,0:T(8,128)(2,1)S(1)}, u32[]{:S(2)}, u32[]{:S(2)}) collective-permute-start(bf16[4,16,2048]{2,1,0:T(8,128)(2,1)S(1)} %collective-permute-done.7), channel_id=1, source_target_pairs={{0,224},{1,225},{2,226},{3,227},{4,228},{5,229},{6,230},{7,231},{8... | collective-permute-start | bytes 786440 | tf_op jit(solution)/shard_map/ppermute | solution.py:41
  23.1 3.7 %collective-permute-done.4 = bf16[4,16,2048]{2,1,0:T(8,128)(2,1)S(1)} collective-permute-done((bf16[4,16,2048]{2,1,0:T(8,128)(2,1)S(1)}, bf16[4,16,2048]{2,1,0:T(8,128)(2,1)S(1)}, u32[]{:S(2)}, u32[]{:S(2)}) %collective-permute-start.4) | collective-permute-done | bytes 262176 | tf_op jit(solution)/shard_map/ppermute | solution.py:41
  26.8 2.7 %collective-permute-start.9 = (bf16[4,16,2048]{2,1,0:T(8,128)(2,1)S(1)}, bf16[4,16,2048]{2,1,0:T(8,128)(2,1)S(1)}, u32[]{:S(2)}, u32[]{:S(2)}) collective-permute-start(bf16[4,16,2048]{2,1,0:T(8,128)(2,1)S(1)} %collective-permute-done.8), channel_id=1, source_target_pairs={{0,224},{1,225},{2,226},{3,227},{4,228},{5,229},{6,230},{7,231},{8... | collective-permute-start | bytes 786440 | tf_op jit(solution)/shard_map/ppermute | solution.py:41
  29.5 3.7 %collective-permute-done.5 = bf16[4,16,2048]{2,1,0:T(8,128)(2,1)S(1)} collective-permute-done((bf16[4,16,2048]{2,1,0:T(8,128)(2,1)S(1)}, bf16[4,16,2048]{2,1,0:T(8,128)(2,1)S(1)}, u32[]{:S(2)}, u32[]{:S(2)}) %collective-permute-start.5) | collective-permute-done | bytes 262176 | tf_op jit(solution)/shard_map/ppermute | solution.py:41
  33.3 6.9 %collective-permute-done.6 = bf16[4,16,2048]{2,1,0:T(8,128)(2,1)S(1)} collective-permute-done((bf16[4,16,2048]{2,1,0:T(8,128)(2,1)S(1)}, bf16[4,16,2048]{2,1,0:T(8,128)(2,1)S(1)}, u32[]{:S(2)}, u32[]{:S(2)}) %collective-permute-start.6) | collective-permute-done | bytes 262176 | tf_op jit(solution)/shard_map/ppermute | solution.py:41
  40.3 6.1 %collective-permute-start.10 = (bf16[512,2048]{1,0:T(8,128)(2,1)S(1)}, bf16[512,2048]{1,0:T(8,128)(2,1)}, u32[]{:S(2)}, u32[]{:S(2)}) collective-permute-start(bf16[512,2048]{1,0:T(8,128)(2,1)S(1)} %bitcast.138), channel_id=1, source_target_pairs={{0,1},{1,0},{2,3},{3,2},{4,5},{5,4},{6,7},{7,6},{8,9},{9,8},{10,11... | collective-permute-start | bytes 6291464 | tf_op jit(solution)/shard_map/ppermute | solution.py:41
  46.4 2.1 %and_reduce_fusion = pred[]{:T(512)} fusion(s32[3]{0:T(128)S(1)} %copy-done.6, s32[1]{0:T(128)} %get-tuple-element.64, s32[1]{0:T(128)} %constant.311.clone.1, s32[1]{0:T(128)} %get-tuple-element.63), kind=kLoop, calls=%fused_computation.102 | loop fusion | flops 17 | bytes 25 | tf_op jit(solution)/shard_map/reduce.7
  48.9 2.1 %broadcast_select_fusion.2 = bf16[64,32,2]{0,2,1:T(2,128)(2,1)S(1)} fusion(pred[]{:T(512)} %and_reduce_fusion, bf16[384,32,16]{0,2,1:T(8,128)(2,1)S(1)} %fusion.14, s32[]{:T(128)} %bitcast.4, s32[]{:T(128)} %bitcast.5, s32[32,2]{1,0:T(8,128)S(1)} %multiply_add_fusion), kind=kLoop, calls=%fused_computation.62 | loop fusion | flops 12288 | bytes 16649 | tf_op jit(solution)/shard_map/select.7
  51.1 2.5 %scatter.19 = bf16[384,32,16]{0,2,1:T(8,128)(2,1)S(1)} dynamic-update-slice(bf16[384,32,16]{0,2,1:T(8,128)(2,1)S(1)} %fusion.14, bf16[64,32,2]{0,2,1:T(2,128)(2,1)S(1)} %broadcast_select_fusion.2, s32[]{:T(128)} %bitcast.4, s32[]{:T(128)} %constant.297.clone.1, s32[]{:T(128)} %bitcast.5) | dynamic-update-slice | bytes 16388 | tf_op jit(solution)/shard_map/scatter | solution.py:59
  55.6 2.6 %convolution_convert_fusion.1 = bf16[384,2048]{1,0:T(8,128)(2,1)S(1)} fusion(bf16[384,512]{0,1:T(8,128)(2,1)S(1)} %bitcast_select_fusion, bf16[512,2048]{1,0:T(8,128)(2,1)S(1)} %bitcast.139, bf16[512,2048]{1,0:T(8,128)(2,1)} %collective-permute-done.10, pred[]{:T(512)S(6)} %eq.28), kind=kOutput, calls=%fused_computation.5 | convolution fusion | flops 807141376 | bytes 6160385 | tf_op jit(solution)/shard_map/dot_general | solution.py:125
  61.5 1.3 %fusion.6 = f32[512,256]{0,1:T(8,128)S(1)} fusion(bf16[512,4096]{1,0:T(8,128)(2,1)S(1)} %bitcast.171, bf16[384,2048]{1,0:T(8,128)(2,1)S(1)} %convolution_convert_fusion, bf16[384,2048]{1,0:T(8,128)(2,1)S(1)} %convolution_convert_fusion.1), kind=kOutput, calls=%fused_computation.13 | convolution fusion | flops 1077936128 | bytes 7864320 | tf_op jit(solution)/shard_map/dot_general | solution.py:132
  63.4 3.0 %collective-permute-start.12 = (f32[2,128,256]{1,2,0:T(8,128)S(1)}, f32[2,128,256]{1,2,0:T(8,128)S(1)}, u32[]{:S(2)}, u32[]{:S(2)}) collective-permute-start(f32[2,128,256]{1,2,0:T(8,128)S(1)} %bitcast.145), channel_id=1, source_target_pairs={{0,4},{1,5},{2,6},{3,7},{4,0},{5,1},{6,2},{7,3},{8,12},{9,13},{10,... | collective-permute-start | bytes 786440 | tf_op jit(solution)/shard_map/ppermute | solution.py:41
  66.4 3.9 %convolution_bitcast_fusion = f32[512,128]{0,1:T(8,128)S(1)} fusion(bf16[512,4096]{1,0:T(8,128)(2,1)} %bitcast.141, bf16[384,2048]{1,0:T(8,128)(2,1)} %copy-done.2, bf16[384,2048]{1,0:T(8,128)(2,1)S(1)} %copy-done.1), kind=kOutput, calls=%fused_computation.14 | convolution fusion | flops 538968064 | bytes 7602176 | tf_op jit(solution)/shard_map/dot_general | solution.py:138
  71.4 5.9 %collective-permute-done.11 = f32[2,128,128]{2,1,0:T(8,128)S(1)} collective-permute-done((f32[2,128,128]{2,1,0:T(8,128)S(1)}, f32[2,128,128]{2,1,0:T(8,128)S(1)}, u32[]{:S(2)}, u32[]{:S(2)}) %collective-permute-start.11) | collective-permute-done | bytes 131104 | tf_op jit(solution)/shard_map/ppermute | solution.py:41
  80.0 2.2 %collective-permute-done.14 = f32[2,2048]{1,0:T(2,128)S(1)} collective-permute-done((f32[2,2048]{1,0:T(2,128)S(1)}, f32[2,2048]{1,0:T(2,128)S(1)}, u32[]{:S(2)}, u32[]{:S(2)}) %collective-permute-start.14) | collective-permute-done | bytes 16416 | tf_op jit(solution)/shard_map/ppermute | solution.py:41
  82.6 3.2 %collective-permute-start.16 = (bf16[2,2048]{1,0:T(2,128)(2,1)S(1)}, bf16[2,2048]{1,0:T(2,128)(2,1)S(1)}, u32[]{:S(2)}, u32[]{:S(2)}) collective-permute-start(bf16[2,2048]{1,0:T(2,128)(2,1)S(1)} %fusion.19), channel_id=1, source_target_pairs={{0,16},{1,17},{2,18},{3,19},{4,20},{5,21},{6,22},{7,23},{8,24},{9,... | collective-permute-start | bytes 24584 | tf_op jit(solution)/shard_map/ppermute | solution.py:41
  86.0 2.2 %collective-permute-start.29 = (f32[1,128]{1,0:T(1,128)S(1)}, f32[1,128]{1,0:T(1,128)S(1)}, u32[]{:S(2)}, u32[]{:S(2)}) collective-permute-start(f32[1,128]{1,0:T(1,128)S(1)} %bitcast.170), channel_id=1, source_target_pairs={{0,1},{1,0},{2,3},{3,2},{4,5},{5,4},{6,7},{7,6},{8,9},{9,8},{10,11... | collective-permute-start | bytes 1544 | tf_op jit(solution)/shard_map/ppermute | solution.py:41
  89.0 2.7 %collective-permute-start.22 = (bf16[4,2,2048]{2,1,0:T(2,128)(2,1)S(1)}, bf16[4,2,2048]{2,1,0:T(2,128)(2,1)S(1)}, u32[]{:S(2)}, u32[]{:S(2)}) collective-permute-start(bf16[4,2,2048]{2,1,0:T(2,128)(2,1)S(1)} %pad_maximum_fusion.6), channel_id=1, source_target_pairs={{0,224},{1,225},{2,226},{3,227},{4,228},{5,229},{6,230},{7,231},{8... | collective-permute-start | bytes 98312 | tf_op jit(solution)/shard_map/ppermute | solution.py:41
  93.0 2.7 %collective-permute-start.23 = (bf16[4,2,2048]{2,1,0:T(2,128)(2,1)S(1)}, bf16[4,2,2048]{2,1,0:T(2,128)(2,1)S(1)}, u32[]{:S(2)}, u32[]{:S(2)}) collective-permute-start(bf16[4,2,2048]{2,1,0:T(2,128)(2,1)S(1)} %collective-permute-done.22), channel_id=1, source_target_pairs={{0,224},{1,225},{2,226},{3,227},{4,228},{5,229},{6,230},{7,231},{8... | collective-permute-start | bytes 98312 | tf_op jit(solution)/shard_map/ppermute | solution.py:41
  97.0 2.8 %collective-permute-start.24 = (bf16[4,2,2048]{2,1,0:T(2,128)(2,1)S(1)}, bf16[4,2,2048]{2,1,0:T(2,128)(2,1)S(1)}, u32[]{:S(2)}, u32[]{:S(2)}) collective-permute-start(bf16[4,2,2048]{2,1,0:T(2,128)(2,1)S(1)} %collective-permute-done.23), channel_id=1, source_target_pairs={{0,224},{1,225},{2,226},{3,227},{4,228},{5,229},{6,230},{7,231},{8... | collective-permute-start | bytes 98312 | tf_op jit(solution)/shard_map/ppermute | solution.py:41
  101.0 3.9 %collective-permute-done.21 = bf16[4,2,2048]{2,1,0:T(2,128)(2,1)S(1)} collective-permute-done((bf16[4,2,2048]{2,1,0:T(2,128)(2,1)S(1)}, bf16[4,2,2048]{2,1,0:T(2,128)(2,1)S(1)}, u32[]{:S(2)}, u32[]{:S(2)}) %collective-permute-start.21) | collective-permute-done | bytes 32800 | tf_op jit(solution)/shard_map/ppermute | solution.py:41
  107.6 7.6 %collective-permute-start.25 = (f32[2,16,256]{2,1,0:T(8,128)S(1)}, f32[2,16,256]{2,1,0:T(8,128)S(1)}, u32[]{:S(2)}, u32[]{:S(2)}) collective-permute-start(f32[2,16,256]{2,1,0:T(8,128)S(1)} %dynamic-slice_bitcast_fusion.1), channel_id=1, source_target_pairs={{0,1},{1,0},{2,3},{3,2},{4,5},{5,4},{6,7},{7,6},{8,9},{9,8},{10,11... | collective-permute-start | bytes 98312 | tf_op jit(solution)/shard_map/ppermute | solution.py:41
  116.7 1.3 %collective-permute-start.28 = (f32[16,256]{1,0:T(8,128)S(1)}, f32[16,256]{1,0:T(8,128)S(1)}, u32[]{:S(2)}, u32[]{:S(2)}) collective-permute-start(f32[16,256]{1,0:T(8,128)S(1)} %get-tuple-element.59), channel_id=1, source_target_pairs={{0,6},{1,7},{2,4},{3,5},{4,2},{5,3},{6,0},{7,1},{8,14},{9,15},{10,... | collective-permute-start | bytes 49160 | tf_op jit(solution)/shard_map/ppermute | solution.py:41
  118.0 1.3 %collective-permute-start.27 = (f32[16,256]{1,0:T(8,128)S(1)}, f32[16,256]{1,0:T(8,128)S(1)}, u32[]{:S(2)}, u32[]{:S(2)}) collective-permute-start(f32[16,256]{1,0:T(8,128)S(1)} %get-tuple-element.60), channel_id=1, source_target_pairs={{0,4},{1,5},{2,6},{3,7},{4,0},{5,1},{6,2},{7,3},{8,12},{9,13},{10,... | collective-permute-start | bytes 49160 | tf_op jit(solution)/shard_map/ppermute | solution.py:41
  119.4 2.7 %collective-permute-done.27 = f32[16,256]{1,0:T(8,128)S(1)} collective-permute-done((f32[16,256]{1,0:T(8,128)S(1)}, f32[16,256]{1,0:T(8,128)S(1)}, u32[]{:S(2)}, u32[]{:S(2)}) %collective-permute-start.27) | collective-permute-done | bytes 16416 | tf_op jit(solution)/shard_map/ppermute | solution.py:41
  (146 shorter events, 22.5 us)
Async XLA Ops:
  1.7 5.7 %collective-permute-start = (bf16[16,2048]{1,0:T(8,128)(2,1)S(1)}, bf16[16,2048]{1,0:T(8,128)(2,1)S(1)}, u32[]{:S(2)}, u32[]{:S(2)}) collective-permute-start(bf16[16,2048]{1,0:T(8,128)(2,1)S(1)} %constant_dynamic-slice_fusion.6), channel_id=1, source_target_pairs={{0,8},{1,9},{2,10},{3,11},{4,12},{5,13},{6,14},{7,15},{8,16},{9,17... | collective-permute-start | bytes 196616 | tf_op jit(solution)/shard_map/ppermute | solution.py:41
  3.8 5.1 %collective-permute-start.1 = (bf16[16,2048]{1,0:T(8,128)(2,1)S(1)}, bf16[16,2048]{1,0:T(8,128)(2,1)S(1)}, u32[]{:S(2)}, u32[]{:S(2)}) collective-permute-start(bf16[16,2048]{1,0:T(8,128)(2,1)S(1)} %constant_dynamic-slice_fusion.6), channel_id=1, source_target_pairs={{0,16},{1,17},{2,18},{3,19},{4,20},{5,21},{6,22},{7,23},{8,24},{9,... | collective-permute-start | bytes 196616 | tf_op jit(solution)/shard_map/ppermute | solution.py:41
  6.3 3.4 %collective-permute-start.2 = (bf16[16,2048]{1,0:T(8,128)(2,1)S(1)}, bf16[16,2048]{1,0:T(8,128)(2,1)S(1)}, u32[]{:S(2)}, u32[]{:S(2)}) collective-permute-start(bf16[16,2048]{1,0:T(8,128)(2,1)S(1)} %constant_dynamic-slice_fusion.6), channel_id=1, source_target_pairs={{0,24},{1,25},{2,26},{3,27},{4,28},{5,29},{6,30},{7,31},{8,0},{9,1... | collective-permute-start | bytes 196616 | tf_op jit(solution)/shard_map/ppermute | solution.py:41
  9.7 10.7 %collective-permute-start.3 = (bf16[4,16,2048]{2,1,0:T(8,128)(2,1)S(1)}, bf16[4,16,2048]{2,1,0:T(8,128)(2,1)S(1)}, u32[]{:S(2)}, u32[]{:S(2)}) collective-permute-start(bf16[4,16,2048]{2,1,0:T(8,128)(2,1)S(1)} %pad_maximum_fusion.4), channel_id=1, source_target_pairs={{0,32},{1,33},{2,34},{3,35},{4,36},{5,37},{6,38},{7,39},{8,40},{9,... | collective-permute-start | bytes 786440 | tf_op jit(solution)/shard_map/ppermute | solution.py:41
  11.7 8.7 %collective-permute-start.7 = (bf16[4,16,2048]{2,1,0:T(8,128)(2,1)S(1)}, bf16[4,16,2048]{2,1,0:T(8,128)(2,1)S(1)}, u32[]{:S(2)}, u32[]{:S(2)}) collective-permute-start(bf16[4,16,2048]{2,1,0:T(8,128)(2,1)S(1)} %pad_maximum_fusion.4), channel_id=1, source_target_pairs={{0,224},{1,225},{2,226},{3,227},{4,228},{5,229},{6,230},{7,231},{8... | collective-permute-start | bytes 786440 | tf_op jit(solution)/shard_map/ppermute | solution.py:41
  16.4 32.4 %copy-start.4 = (bf16[128,128]{1,0:T(8,128)(2,1)S(1)}, bf16[128,128]{1,0:T(8,128)(2,1)}, u32[]{:S(2)}) copy-start(bf16[128,128]{1,0:T(8,128)(2,1)} %param.24) | copy-start | bytes 98308
  20.4 6.4 %collective-permute-start.4 = (bf16[4,16,2048]{2,1,0:T(8,128)(2,1)S(1)}, bf16[4,16,2048]{2,1,0:T(8,128)(2,1)S(1)}, u32[]{:S(2)}, u32[]{:S(2)}) collective-permute-start(bf16[4,16,2048]{2,1,0:T(8,128)(2,1)S(1)} %collective-permute-done.3), channel_id=1, source_target_pairs={{0,32},{1,33},{2,34},{3,35},{4,36},{5,37},{6,38},{7,39},{8,40},{9,... | collective-permute-start | bytes 786440 | tf_op jit(solution)/shard_map/ppermute | solution.py:41
  20.4 6.4 %collective-permute-start.8 = (bf16[4,16,2048]{2,1,0:T(8,128)(2,1)S(1)}, bf16[4,16,2048]{2,1,0:T(8,128)(2,1)S(1)}, u32[]{:S(2)}, u32[]{:S(2)}) collective-permute-start(bf16[4,16,2048]{2,1,0:T(8,128)(2,1)S(1)} %collective-permute-done.7), channel_id=1, source_target_pairs={{0,224},{1,225},{2,226},{3,227},{4,228},{5,229},{6,230},{7,231},{8... | collective-permute-start | bytes 786440 | tf_op jit(solution)/shard_map/ppermute | solution.py:41
  26.8 6.4 %collective-permute-start.5 = (bf16[4,16,2048]{2,1,0:T(8,128)(2,1)S(1)}, bf16[4,16,2048]{2,1,0:T(8,128)(2,1)S(1)}, u32[]{:S(2)}, u32[]{:S(2)}) collective-permute-start(bf16[4,16,2048]{2,1,0:T(8,128)(2,1)S(1)} %collective-permute-done.4), channel_id=1, source_target_pairs={{0,32},{1,33},{2,34},{3,35},{4,36},{5,37},{6,38},{7,39},{8,40},{9,... | collective-permute-start | bytes 786440 | tf_op jit(solution)/shard_map/ppermute | solution.py:41
  26.8 13.4 %collective-permute-start.9 = (bf16[4,16,2048]{2,1,0:T(8,128)(2,1)S(1)}, bf16[4,16,2048]{2,1,0:T(8,128)(2,1)S(1)}, u32[]{:S(2)}, u32[]{:S(2)}) collective-permute-start(bf16[4,16,2048]{2,1,0:T(8,128)(2,1)S(1)} %collective-permute-done.8), channel_id=1, source_target_pairs={{0,224},{1,225},{2,226},{3,227},{4,228},{5,229},{6,230},{7,231},{8... | collective-permute-start | bytes 786440 | tf_op jit(solution)/shard_map/ppermute | solution.py:41
  33.2 6.9 %collective-permute-start.6 = (bf16[4,16,2048]{2,1,0:T(8,128)(2,1)S(1)}, bf16[4,16,2048]{2,1,0:T(8,128)(2,1)S(1)}, u32[]{:S(2)}, u32[]{:S(2)}) collective-permute-start(bf16[4,16,2048]{2,1,0:T(8,128)(2,1)S(1)} %collective-permute-done.5), channel_id=1, source_target_pairs={{0,32},{1,33},{2,34},{3,35},{4,36},{5,37},{6,38},{7,39},{8,40},{9,... | collective-permute-start | bytes 786440 | tf_op jit(solution)/shard_map/ppermute | solution.py:41
  40.3 15.3 %collective-permute-start.10 = (bf16[512,2048]{1,0:T(8,128)(2,1)S(1)}, bf16[512,2048]{1,0:T(8,128)(2,1)}, u32[]{:S(2)}, u32[]{:S(2)}) collective-permute-start(bf16[512,2048]{1,0:T(8,128)(2,1)S(1)} %bitcast.138), channel_id=1, source_target_pairs={{0,1},{1,0},{2,3},{3,2},{4,5},{5,4},{6,7},{7,6},{8,9},{9,8},{10,11... | collective-permute-start | bytes 6291464 | tf_op jit(solution)/shard_map/ppermute | solution.py:41
  63.4 14.1 %collective-permute-start.12 = (f32[2,128,256]{1,2,0:T(8,128)S(1)}, f32[2,128,256]{1,2,0:T(8,128)S(1)}, u32[]{:S(2)}, u32[]{:S(2)}) collective-permute-start(f32[2,128,256]{1,2,0:T(8,128)S(1)} %bitcast.145), channel_id=1, source_target_pairs={{0,4},{1,5},{2,6},{3,7},{4,0},{5,1},{6,2},{7,3},{8,12},{9,13},{10,... | collective-permute-start | bytes 786440 | tf_op jit(solution)/shard_map/ppermute | solution.py:41
  70.5 6.8 %collective-permute-start.11 = (f32[2,128,128]{2,1,0:T(8,128)S(1)}, f32[2,128,128]{2,1,0:T(8,128)S(1)}, u32[]{:S(2)}, u32[]{:S(2)}) collective-permute-start(f32[2,128,128]{2,1,0:T(8,128)S(1)} %dynamic-slice_bitcast_fusion), channel_id=1, source_target_pairs={{0,4},{1,5},{2,6},{3,7},{4,0},{5,1},{6,2},{7,3},{8,12},{9,13},{10,... | collective-permute-start | bytes 393224 | tf_op jit(solution)/shard_map/ppermute | solution.py:41
  77.8 1.6 %collective-permute-start.13 = (f32[2,2,2048]{2,0,1:T(2,128)S(1)}, f32[2,2,2048]{2,0,1:T(2,128)S(1)}, u32[]{:S(2)}, u32[]{:S(2)}) collective-permute-start(f32[2,2,2048]{2,0,1:T(2,128)S(1)} %bitcast.158), channel_id=1, source_target_pairs={{0,1},{1,0},{2,3},{3,2},{4,5},{5,4},{6,7},{7,6},{8,9},{9,8},{10,11... | collective-permute-start | bytes 98312 | tf_op jit(solution)/shard_map/ppermute | solution.py:41
  79.5 2.7 %collective-permute-start.14 = (f32[2,2048]{1,0:T(2,128)S(1)}, f32[2,2048]{1,0:T(2,128)S(1)}, u32[]{:S(2)}, u32[]{:S(2)}) collective-permute-start(f32[2,2048]{1,0:T(2,128)S(1)} %bitcast.169), channel_id=1, source_target_pairs={{0,2},{1,3},{2,0},{3,1},{4,6},{5,7},{6,4},{7,5},{8,10},{9,11},{10,... | collective-permute-start | bytes 49160 | tf_op jit(solution)/shard_map/ppermute | solution.py:41
  82.2 6.2 %collective-permute-start.15 = (bf16[2,2048]{1,0:T(2,128)(2,1)S(1)}, bf16[2,2048]{1,0:T(2,128)(2,1)S(1)}, u32[]{:S(2)}, u32[]{:S(2)}) collective-permute-start(bf16[2,2048]{1,0:T(2,128)(2,1)S(1)} %fusion.19), channel_id=1, source_target_pairs={{0,8},{1,9},{2,10},{3,11},{4,12},{5,13},{6,14},{7,15},{8,16},{9,17... | collective-permute-start | bytes 24584 | tf_op jit(solution)/shard_map/ppermute | solution.py:41
  82.6 5.9 %collective-permute-start.16 = (bf16[2,2048]{1,0:T(2,128)(2,1)S(1)}, bf16[2,2048]{1,0:T(2,128)(2,1)S(1)}, u32[]{:S(2)}, u32[]{:S(2)}) collective-permute-start(bf16[2,2048]{1,0:T(2,128)(2,1)S(1)} %fusion.19), channel_id=1, source_target_pairs={{0,16},{1,17},{2,18},{3,19},{4,20},{5,21},{6,22},{7,23},{8,24},{9,... | collective-permute-start | bytes 24584 | tf_op jit(solution)/shard_map/ppermute | solution.py:41
  85.8 2.8 %collective-permute-start.17 = (bf16[2,2048]{1,0:T(2,128)(2,1)S(1)}, bf16[2,2048]{1,0:T(2,128)(2,1)S(1)}, u32[]{:S(2)}, u32[]{:S(2)}) collective-permute-start(bf16[2,2048]{1,0:T(2,128)(2,1)S(1)} %fusion.19), channel_id=1, source_target_pairs={{0,24},{1,25},{2,26},{3,27},{4,28},{5,29},{6,30},{7,31},{8,0},{9,1... | collective-permute-start | bytes 24584 | tf_op jit(solution)/shard_map/ppermute | solution.py:41
  86.0 29.1 %collective-permute-start.29 = (f32[1,128]{1,0:T(1,128)S(1)}, f32[1,128]{1,0:T(1,128)S(1)}, u32[]{:S(2)}, u32[]{:S(2)}) collective-permute-start(f32[1,128]{1,0:T(1,128)S(1)} %bitcast.170), channel_id=1, source_target_pairs={{0,1},{1,0},{2,3},{3,2},{4,5},{5,4},{6,7},{7,6},{8,9},{9,8},{10,11... | collective-permute-start | bytes 1544 | tf_op jit(solution)/shard_map/ppermute | solution.py:41
  88.7 4.3 %collective-permute-start.18 = (bf16[4,2,2048]{2,1,0:T(2,128)(2,1)S(1)}, bf16[4,2,2048]{2,1,0:T(2,128)(2,1)S(1)}, u32[]{:S(2)}, u32[]{:S(2)}) collective-permute-start(bf16[4,2,2048]{2,1,0:T(2,128)(2,1)S(1)} %pad_maximum_fusion.6), channel_id=1, source_target_pairs={{0,32},{1,33},{2,34},{3,35},{4,36},{5,37},{6,38},{7,39},{8,40},{9,... | collective-permute-start | bytes 98312 | tf_op jit(solution)/shard_map/ppermute | solution.py:41
  89.0 4.0 %collective-permute-start.22 = (bf16[4,2,2048]{2,1,0:T(2,128)(2,1)S(1)}, bf16[4,2,2048]{2,1,0:T(2,128)(2,1)S(1)}, u32[]{:S(2)}, u32[]{:S(2)}) collective-permute-start(bf16[4,2,2048]{2,1,0:T(2,128)(2,1)S(1)} %pad_maximum_fusion.6), channel_id=1, source_target_pairs={{0,224},{1,225},{2,226},{3,227},{4,228},{5,229},{6,230},{7,231},{8... | collective-permute-start | bytes 98312 | tf_op jit(solution)/shard_map/ppermute | solution.py:41
  93.0 4.0 %collective-permute-start.19 = (bf16[4,2,2048]{2,1,0:T(2,128)(2,1)S(1)}, bf16[4,2,2048]{2,1,0:T(2,128)(2,1)S(1)}, u32[]{:S(2)}, u32[]{:S(2)}) collective-permute-start(bf16[4,2,2048]{2,1,0:T(2,128)(2,1)S(1)} %collective-permute-done.18), channel_id=1, source_target_pairs={{0,32},{1,33},{2,34},{3,35},{4,36},{5,37},{6,38},{7,39},{8,40},{9,... | collective-permute-start | bytes 98312 | tf_op jit(solution)/shard_map/ppermute | solution.py:41
  93.0 4.0 %collective-permute-start.23 = (bf16[4,2,2048]{2,1,0:T(2,128)(2,1)S(1)}, bf16[4,2,2048]{2,1,0:T(2,128)(2,1)S(1)}, u32[]{:S(2)}, u32[]{:S(2)}) collective-permute-start(bf16[4,2,2048]{2,1,0:T(2,128)(2,1)S(1)} %collective-permute-done.22), channel_id=1, source_target_pairs={{0,224},{1,225},{2,226},{3,227},{4,228},{5,229},{6,230},{7,231},{8... | collective-permute-start | bytes 98312 | tf_op jit(solution)/shard_map/ppermute | solution.py:41
  96.9 4.0 %collective-permute-start.20 = (bf16[4,2,2048]{2,1,0:T(2,128)(2,1)S(1)}, bf16[4,2,2048]{2,1,0:T(2,128)(2,1)S(1)}, u32[]{:S(2)}, u32[]{:S(2)}) collective-permute-start(bf16[4,2,2048]{2,1,0:T(2,128)(2,1)S(1)} %collective-permute-done.19), channel_id=1, source_target_pairs={{0,32},{1,33},{2,34},{3,35},{4,36},{5,37},{6,38},{7,39},{8,40},{9,... | collective-permute-start | bytes 98312 | tf_op jit(solution)/shard_map/ppermute | solution.py:41
  97.0 8.0 %collective-permute-start.24 = (bf16[4,2,2048]{2,1,0:T(2,128)(2,1)S(1)}, bf16[4,2,2048]{2,1,0:T(2,128)(2,1)S(1)}, u32[]{:S(2)}, u32[]{:S(2)}) collective-permute-start(bf16[4,2,2048]{2,1,0:T(2,128)(2,1)S(1)} %collective-permute-done.23), channel_id=1, source_target_pairs={{0,224},{1,225},{2,226},{3,227},{4,228},{5,229},{6,230},{7,231},{8... | collective-permute-start | bytes 98312 | tf_op jit(solution)/shard_map/ppermute | solution.py:41
  100.9 4.0 %collective-permute-start.21 = (bf16[4,2,2048]{2,1,0:T(2,128)(2,1)S(1)}, bf16[4,2,2048]{2,1,0:T(2,128)(2,1)S(1)}, u32[]{:S(2)}, u32[]{:S(2)}) collective-permute-start(bf16[4,2,2048]{2,1,0:T(2,128)(2,1)S(1)} %collective-permute-done.20), channel_id=1, source_target_pairs={{0,32},{1,33},{2,34},{3,35},{4,36},{5,37},{6,38},{7,39},{8,40},{9,... | collective-permute-start | bytes 98312 | tf_op jit(solution)/shard_map/ppermute | solution.py:41
  107.6 8.4 %collective-permute-start.25 = (f32[2,16,256]{2,1,0:T(8,128)S(1)}, f32[2,16,256]{2,1,0:T(8,128)S(1)}, u32[]{:S(2)}, u32[]{:S(2)}) collective-permute-start(f32[2,16,256]{2,1,0:T(8,128)S(1)} %dynamic-slice_bitcast_fusion.1), channel_id=1, source_target_pairs={{0,1},{1,0},{2,3},{3,2},{4,5},{5,4},{6,7},{7,6},{8,9},{9,8},{10,11... | collective-permute-start | bytes 98312 | tf_op jit(solution)/shard_map/ppermute | solution.py:41
  115.2 4.2 %collective-permute-start.30 = (f32[1,128]{1,0:T(1,128)S(1)}, f32[1,128]{1,0:T(1,128)S(1)}, u32[]{:S(2)}, u32[]{:S(2)}) collective-permute-start(f32[1,128]{1,0:T(1,128)S(1)} %bitcast_add_fusion.4), channel_id=1, source_target_pairs={{0,2},{1,3},{2,0},{3,1},{4,6},{5,7},{6,4},{7,5},{8,10},{9,11},{10,... | collective-permute-start | bytes 1544 | tf_op jit(solution)/shard_map/ppermute | solution.py:41
  116.0 3.4 %collective-permute-start.26 = (f32[16,256]{1,0:T(8,128)S(1)}, f32[16,256]{1,0:T(8,128)S(1)}, u32[]{:S(2)}, u32[]{:S(2)}) collective-permute-start(f32[16,256]{1,0:T(8,128)S(1)} %get-tuple-element.59), channel_id=1, source_target_pairs={{0,2},{1,3},{2,0},{3,1},{4,6},{5,7},{6,4},{7,5},{8,10},{9,11},{10,... | collective-permute-start | bytes 49160 | tf_op jit(solution)/shard_map/ppermute | solution.py:41
  116.7 5.4 %collective-permute-start.28 = (f32[16,256]{1,0:T(8,128)S(1)}, f32[16,256]{1,0:T(8,128)S(1)}, u32[]{:S(2)}, u32[]{:S(2)}) collective-permute-start(f32[16,256]{1,0:T(8,128)S(1)} %get-tuple-element.59), channel_id=1, source_target_pairs={{0,6},{1,7},{2,4},{3,5},{4,2},{5,3},{6,0},{7,1},{8,14},{9,15},{10,... | collective-permute-start | bytes 49160 | tf_op jit(solution)/shard_map/ppermute | solution.py:41
  118.0 4.1 %collective-permute-start.27 = (f32[16,256]{1,0:T(8,128)S(1)}, f32[16,256]{1,0:T(8,128)S(1)}, u32[]{:S(2)}, u32[]{:S(2)}) collective-permute-start(f32[16,256]{1,0:T(8,128)S(1)} %get-tuple-element.60), channel_id=1, source_target_pairs={{0,4},{1,5},{2,6},{3,7},{4,0},{5,1},{6,2},{7,3},{8,12},{9,13},{10,... | collective-permute-start | bytes 49160 | tf_op jit(solution)/shard_map/ppermute | solution.py:41
  (8 other events, 87.9 us)

commit v2 on v1

v2 whole, which is shorter than its diff:
```python
import math

import jax
import jax.numpy as jnp
from jax import lax
from jax.experimental import pallas as pl
from jax.experimental.pallas import tpu as pltpu
from jax.sharding import PartitionSpec as P

PROBE_ROWS = 64
PROBE_COLUMNS = 128
K = 8192
AXES = ("demo", "fsdp", "sketch")
Z, X, F, S = 8, 4, 2, 4
ROWS = 16
LEFT = 2 * PROBE_ROWS
RIGHT = 2 * PROBE_COLUMNS
CHUNK = 512
FIRST = ((0,), (0,))
LAST = ((1,), (1,))


def pairs(step):
    out = []
    for z in range(Z):
        for x in range(X):
            for f in range(F):
                for s in range(S):
                    z2, x2, f2, s2 = step(z, x, f, s)
                    source = ((z * X + x) * F + f) * S + s
                    target = (((z2 % Z) * X + x2 % X) * F + f2) * S + s2
                    out.append((source, target))
    return out


CORE = pairs(lambda z, x, f, s: (z, x, f, s ^ 1))
NEAR = pairs(lambda z, x, f, s: (z, x, f, s ^ 2))
CORE_NEAR = pairs(lambda z, x, f, s: (z, x, f, s ^ 3))
FAR = pairs(lambda z, x, f, s: (z, x, f ^ 1, s))
FAR_NEAR = pairs(lambda z, x, f, s: (z, x, f ^ 1, s ^ 2))


def shift(dz, dx):
    return pairs(lambda z, x, f, s: (z + dz, x + dx, f, s))


def send(value, moves):
    return lax.ppermute(value, AXES, moves)


def dot(a, b, contract):
    return lax.dot_general(a, b, (contract, ((), ())), preferred_element_type=jnp.float32)


def cost(flops, moved):
    return pl.CostEstimate(flops=flops, bytes_accessed=moved, transcendentals=0)


def shape(dims, kind=jnp.float32):
    return jax.ShapeDtypeStruct(dims, kind)


def weights_kernel(order_ref, contracting_ref, expanding_ref, queries_ref, weights_ref, squares_ref):
    columns = Z * X * ROWS
    place = order_ref[...]
    kind = lax.broadcasted_iota(jnp.int32, (1, columns), 1) % ROWS

    def chosen(count, width, start):
        inside = (kind >= start) & (kind < start + width)
        target = jnp.where(inside, place * width + kind - start, -1)
        hit = lax.broadcasted_iota(jnp.int32, (count, columns), 0) == target
        return jnp.where(hit, 1.0, 0.0).astype(jnp.bfloat16)

    weights_ref[0:PROBE_ROWS] = chosen(PROBE_ROWS, 2, 12)
    weights_ref[PROBE_ROWS:LEFT] = dot(expanding_ref[...], chosen(128, 4, 0), FIRST).astype(
        jnp.bfloat16
    )
    weights_ref[LEFT : LEFT + PROBE_COLUMNS] = dot(
        contracting_ref[...], chosen(128, 4, 4), FIRST
    ).astype(jnp.bfloat16)
    weights_ref[LEFT + PROBE_COLUMNS :] = chosen(PROBE_COLUMNS, 4, 8)
    values = queries_ref[...].astype(jnp.float32)
    squares = jnp.sum(values * values, axis=1, keepdims=True)
    squares_ref[...] = jnp.broadcast_to(squares, (128, 128)).T[0:8]


def maps_kernel(weights_ref, *refs):
    rows = jnp.concatenate([ref[...] for ref in refs[:-1]], axis=0)
    refs[-1][...] = dot(weights_ref[...], rows, ((1,), (0,))).astype(jnp.bfloat16)


def own_kernel(info_ref, act_ref, cot_ref, maps_ref, left_ref, right_ref):
    left = dot(act_ref[...], maps_ref[0:LEFT], LAST)
    right = dot(cot_ref[...], maps_ref[LEFT:], LAST)

    @pl.when(pl.program_id(0) == 0)
    def _():
        left_ref[...] = left
        right_ref[...] = right

    @pl.when(pl.program_id(0) > 0)
    def _():
        left_ref[...] += left
        right_ref[...] += right


def other_kernel(info_ref, tokens_ref, maps_ref, part_ref, keep_ref, give_ref, total_ref):
    value = dot(tokens_ref[...], maps_ref[...], LAST)
    step = pl.program_id(0)

    @pl.when(step == 0)
    def _():
        total_ref[...] = part_ref[...] + value

    @pl.when(step > 0)
    def _():
        total_ref[...] += value

    @pl.when(step == pl.num_programs(0) - 1)
    def _():
        half = total_ref.shape[0] // F
        f = info_ref[1]
        keep_ref[...] = total_ref[pl.ds(pl.multiple_of(f * half, half), half)]
        give_ref[...] = total_ref[pl.ds(pl.multiple_of((1 - f) * half, half), half)]


def outer_kernel(
    info_ref, keep_left, got_left, keep_right, got_right, own_ref, core_ref, near_ref, both_ref, total_ref
):
    demos = total_ref.shape[0]
    tokens = keep_left.shape[0] // demos
    s = info_ref[2]
    position = s * tokens + lax.broadcasted_iota(jnp.int32, (tokens, 1), 0)
    for j in range(demos):
        at = slice(j * tokens, (j + 1) * tokens)
        padding = jnp.where(position < info_ref[3 + j], 1.0, 0.0)
        left = (keep_left[at] + got_left[at]).astype(jnp.bfloat16)
        right = ((keep_right[at] + got_right[at]) * padding).astype(jnp.bfloat16)
        total_ref[j] = dot(left[:, :PROBE_ROWS], right[:, :PROBE_COLUMNS], FIRST) + dot(
            left[:, PROBE_ROWS:], right[:, PROBE_COLUMNS:], FIRST
        )
    rows = PROBE_ROWS // S
    for k, ref in enumerate((own_ref, core_ref, near_ref, both_ref)):
        start = pl.multiple_of((s ^ k) * rows, rows)
        for j in range(demos):
            ref[j] = total_ref[j, pl.ds(start, rows)]


def inner_kernel(info_ref, demos_ref, queries_ref, squares_ref, keep_ref, give_ref, total_ref):
    sketches = demos_ref[...]
    nq = queries_ref.shape[0]
    values = sketches.astype(jnp.float32)
    total_ref[:, :nq] = dot(sketches, queries_ref[...], LAST)
    total_ref[:, nq:] = jnp.broadcast_to(
        jnp.sum(values * values, axis=1, keepdims=True), (sketches.shape[0], nq)
    )
    s = info_ref[2]
    rows = sketches.shape[0] // S
    for ref, at, k in ((keep_ref, 0, 0), (keep_ref, 1, 2), (give_ref, 0, 1), (give_ref, 1, 3)):
        start = pl.multiple_of((s ^ k) * rows, rows)
        ref[at, 0:rows] = total_ref[pl.ds(start, rows)]
        ref[at, rows:, :nq] = squares_ref[...]
        ref[at, rows:, nq:] = squares_ref[...]


def whole(count):
    return [pl.BlockSpec(memory_space=pltpu.VMEM)] * count


def gather_z(block):
    got = {0: block}
    up = down = block
    for k in range(1, Z // 2 + 1):
        up = send(up, shift(1, 0))
        got[k] = up
        if k < Z // 2:
            down = send(down, shift(-1, 0))
            got[Z - k] = down
    return [got[k] for k in range(Z)]


def shards(
    activations,
    cotangents,
    lengths,
    lowrank_contract_matrix,
    lowrank_expand_matrix,
    input_feature_sketch,
    latent_random_map_contracting,
    latent_random_map_expanding,
    output_feature_sketch,
    queries,
):
    demo_count, tok_local, feat = activations.shape
    own = demo_count // F
    tokens = demo_count * tok_local
    half = feat // 2
    steps = half // CHUNK
    nq = queries.shape[0]
    demo = lax.axis_index("demo")
    z, x = demo // X, demo % X
    f = lax.axis_index("fsdp")
    s = lax.axis_index("sketch")
    core = s % 2
    own_lengths = lax.dynamic_slice_in_dim(lengths, f * own, own)
    info = jnp.concatenate([jnp.stack([core, f, s]).astype(jnp.int32), own_lengths])
    z_order = (z - jnp.arange(Z)) % Z
    x_order = (x - jnp.arange(X)) % X
    order = jnp.repeat((z_order[:, None] * X + x_order[None, :]).reshape(-1), ROWS)[None, :]

    block = jnp.concatenate(
        [
            lowrank_contract_matrix.T,
            lowrank_expand_matrix.T,
            output_feature_sketch.T,
            input_feature_sketch.T,
            jnp.zeros((2, feat), jnp.bfloat16),
        ],
        axis=0,
    )
    block = lax.dynamic_slice_in_dim(block, core * half, half, axis=1)
    weights, query_squares = pl.pallas_call(
        weights_kernel,
        out_shape=[shape((LEFT + RIGHT, Z * X * ROWS), jnp.bfloat16), shape((8, 128))],
        in_specs=whole(4),
        out_specs=whole(2),
        cost_estimate=cost(10**8, 10**6),
    )(
        order.astype(jnp.int32),
        latent_random_map_contracting,
        latent_random_map_expanding,
        queries,
    )
    line = jnp.concatenate([block] + [send(block, shift(0, k)) for k in range(1, X)])
    line, weights, query_squares = lax.optimization_barrier((line, weights, query_squares))
    arrived = gather_z(line)
    maps = pl.pallas_call(
        maps_kernel,
        grid=(steps,),
        out_shape=shape((LEFT + RIGHT, half), jnp.bfloat16),
        in_specs=[pl.BlockSpec((LEFT + RIGHT, Z * X * ROWS), lambda j: (0, 0))]
        + [pl.BlockSpec((X * ROWS, CHUNK), lambda j: (0, j))] * Z,
        out_specs=pl.BlockSpec((LEFT + RIGHT, CHUNK), lambda j: (0, j)),
        cost_estimate=cost(2 * 384 * 512 * 2048, 4 * 10**6),
    )(weights, *arrived)
    other_maps = send(maps, CORE)

    act = activations.reshape(tokens, feat)
    cot = cotangents.reshape(tokens, feat)
    left_part, right_part = pl.pallas_call(
        own_kernel,
        out_shape=[shape((tokens, LEFT)), shape((tokens, RIGHT))],
        grid_spec=pltpu.PrefetchScalarGridSpec(
            num_scalar_prefetch=1,
            grid=(steps,),
            in_specs=[
                pl.BlockSpec((tokens, CHUNK), lambda j, info: (0, info[0] * steps + j)),
                pl.BlockSpec((tokens, CHUNK), lambda j, info: (0, info[0] * steps + j)),
                pl.BlockSpec((LEFT + RIGHT, CHUNK), lambda j, info: (0, j)),
            ],
            out_specs=[
                pl.BlockSpec((tokens, LEFT), lambda j, info: (0, 0)),
                pl.BlockSpec((tokens, RIGHT), lambda j, info: (0, 0)),
            ],
        ),
        cost_estimate=cost(2 * 512 * 384 * 2048, 6 * 10**6),
    )(info, act, cot, maps)

    def other_half(values, part, first, width):
        return pl.pallas_call(
            other_kernel,
            out_shape=[shape((tokens // F, width))] * 2,
            grid_spec=pltpu.PrefetchScalarGridSpec(
                num_scalar_prefetch=1,
                grid=(steps,),
                in_specs=[
                    pl.BlockSpec((tokens, CHUNK), lambda j, info: (0, (1 - info[0]) * steps + j)),
                    pl.BlockSpec(
                        (pl.Element(width), pl.Element(CHUNK)), lambda j, info: (first, j * CHUNK)
                    ),
                    pl.BlockSpec((tokens, width), lambda j, info: (0, 0)),
                ],
                out_specs=[pl.BlockSpec((tokens // F, width), lambda j, info: (0, 0))] * 2,
                scratch_shapes=[pltpu.VMEM((tokens, width), jnp.float32)],
            ),
            cost_estimate=cost(2 * 512 * width * 2048, 4 * 10**6),
        )(info, values, other_maps, part)

    keep_right, give_right = other_half(cot, right_part, LEFT, RIGHT)
    got_right = send(give_right, FAR)
    keep_left, give_left = other_half(act, left_part, 0, LEFT)
    got_left = send(give_left, FAR)

    rows = PROBE_ROWS // S
    mine, to_core, to_near, to_both = pl.pallas_call(
        outer_kernel,
        out_shape=[shape((own, rows, PROBE_COLUMNS))] * 4,
        in_specs=[pl.BlockSpec(memory_space=pltpu.SMEM)] + whole(4),
        out_specs=whole(4),
        scratch_shapes=[pltpu.VMEM((own, PROBE_ROWS, PROBE_COLUMNS), jnp.float32)],
        cost_estimate=cost(2 * 10**7, 10**6),
    )(info, keep_left, got_left, keep_right, got_right)
    summed = (mine + send(to_core, CORE)) + (send(to_near, NEAR) + send(to_both, CORE_NEAR))
    demo_sketch = summed.astype(jnp.bfloat16).reshape(own, K // S)

    copies = jnp.broadcast_to(demo_sketch[None], (Z * X, own, K // S))
    every_demo = lax.all_to_all(copies, "demo", 0, 0).reshape(Z * X * own, K // S)
    block_rows = Z * X * own // S
    keep, give = pl.pallas_call(
        inner_kernel,
        out_shape=[shape((2, block_rows + 8, 2 * nq))] * 2,
        in_specs=[pl.BlockSpec(memory_space=pltpu.SMEM)] + whole(3),
        out_specs=whole(2),
        scratch_shapes=[pltpu.VMEM((Z * X * own, 2 * nq), jnp.float32)],
        cost_estimate=cost(4 * 10**7, 10**6),
    )(info, every_demo, queries, query_squares)
    pair = keep + send(give, CORE)
    here = pair[0] + send(pair[1], NEAR)
    there = send(pair[0], FAR) + send(pair[1], FAR_NEAR)
    query_squares = here[block_rows : block_rows + 1, :nq]
    here, there = here[:block_rows], there[:block_rows]
    total = jnp.stack([jnp.where(f == 0, here, there), jnp.where(f == 0, there, here)])
    total = total.reshape(F, block_rows // own, own, 2 * nq).transpose(1, 0, 2, 3)
    total = total.reshape(F * block_rows, 2 * nq)
    demo_norm = jnp.sqrt(total[:, nq:] + 1e-06)
    query_norm = jnp.sqrt(query_squares + 1e-06)
    return math.sqrt(K) * total[:, :nq] / (demo_norm * query_norm)


def solution(mesh):
    placed = (
        P("demo", "sketch", "fsdp"),
        P("demo", "sketch", "fsdp"),
        P("demo"),
        P("fsdp", "demo"),
        P("fsdp", "demo"),
        P("fsdp", "demo"),
        P(),
        P(),
        P("fsdp", "demo"),
        P("demo", "sketch"),
    )
    return jax.shard_map(
        shards, mesh=mesh, in_specs=placed, out_specs=P("sketch", "demo"), check_vma=False
    )
```

time: 123 us -> 122 us (level)
  Pallas kernels: 0 us -> 26.7 us
  starting transfers between devices: 54 us -> 33.1 us
  blocking collectives: 0 us -> 18.8 us
  matrix products: 9.27 us -> 0 us
  waiting for transfers between devices: 40.5 us -> 31.4 us
  local copies, waits for them, and re-layouts: 12.1 us -> 7.65 us
  other arithmetic: 6.39 us -> 2.87 us
    pallas_call x0 -> x7, Pallas kernels: none -> 26.7 us  [the longest x2 9.85 us: other_half(): pl.pallas_call(other_kernel, out_shape=[shape((tokens // F, width))] * 2,...]
    ppermute x31 -> x20, starting transfers between devices: 54 us -> 33.1 us  [send(): return lax.ppermute(value, AXES, moves)]
    all_to_all x0 -> x1, blocking collectives: none -> 18.8 us  [shards(): lax.all_to_all(copies, 'demo', 0, 0).reshape(Z * X * own, K // S)]
    dot_general x6 -> x0, matrix products: 9.27 us -> none  [the longest x1 3.88 us: shards(): lax.dot_general(activations.reshape(tok_rows, feat), maps[:2 * PROBE_ROWS...]
    ppermute x31 -> x20, waiting for transfers between devices: 40.5 us -> 31.4 us  [send(): return lax.ppermute(value, AXES, moves)]
    another operation x5 -> x0, other arithmetic: 4.35 us -> none
    scatter x3 -> x0, local copies, waits for them, and re-layouts: 2.62 us -> none  [the longest x1 2.48 us: map_weights(): weights.at[:PROBE_ROWS, :, 12:14]]
    gather x7 -> x0, local copies, waits for them, and re-layouts: 2.53 us -> none  [the longest x3 1.3 us: map_weights(): weights = jnp.take(jnp.take(weights, z_order, axis=1), x_order, axis=2)]
  transfers between devices with their start and end apart: 31 -> 20, of which waited for: 16 -> 9; matrix products, arithmetic and copies ran while one was open for 14% -> 2% of each run, Pallas kernels for 0% -> 10%
where the time goes in v2:
time: 122 us; the launch traced here: 121 us
  starting transfers between devices  33.1 us (27%)
  waiting for transfers between devices  31.4 us (26%)
  Pallas kernels  26.7 us (22%)
  blocking collectives  18.8 us (15%)
  local copies, waits for them, and re-layouts  7.65 us (6%)
  other arithmetic  2.87 us (2%)
    ppermute x20, starting transfers between devices, send(): return lax.ppermute(value, AXES, moves)  33.1 us
    ppermute x20, waiting for transfers between devices, send(): return lax.ppermute(value, AXES, moves)  31.4 us
    all_to_all x1, blocking collectives, shards(): lax.all_to_all(copies, 'demo', 0, 0).reshape(Z * X * own, K // S)  18.8 us
    pallas_call x2, Pallas kernels, other_half(): pl.pallas_call(other_kernel, out_shape=[shape((tokens // F, width))] * 2,...  9.85 us
    pallas_call x1, Pallas kernels, shards(): pl.pallas_call(own_kernel, out_shape=[shape((tokens, LEFT)), shape((token...  5.86 us
    pallas_call x1, Pallas kernels, shards(): pl.pallas_call(maps_kernel, grid=(steps,), out_shape=shape((LEFT + RIGHT,...  4.77 us
    unnamed x26, local copies, waits for them, and re-layouts  4.09 us
  transfers between devices with their start and end apart: 20, of which 9 were waited for; matrix products, arithmetic and copies ran while one was open for 2% of the time, Pallas kernels for 10%

profile of v2, /device:TPU:1, one launch (start us, length us, event | category | flops | bytes accessed | tf_op | source)
XLA Modules:
  0.0 120.8 jit_solution(304927148214029750)
XLA Ops:
  0.0 1.6 %concatenate.11 = bf16[16,4096]{1,0:T(8,128)(2,1)S(1)} concatenate(bf16[4,4096]{1,0:T(4,128)(2,1)} %bitcast.29, bf16[4,4096]{1,0:T(4,128)(2,1)} %bitcast.30, bf16[4,4096]{1,0:T(4,128)(2,1)} %bitcast.31, bf16[2,4096]{1,0:T(2,128)(2,1)} %bitcast.32, bf16[2,4096]{1,0:T(2,128)(2,1)S(1)} %broadcast_in_dim.15), dimensions={0} | concatenate | bytes 262144 | tf_op jit(solution)/shard_map/concatenate | solution.py:211
  1.7 3.4 %collective-permute-start.2 = (bf16[16,2048]{1,0:T(8,128)(2,1)S(1)}, bf16[16,2048]{1,0:T(8,128)(2,1)S(1)}, u32[]{:S(2)}, u32[]{:S(2)}) collective-permute-start(bf16[16,2048]{1,0:T(8,128)(2,1)S(1)} %constant_dynamic-slice_fusion), channel_id=1, source_target_pairs={{0,24},{1,25},{2,26},{3,27},{4,28},{5,29},{6,30},{7,31},{8,0},{9,1... | collective-permute-start | bytes 196616 | tf_op jit(solution)/shard_map/ppermute | solution.py:48
  7.1 1.4 %copy.13.expanding_ref = bf16[128,64]{1,0:T(8,128)(2,1)} copy(bf16[128,64]{0,1:T(8,128)(2,1)} %param.17) | data formatting | bytes 32768 | tf_op args[7]
  8.5 2.1 %shard_map.100 = (bf16[384,512]{1,0:T(8,128)(2,1)}, f32[8,128]{1,0:T(8,128)}) custom-call(s32[1,512]{1,0:T(1,128)} %broadcast_in_dim_reshape.4.order_ref, bf16[128,128]{1,0:T(8,128)(2,1)} %contracting_ref.1, bf16[128,64]{1,0:T(8,128)(2,1)} %copy.13.expanding_ref, bf16[128,2048]{1,0:T(8,128)(2,1)} %queries_ref.3), custom_call_target="tpu_custom_call" | custom-call | flops 100000000 | bytes 1000000 | tf_op jit(solution)/shard_map/pallas_call | solution.py:222
  10.7 1.7 %collective-permute-start.3 = (bf16[64,2048]{1,0:T(8,128)(2,1)S(1)}, bf16[64,2048]{1,0:T(8,128)(2,1)S(1)}, u32[]{:S(2)}, u32[]{:S(2)}) collective-permute-start(bf16[64,2048]{1,0:T(8,128)(2,1)S(1)} %pad_maximum_fusion.refs_0_), channel_id=1, source_target_pairs={{0,32},{1,33},{2,34},{3,35},{4,36},{5,37},{6,38},{7,39},{8,40},{9,... | collective-permute-start | bytes 786440 | tf_op jit(solution)/shard_map/ppermute | solution.py:48
  12.4 4.0 %collective-permute-start.7 = (bf16[64,2048]{1,0:T(8,128)(2,1)S(1)}, bf16[64,2048]{1,0:T(8,128)(2,1)S(1)}, u32[]{:S(2)}, u32[]{:S(2)}) collective-permute-start(bf16[64,2048]{1,0:T(8,128)(2,1)S(1)} %pad_maximum_fusion.refs_0_), channel_id=1, source_target_pairs={{0,224},{1,225},{2,226},{3,227},{4,228},{5,229},{6,230},{7,231},{8... | collective-permute-start | bytes 786440 | tf_op jit(solution)/shard_map/ppermute | solution.py:48
  16.4 4.7 %collective-permute-done.3.refs_1_ = bf16[64,2048]{1,0:T(8,128)(2,1)S(1)} collective-permute-done((bf16[64,2048]{1,0:T(8,128)(2,1)S(1)}, bf16[64,2048]{1,0:T(8,128)(2,1)S(1)}, u32[]{:S(2)}, u32[]{:S(2)}) %collective-permute-start.3) | collective-permute-done | bytes 262176 | tf_op jit(solution)/shard_map/ppermute | solution.py:48
  21.2 2.7 %collective-permute-start.8 = (bf16[64,2048]{1,0:T(8,128)(2,1)S(1)}, bf16[64,2048]{1,0:T(8,128)(2,1)S(1)}, u32[]{:S(2)}, u32[]{:S(2)}) collective-permute-start(bf16[64,2048]{1,0:T(8,128)(2,1)S(1)} %collective-permute-done.7.refs_7_), channel_id=1, source_target_pairs={{0,224},{1,225},{2,226},{3,227},{4,228},{5,229},{6,230},{7,231},{8... | collective-permute-start | bytes 786440 | tf_op jit(solution)/shard_map/ppermute | solution.py:48
  23.8 3.8 %collective-permute-done.4.refs_2_ = bf16[64,2048]{1,0:T(8,128)(2,1)S(1)} collective-permute-done((bf16[64,2048]{1,0:T(8,128)(2,1)S(1)}, bf16[64,2048]{1,0:T(8,128)(2,1)S(1)}, u32[]{:S(2)}, u32[]{:S(2)}) %collective-permute-start.4) | collective-permute-done | bytes 262176 | tf_op jit(solution)/shard_map/ppermute | solution.py:48
  27.6 2.7 %collective-permute-start.9 = (bf16[64,2048]{1,0:T(8,128)(2,1)S(1)}, bf16[64,2048]{1,0:T(8,128)(2,1)S(1)}, u32[]{:S(2)}, u32[]{:S(2)}) collective-permute-start(bf16[64,2048]{1,0:T(8,128)(2,1)S(1)} %collective-permute-done.8.refs_6_), channel_id=1, source_target_pairs={{0,224},{1,225},{2,226},{3,227},{4,228},{5,229},{6,230},{7,231},{8... | collective-permute-start | bytes 786440 | tf_op jit(solution)/shard_map/ppermute | solution.py:48
  30.3 3.8 %collective-permute-done.5.refs_3_ = bf16[64,2048]{1,0:T(8,128)(2,1)S(1)} collective-permute-done((bf16[64,2048]{1,0:T(8,128)(2,1)S(1)}, bf16[64,2048]{1,0:T(8,128)(2,1)S(1)}, u32[]{:S(2)}, u32[]{:S(2)}) %collective-permute-start.5) | collective-permute-done | bytes 262176 | tf_op jit(solution)/shard_map/ppermute | solution.py:48
  34.0 6.9 %collective-permute-done.6.refs_4_ = bf16[64,2048]{1,0:T(8,128)(2,1)S(1)} collective-permute-done((bf16[64,2048]{1,0:T(8,128)(2,1)S(1)}, bf16[64,2048]{1,0:T(8,128)(2,1)S(1)}, u32[]{:S(2)}, u32[]{:S(2)}) %collective-permute-start.6) | collective-permute-done | bytes 262176 | tf_op jit(solution)/shard_map/ppermute | solution.py:48
  41.7 4.8 %shard_map.101.maps_ref = bf16[384,2048]{1,0:T(8,128)(2,1)} custom-call(bf16[384,512]{1,0:T(8,128)(2,1)} %get-tuple-element.24.weights_ref, bf16[64,2048]{1,0:T(8,128)(2,1)} %copy-done.1, bf16[64,2048]{1,0:T(8,128)(2,1)} %copy-done.2, bf16[64,2048]{1,0:T(8,128)(2,1)} %copy-done.4, bf16[64,2048]{1,0:T(8,128)(2,1)} %copy-done.6, bf16[64,2048]{1,0:T(8,128)(2,1)} %copy-done.8, ...), custom_call_target="tpu_custom_call" | custom-call | flops 805306368 | bytes 4000000 | tf_op jit(solution)/shard_map/pallas_call | solution.py:237
  46.4 5.9 %collective-permute-start.10 = (bf16[384,2048]{1,0:T(8,128)(2,1)}, bf16[384,2048]{1,0:T(8,128)(2,1)S(1)}, u32[]{:S(2)}, u32[]{:S(2)}) collective-permute-start(bf16[384,2048]{1,0:T(8,128)(2,1)} %shard_map.101.maps_ref), channel_id=1, source_target_pairs={{0,1},{1,0},{2,3},{3,2},{4,5},{5,4},{6,7},{7,6},{8,9},{9,8},{10,11... | collective-permute-start | bytes 4718600 | tf_op jit(solution)/shard_map/ppermute | solution.py:48
  52.9 5.9 %shard_map.102 = (f32[512,128]{1,0:T(8,128)}, f32[512,256]{1,0:T(8,128)}) custom-call(s32[5]{0:T(128)} %pad_add_fusion.info_ref, bf16[512,4096]{1,0:T(8,128)(2,1)} %bitcast.26, bf16[512,4096]{1,0:T(8,128)(2,1)} %bitcast.24, bf16[384,2048]{1,0:T(8,128)(2,1)} %shard_map.101.maps_ref), custom_call_target="tpu_custom_call" | custom-call | flops 805306368 | bytes 6000000 | tf_op jit(solution)/shard_map/pallas_call | solution.py:250
  58.8 1.2 copy-done
  60.0 5.2 %shard_map.104 = (f32[256,256]{1,0:T(8,128)}, f32[256,256]{1,0:T(8,128)}) custom-call(s32[5]{0:T(128)} %pad_add_fusion.info_ref, bf16[512,4096]{1,0:T(8,128)(2,1)} %bitcast.25, bf16[384,2048]{1,0:T(8,128)(2,1)} %copy-done, f32[512,256]{1,0:T(8,128)} %get-tuple-element.29.part_ref), custom_call_target="tpu_custom_call" | custom-call | flops 536870912 | bytes 4000000 | tf_op jit(solution)/shard_map/pallas_call | solution.py:270
  65.2 2.9 %collective-permute-start.12 = (f32[256,256]{1,0:T(8,128)}, f32[256,256]{1,0:T(8,128)S(1)}, u32[]{:S(2)}, u32[]{:S(2)}) collective-permute-start(f32[256,256]{1,0:T(8,128)} %get-tuple-element.31), channel_id=1, source_target_pairs={{0,4},{1,5},{2,6},{3,7},{4,0},{5,1},{6,2},{7,3},{8,12},{9,13},{10,... | collective-permute-start | bytes 786440 | tf_op jit(solution)/shard_map/ppermute | solution.py:48
  68.1 4.7 %shard_map.103 = (f32[256,128]{1,0:T(8,128)}, f32[256,128]{1,0:T(8,128)}) custom-call(s32[5]{0:T(128)} %pad_add_fusion.info_ref, bf16[512,4096]{1,0:T(8,128)(2,1)} %bitcast.27, bf16[384,2048]{1,0:T(8,128)(2,1)} %copy-done, f32[512,128]{1,0:T(8,128)} %get-tuple-element.26.part_ref), custom_call_target="tpu_custom_call" | custom-call | flops 268435456 | bytes 4000000 | tf_op jit(solution)/shard_map/pallas_call | solution.py:270
  72.8 6.4 %collective-permute-done.11.got_left = f32[256,128]{1,0:T(8,128)S(1)} collective-permute-done((f32[256,128]{1,0:T(8,128)}, f32[256,128]{1,0:T(8,128)S(1)}, u32[]{:S(2)}, u32[]{:S(2)}) %collective-permute-start.11) | collective-permute-done | bytes 131104 | tf_op jit(solution)/shard_map/ppermute | solution.py:48
  80.0 2.1 %shard_map.105 = (f32[2,16,128]{2,1,0:T(8,128)}, f32[2,16,128]{2,1,0:T(8,128)}, f32[2,16,128]{2,1,0:T(8,128)}, f32[2,16,128]{2,1,0:T(8,128)}) custom-call(s32[5]{0:T(128)} %pad_add_fusion.info_ref, f32[256,128]{1,0:T(8,128)} %get-tuple-element.27.keep_left, f32[256,128]{1,0:T(8,128)} %copy-done.10, f32[256,256]{1,0:T(8,128)} %get-tuple-element.30.keep_right, ...), custom_call_target="tpu_custom_call" | custom-call | flops 20000000 | bytes 1000000 | tf_op jit(solution)/shard_map/pallas_call | solution.py:295
  82.1 1.1 collective-permute-start.13
  83.6 1.5 %collective-permute-start.15 = (f32[2,16,128]{2,1,0:T(8,128)}, f32[2,16,128]{2,1,0:T(8,128)S(1)}, u32[]{:S(2)}, u32[]{:S(2)}) collective-permute-start(f32[2,16,128]{2,1,0:T(8,128)} %get-tuple-element.35), channel_id=1, source_target_pairs={{0,3},{1,2},{2,1},{3,0},{4,7},{5,6},{6,5},{7,4},{8,11},{9,10},{10,... | collective-permute-start | bytes 49160 | tf_op jit(solution)/shard_map/ppermute | solution.py:48
  85.1 0.9 collective-permute-done.14
  86.0 1.3 %collective-permute-done.15 = f32[2,16,128]{2,1,0:T(8,128)S(1)} collective-permute-done((f32[2,16,128]{2,1,0:T(8,128)}, f32[2,16,128]{2,1,0:T(8,128)S(1)}, u32[]{:S(2)}, u32[]{:S(2)}) %collective-permute-start.15) | collective-permute-done | bytes 16416 | tf_op jit(solution)/shard_map/ppermute | solution.py:48
  88.2 18.8 %all_to_all.5 = bf16[32,2,2048]{2,1,0:T(2,128)(2,1)S(1)} all-to-all(bf16[32,2,2048]{2,1,0:T(2,128)(2,1)S(1)} %broadcast_in_dim.18), channel_id=1, replica_groups=mesh['demo'=32,'fsdp'=2,'sketch'=4] {'demo'}, dimensions={0} | all-to-all | bytes 524288 | tf_op jit(solution)/shard_map/all_to_all | solution.py:307
  107.7 2.1 %shard_map.106 = (f32[2,24,256]{2,1,0:T(8,128)}, f32[2,24,256]{2,1,0:T(8,128)}) custom-call(s32[5]{0:T(128)} %pad_add_fusion.info_ref, bf16[64,2048]{1,0:T(8,128)(2,1)} %reshape.56.demos_ref, bf16[128,2048]{1,0:T(8,128)(2,1)} %queries_ref.3, f32[8,128]{1,0:T(8,128)} %get-tuple-element.36.squares_ref), custom_call_target="tpu_custom_call" | custom-call | flops 40000000 | bytes 1000000 | tf_op jit(solution)/shard_map/pallas_call | solution.py:309
  109.8 2.3 %collective-permute-start.16 = (f32[2,24,256]{2,1,0:T(8,128)}, f32[2,24,256]{2,1,0:T(8,128)S(1)}, u32[]{:S(2)}, u32[]{:S(2)}) collective-permute-start(f32[2,24,256]{2,1,0:T(8,128)} %get-tuple-element.38), channel_id=1, source_target_pairs={{0,1},{1,0},{2,3},{3,2},{4,5},{5,4},{6,7},{7,6},{8,9},{9,8},{10,11... | collective-permute-start | bytes 147464 | tf_op jit(solution)/shard_map/ppermute | solution.py:48
  112.1 1.1 collective-permute-done.16
  114.0 1.0 collective-permute-start.17
  115.9 1.5 %collective-permute-start.18 = (f32[24,256]{1,0:T(8,128)S(1)}, f32[24,256]{1,0:T(8,128)S(1)}, u32[]{:S(2)}, u32[]{:S(2)}) collective-permute-start(f32[24,256]{1,0:T(8,128)S(1)} %get-tuple-element.41), channel_id=1, source_target_pairs={{0,4},{1,5},{2,6},{3,7},{4,0},{5,1},{6,2},{7,3},{8,12},{9,13},{10,... | collective-permute-start | bytes 73736 | tf_op jit(solution)/shard_map/ppermute | solution.py:48
  117.4 2.6 %collective-permute-done.18 = f32[24,256]{1,0:T(8,128)S(1)} collective-permute-done((f32[24,256]{1,0:T(8,128)S(1)}, f32[24,256]{1,0:T(8,128)S(1)}, u32[]{:S(2)}, u32[]{:S(2)}) %collective-permute-start.18) | collective-permute-done | bytes 24608 | tf_op jit(solution)/shard_map/ppermute | solution.py:48
  (68 shorter events, 8.7 us)
Async XLA Ops:
  0.0 52.3 %copy-start.11 = (s32[4]{0:T(128)S(1)}, s32[4]{0:T(128)}, u32[]{:S(2)}) copy-start(s32[4]{0:T(128)} %param.12) | copy-start | bytes 52
  1.7 9.0 %collective-permute-start.2 = (bf16[16,2048]{1,0:T(8,128)(2,1)S(1)}, bf16[16,2048]{1,0:T(8,128)(2,1)S(1)}, u32[]{:S(2)}, u32[]{:S(2)}) collective-permute-start(bf16[16,2048]{1,0:T(8,128)(2,1)S(1)} %constant_dynamic-slice_fusion), channel_id=1, source_target_pairs={{0,24},{1,25},{2,26},{3,27},{4,28},{5,29},{6,30},{7,31},{8,0},{9,1... | collective-permute-start | bytes 196616 | tf_op jit(solution)/shard_map/ppermute | solution.py:48
  5.1 5.6 %collective-permute-start.1 = (bf16[16,2048]{1,0:T(8,128)(2,1)S(1)}, bf16[16,2048]{1,0:T(8,128)(2,1)S(1)}, u32[]{:S(2)}, u32[]{:S(2)}) collective-permute-start(bf16[16,2048]{1,0:T(8,128)(2,1)S(1)} %constant_dynamic-slice_fusion), channel_id=1, source_target_pairs={{0,16},{1,17},{2,18},{3,19},{4,20},{5,21},{6,22},{7,23},{8,24},{9,... | collective-permute-start | bytes 196616 | tf_op jit(solution)/shard_map/ppermute | solution.py:48
  5.6 5.1 %collective-permute-start = (bf16[16,2048]{1,0:T(8,128)(2,1)S(1)}, bf16[16,2048]{1,0:T(8,128)(2,1)S(1)}, u32[]{:S(2)}, u32[]{:S(2)}) collective-permute-start(bf16[16,2048]{1,0:T(8,128)(2,1)S(1)} %constant_dynamic-slice_fusion), channel_id=1, source_target_pairs={{0,8},{1,9},{2,10},{3,11},{4,12},{5,13},{6,14},{7,15},{8,16},{9,17... | collective-permute-start | bytes 196616 | tf_op jit(solution)/shard_map/ppermute | solution.py:48
  10.7 30.2 %copy-start.1 = (bf16[64,2048]{1,0:T(8,128)(2,1)}, bf16[64,2048]{1,0:T(8,128)(2,1)S(1)}, u32[]{:S(2)}) copy-start(bf16[64,2048]{1,0:T(8,128)(2,1)S(1)} %pad_maximum_fusion.refs_0_) | copy-start | bytes 786436
  10.7 10.4 %collective-permute-start.3 = (bf16[64,2048]{1,0:T(8,128)(2,1)S(1)}, bf16[64,2048]{1,0:T(8,128)(2,1)S(1)}, u32[]{:S(2)}, u32[]{:S(2)}) collective-permute-start(bf16[64,2048]{1,0:T(8,128)(2,1)S(1)} %pad_maximum_fusion.refs_0_), channel_id=1, source_target_pairs={{0,32},{1,33},{2,34},{3,35},{4,36},{5,37},{6,38},{7,39},{8,40},{9,... | collective-permute-start | bytes 786440 | tf_op jit(solution)/shard_map/ppermute | solution.py:48
  12.4 8.7 %collective-permute-start.7 = (bf16[64,2048]{1,0:T(8,128)(2,1)S(1)}, bf16[64,2048]{1,0:T(8,128)(2,1)S(1)}, u32[]{:S(2)}, u32[]{:S(2)}) collective-permute-start(bf16[64,2048]{1,0:T(8,128)(2,1)S(1)} %pad_maximum_fusion.refs_0_), channel_id=1, source_target_pairs={{0,224},{1,225},{2,226},{3,227},{4,228},{5,229},{6,230},{7,231},{8... | collective-permute-start | bytes 786440 | tf_op jit(solution)/shard_map/ppermute | solution.py:48
  21.1 19.8 %copy-start.2 = (bf16[64,2048]{1,0:T(8,128)(2,1)}, bf16[64,2048]{1,0:T(8,128)(2,1)S(1)}, u32[]{:S(2)}) copy-start(bf16[64,2048]{1,0:T(8,128)(2,1)S(1)} %collective-permute-done.3.refs_1_) | copy-start | bytes 786436
  21.1 6.4 %collective-permute-start.4 = (bf16[64,2048]{1,0:T(8,128)(2,1)S(1)}, bf16[64,2048]{1,0:T(8,128)(2,1)S(1)}, u32[]{:S(2)}, u32[]{:S(2)}) collective-permute-start(bf16[64,2048]{1,0:T(8,128)(2,1)S(1)} %collective-permute-done.3.refs_1_), channel_id=1, source_target_pairs={{0,32},{1,33},{2,34},{3,35},{4,36},{5,37},{6,38},{7,39},{8,40},{9,... | collective-permute-start | bytes 786440 | tf_op jit(solution)/shard_map/ppermute | solution.py:48
  21.2 19.8 %copy-start.3 = (bf16[64,2048]{1,0:T(8,128)(2,1)}, bf16[64,2048]{1,0:T(8,128)(2,1)S(1)}, u32[]{:S(2)}) copy-start(bf16[64,2048]{1,0:T(8,128)(2,1)S(1)} %collective-permute-done.7.refs_7_) | copy-start | bytes 786436
  21.2 6.4 %collective-permute-start.8 = (bf16[64,2048]{1,0:T(8,128)(2,1)S(1)}, bf16[64,2048]{1,0:T(8,128)(2,1)S(1)}, u32[]{:S(2)}, u32[]{:S(2)}) collective-permute-start(bf16[64,2048]{1,0:T(8,128)(2,1)S(1)} %collective-permute-done.7.refs_7_), channel_id=1, source_target_pairs={{0,224},{1,225},{2,226},{3,227},{4,228},{5,229},{6,230},{7,231},{8... | collective-permute-start | bytes 786440 | tf_op jit(solution)/shard_map/ppermute | solution.py:48
  27.6 13.3 %copy-start.4 = (bf16[64,2048]{1,0:T(8,128)(2,1)}, bf16[64,2048]{1,0:T(8,128)(2,1)S(1)}, u32[]{:S(2)}) copy-start(bf16[64,2048]{1,0:T(8,128)(2,1)S(1)} %collective-permute-done.4.refs_2_) | copy-start | bytes 786436
  27.6 6.4 %collective-permute-start.5 = (bf16[64,2048]{1,0:T(8,128)(2,1)S(1)}, bf16[64,2048]{1,0:T(8,128)(2,1)S(1)}, u32[]{:S(2)}, u32[]{:S(2)}) collective-permute-start(bf16[64,2048]{1,0:T(8,128)(2,1)S(1)} %collective-permute-done.4.refs_2_), channel_id=1, source_target_pairs={{0,32},{1,33},{2,34},{3,35},{4,36},{5,37},{6,38},{7,39},{8,40},{9,... | collective-permute-start | bytes 786440 | tf_op jit(solution)/shard_map/ppermute | solution.py:48
  27.6 13.3 %copy-start.5 = (bf16[64,2048]{1,0:T(8,128)(2,1)}, bf16[64,2048]{1,0:T(8,128)(2,1)S(1)}, u32[]{:S(2)}) copy-start(bf16[64,2048]{1,0:T(8,128)(2,1)S(1)} %collective-permute-done.8.refs_6_) | copy-start | bytes 786436
  27.6 6.4 %collective-permute-start.9 = (bf16[64,2048]{1,0:T(8,128)(2,1)S(1)}, bf16[64,2048]{1,0:T(8,128)(2,1)S(1)}, u32[]{:S(2)}, u32[]{:S(2)}) collective-permute-start(bf16[64,2048]{1,0:T(8,128)(2,1)S(1)} %collective-permute-done.8.refs_6_), channel_id=1, source_target_pairs={{0,224},{1,225},{2,226},{3,227},{4,228},{5,229},{6,230},{7,231},{8... | collective-permute-start | bytes 786440 | tf_op jit(solution)/shard_map/ppermute | solution.py:48
  34.0 6.9 %copy-start.6 = (bf16[64,2048]{1,0:T(8,128)(2,1)}, bf16[64,2048]{1,0:T(8,128)(2,1)S(1)}, u32[]{:S(2)}) copy-start(bf16[64,2048]{1,0:T(8,128)(2,1)S(1)} %collective-permute-done.5.refs_3_) | copy-start | bytes 786436
  34.0 6.9 %collective-permute-start.6 = (bf16[64,2048]{1,0:T(8,128)(2,1)S(1)}, bf16[64,2048]{1,0:T(8,128)(2,1)S(1)}, u32[]{:S(2)}, u32[]{:S(2)}) collective-permute-start(bf16[64,2048]{1,0:T(8,128)(2,1)S(1)} %collective-permute-done.5.refs_3_), channel_id=1, source_target_pairs={{0,32},{1,33},{2,34},{3,35},{4,36},{5,37},{6,38},{7,39},{8,40},{9,... | collective-permute-start | bytes 786440 | tf_op jit(solution)/shard_map/ppermute | solution.py:48
  34.0 6.9 %copy-start.7 = (bf16[64,2048]{1,0:T(8,128)(2,1)}, bf16[64,2048]{1,0:T(8,128)(2,1)S(1)}, u32[]{:S(2)}) copy-start(bf16[64,2048]{1,0:T(8,128)(2,1)S(1)} %collective-permute-done.9.refs_5_) | copy-start | bytes 786436
  41.0 0.7 copy-start.8
  46.4 12.4 %collective-permute-start.10 = (bf16[384,2048]{1,0:T(8,128)(2,1)}, bf16[384,2048]{1,0:T(8,128)(2,1)S(1)}, u32[]{:S(2)}, u32[]{:S(2)}) collective-permute-start(bf16[384,2048]{1,0:T(8,128)(2,1)} %shard_map.101.maps_ref), channel_id=1, source_target_pairs={{0,1},{1,0},{2,3},{3,2},{4,5},{5,4},{6,7},{7,6},{8,9},{9,8},{10,11... | collective-permute-start | bytes 4718600 | tf_op jit(solution)/shard_map/ppermute | solution.py:48
  58.8 1.2 copy-start
  65.2 14.1 %collective-permute-start.12 = (f32[256,256]{1,0:T(8,128)}, f32[256,256]{1,0:T(8,128)S(1)}, u32[]{:S(2)}, u32[]{:S(2)}) collective-permute-start(f32[256,256]{1,0:T(8,128)} %get-tuple-element.31), channel_id=1, source_target_pairs={{0,4},{1,5},{2,6},{3,7},{4,0},{5,1},{6,2},{7,3},{8,12},{9,13},{10,... | collective-permute-start | bytes 786440 | tf_op jit(solution)/shard_map/ppermute | solution.py:48
  72.7 6.5 %collective-permute-start.11 = (f32[256,128]{1,0:T(8,128)}, f32[256,128]{1,0:T(8,128)S(1)}, u32[]{:S(2)}, u32[]{:S(2)}) collective-permute-start(f32[256,128]{1,0:T(8,128)} %get-tuple-element.28), channel_id=1, source_target_pairs={{0,4},{1,5},{2,6},{3,7},{4,0},{5,1},{6,2},{7,3},{8,12},{9,13},{10,... | collective-permute-start | bytes 393224 | tf_op jit(solution)/shard_map/ppermute | solution.py:48
  79.2 0.6 copy-start.10
  79.2 0.7 copy-start.9
  82.1 3.0 %collective-permute-start.13 = (f32[2,16,128]{2,1,0:T(8,128)}, f32[2,16,128]{2,1,0:T(8,128)S(1)}, u32[]{:S(2)}, u32[]{:S(2)}) collective-permute-start(f32[2,16,128]{2,1,0:T(8,128)} %get-tuple-element.33), channel_id=1, source_target_pairs={{0,1},{1,0},{2,3},{3,2},{4,5},{5,4},{6,7},{7,6},{8,9},{9,8},{10,11... | collective-permute-start | bytes 49160 | tf_op jit(solution)/shard_map/ppermute | solution.py:48
  83.2 2.8 %collective-permute-start.14 = (f32[2,16,128]{2,1,0:T(8,128)}, f32[2,16,128]{2,1,0:T(8,128)S(1)}, u32[]{:S(2)}, u32[]{:S(2)}) collective-permute-start(f32[2,16,128]{2,1,0:T(8,128)} %get-tuple-element.34), channel_id=1, source_target_pairs={{0,2},{1,3},{2,0},{3,1},{4,6},{5,7},{6,4},{7,5},{8,10},{9,11},{10,... | collective-permute-start | bytes 49160 | tf_op jit(solution)/shard_map/ppermute | solution.py:48
  83.6 3.7 %collective-permute-start.15 = (f32[2,16,128]{2,1,0:T(8,128)}, f32[2,16,128]{2,1,0:T(8,128)S(1)}, u32[]{:S(2)}, u32[]{:S(2)}) collective-permute-start(f32[2,16,128]{2,1,0:T(8,128)} %get-tuple-element.35), channel_id=1, source_target_pairs={{0,3},{1,2},{2,1},{3,0},{4,7},{5,6},{6,5},{7,4},{8,11},{9,10},{10,... | collective-permute-start | bytes 49160 | tf_op jit(solution)/shard_map/ppermute | solution.py:48
  109.8 3.4 %collective-permute-start.16 = (f32[2,24,256]{2,1,0:T(8,128)}, f32[2,24,256]{2,1,0:T(8,128)S(1)}, u32[]{:S(2)}, u32[]{:S(2)}) collective-permute-start(f32[2,24,256]{2,1,0:T(8,128)} %get-tuple-element.38), channel_id=1, source_target_pairs={{0,1},{1,0},{2,3},{3,2},{4,5},{5,4},{6,7},{7,6},{8,9},{9,8},{10,11... | collective-permute-start | bytes 147464 | tf_op jit(solution)/shard_map/ppermute | solution.py:48
  114.0 3.3 %collective-permute-start.17 = (f32[24,256]{1,0:T(8,128)S(1)}, f32[24,256]{1,0:T(8,128)S(1)}, u32[]{:S(2)}, u32[]{:S(2)}) collective-permute-start(f32[24,256]{1,0:T(8,128)S(1)} %get-tuple-element.42), channel_id=1, source_target_pairs={{0,2},{1,3},{2,0},{3,1},{4,6},{5,7},{6,4},{7,5},{8,10},{9,11},{10,... | collective-permute-start | bytes 73736 | tf_op jit(solution)/shard_map/ppermute | solution.py:48
  115.1 5.0 %collective-permute-start.19 = (f32[24,256]{1,0:T(8,128)S(1)}, f32[24,256]{1,0:T(8,128)S(1)}, u32[]{:S(2)}, u32[]{:S(2)}) collective-permute-start(f32[24,256]{1,0:T(8,128)S(1)} %get-tuple-element.42), channel_id=1, source_target_pairs={{0,6},{1,7},{2,4},{3,5},{4,2},{5,3},{6,0},{7,1},{8,14},{9,15},{10,... | collective-permute-start | bytes 73736 | tf_op jit(solution)/shard_map/ppermute | solution.py:48
  115.9 4.2 %collective-permute-start.18 = (f32[24,256]{1,0:T(8,128)S(1)}, f32[24,256]{1,0:T(8,128)S(1)}, u32[]{:S(2)}, u32[]{:S(2)}) collective-permute-start(f32[24,256]{1,0:T(8,128)S(1)} %get-tuple-element.41), channel_id=1, source_target_pairs={{0,4},{1,5},{2,6},{3,7},{4,0},{5,1},{6,2},{7,3},{8,12},{9,13},{10,... | collective-permute-start | bytes 73736 | tf_op jit(solution)/shard_map/ppermute | solution.py:48

commit v3 on v1

v3 whole, which is shorter than its diff:
```python
import math

import jax
import jax.numpy as jnp
from jax import lax
from jax.experimental import pallas as pl
from jax.experimental.pallas import tpu as pltpu
from jax.sharding import PartitionSpec as P

PROBE_ROWS = 64
PROBE_COLUMNS = 128
K = 8192
AXES = ("demo", "fsdp", "sketch")
Z, X, F, S = 8, 4, 2, 4
ROWS = 16
LEFT = 2 * PROBE_ROWS
RIGHT = 2 * PROBE_COLUMNS
LAST = ((1,), (1,))


def pairs(step):
    out = []
    for z in range(Z):
        for x in range(X):
            for f in range(F):
                for s in range(S):
                    z2, x2, f2, s2 = step(z, x, f, s)
                    source = ((z * X + x) * F + f) * S + s
                    target = (((z2 % Z) * X + x2 % X) * F + f2) * S + s2
                    out.append((source, target))
    return out


CORE = pairs(lambda z, x, f, s: (z, x, f, s ^ 1))
NEAR = pairs(lambda z, x, f, s: (z, x, f, s ^ 2))
CORE_NEAR = pairs(lambda z, x, f, s: (z, x, f, s ^ 3))
FAR = pairs(lambda z, x, f, s: (z, x, f ^ 1, s))
FAR_NEAR = pairs(lambda z, x, f, s: (z, x, f ^ 1, s ^ 2))


def shift(dz, dx):
    return pairs(lambda z, x, f, s: (z + dz, x + dx, f, s))


def send(value, moves):
    return lax.ppermute(value, AXES, moves)


def dot(a, b, contract):
    return lax.dot_general(a, b, (contract, ((), ())), preferred_element_type=jnp.float32)


def cost(flops, moved):
    return pl.CostEstimate(flops=flops, bytes_accessed=moved, transcendentals=0)


def shape(dims, kind=jnp.float32):
    return jax.ShapeDtypeStruct(dims, kind)


def weights_kernel(info_ref, contracting_ref, expanding_ref, queries_ref, weights_ref, squares_ref):
    columns = Z * X * ROWS
    column = lax.broadcasted_iota(jnp.int32, (1, columns), 1)
    kind = column % ROWS
    z_from = (info_ref[0] + Z - column // (X * ROWS)) % Z
    x_from = (info_ref[1] + X - (column // ROWS) % X) % X
    place = z_from * X + x_from

    def chosen(count, width, start):
        inside = (kind >= start) & (kind < start + width)
        target = jnp.where(inside, place * width + kind - start, -1)
        hit = lax.broadcasted_iota(jnp.int32, (count, columns), 0) == target
        return jnp.where(hit, 1.0, 0.0).astype(jnp.bfloat16)

    weights_ref[0:PROBE_ROWS] = chosen(PROBE_ROWS, 2, 12)
    weights_ref[PROBE_ROWS:LEFT] = dot(expanding_ref[...], chosen(128, 4, 0), ((1,), (0,))).astype(
        jnp.bfloat16
    )
    weights_ref[LEFT : LEFT + PROBE_COLUMNS] = dot(
        contracting_ref[...], chosen(128, 4, 4), ((0,), (0,))
    ).astype(jnp.bfloat16)
    weights_ref[LEFT + PROBE_COLUMNS :] = chosen(PROBE_COLUMNS, 4, 8)
    values = queries_ref[...].astype(jnp.float32)
    squares = jnp.sum(values * values, axis=1, keepdims=True)
    squares_ref[...] = jnp.broadcast_to(squares, (128, 128)).T[0:8]


def pick(value, index):
    return lax.dynamic_index_in_dim(value, index, 0, keepdims=False)


def shards(
    activations,
    cotangents,
    lengths,
    lowrank_contract_matrix,
    lowrank_expand_matrix,
    input_feature_sketch,
    latent_random_map_contracting,
    latent_random_map_expanding,
    output_feature_sketch,
    queries,
):
    demo_count, tok_local, feat = activations.shape
    own = demo_count // F
    tokens = demo_count * tok_local
    half = feat // 2
    nq = queries.shape[0]
    demo = lax.axis_index("demo")
    z, x = demo // X, demo % X
    f = lax.axis_index("fsdp")
    s = lax.axis_index("sketch")
    core = s % 2

    block = jnp.concatenate(
        [
            lowrank_contract_matrix.T,
            lowrank_expand_matrix.T,
            output_feature_sketch.T,
            input_feature_sketch.T,
            jnp.zeros((2, feat), jnp.bfloat16),
        ],
        axis=0,
    )
    block = lax.dynamic_slice_in_dim(block, core * half, half, axis=1)
    weights, query_squares = pl.pallas_call(
        weights_kernel,
        out_shape=[shape((LEFT + RIGHT, Z * X * ROWS), jnp.bfloat16), shape((8, 128))],
        in_specs=[pl.BlockSpec(memory_space=pltpu.SMEM)]
        + [pl.BlockSpec(memory_space=pltpu.VMEM)] * 3,
        out_specs=[pl.BlockSpec(memory_space=pltpu.VMEM)] * 2,
        cost_estimate=cost(10**8, 10**6),
    )(
        jnp.stack([z, x]).astype(jnp.int32),
        latent_random_map_contracting,
        latent_random_map_expanding.T,
        queries,
    )
    act = activations.reshape(tokens, feat)
    cot = cotangents.reshape(tokens, feat)

    def side(which):
        return jnp.stack(
            [lax.dynamic_slice_in_dim(v, which * half, half, axis=1) for v in (act, cot)]
        )

    line = jnp.concatenate([block] + [send(block, shift(0, k)) for k in range(1, X)])
    got = [line] + [None] * (Z - 1)
    up = down = line
    for k in range(1, Z // 2 + 1):
        up = send(up, shift(1, 0))
        got[k] = up
        if k < Z // 2:
            down = send(down, shift(-1, 0))
            got[Z - k] = down
        if k == 1:
            give = side(1 - core)
            give, up, down = lax.optimization_barrier((give, up, down))
            theirs = send(give, CORE)
        if k == 2:
            mine = side(core)
            mine, weights, query_squares, up, down = lax.optimization_barrier(
                (mine, weights, query_squares, up, down)
            )
        if k == 3:
            theirs, up, down = lax.optimization_barrier((theirs, up, down))
    rows = jnp.concatenate(got)
    maps = jnp.dot(weights, rows, preferred_element_type=jnp.float32).astype(jnp.bfloat16)
    left_map, right_map = maps[:LEFT], maps[LEFT:]

    right_away = send(dot(theirs[1], right_map, LAST), CORE)
    right = dot(mine[1], right_map, LAST) + right_away
    right = right.reshape(F, own, tok_local, RIGHT)
    right_sum = pick(right, f) + send(pick(right, 1 - f), FAR)
    left_away = send(dot(theirs[0], left_map, LAST), CORE)
    left = dot(mine[0], left_map, LAST) + left_away
    left = left.reshape(F, own, tok_local, LEFT)
    left_sum = pick(left, f) + send(pick(left, 1 - f), FAR)

    positions = s * tok_local + jnp.arange(tok_local, dtype=jnp.int32)
    own_lengths = pick(lengths.reshape(F, own), f)
    padding = (positions[None, :] < own_lengths[:, None]).astype(jnp.float32)
    right_sum = right_sum * padding[:, :, None]
    left_rows = left_sum.astype(jnp.bfloat16).reshape(own, tok_local, 2, PROBE_ROWS)
    right_rows = right_sum.astype(jnp.bfloat16).reshape(own, tok_local, 2, PROBE_COLUMNS)
    partial_value = jnp.einsum(
        "ntpa,ntpb->nab", left_rows, right_rows, preferred_element_type=jnp.float32
    )
    parts = partial_value.reshape(own, S, PROBE_ROWS // S, PROBE_COLUMNS)

    def part(k):
        return lax.dynamic_index_in_dim(parts, s ^ k, 1, keepdims=False)

    summed = (part(0) + send(part(1), CORE)) + (send(part(2), NEAR) + send(part(3), CORE_NEAR))
    demo_sketch = summed.astype(jnp.bfloat16).reshape(own, K // S)

    copies = jnp.broadcast_to(demo_sketch[None], (Z * X, own, K // S))
    every_demo = lax.all_to_all(copies, "demo", 0, 0).reshape(Z * X * own, K // S)
    inner = dot(every_demo, queries, LAST)
    every_f = every_demo.astype(jnp.float32)
    demo_squares = jnp.sum(every_f * every_f, axis=1, keepdims=True)
    both = jnp.concatenate([inner, jnp.broadcast_to(demo_squares, inner.shape)], axis=1)
    block_rows = Z * X * own // S
    both = both.reshape(S, block_rows, 2 * nq)
    extra = jnp.concatenate([query_squares, query_squares], axis=1)
    both = jnp.concatenate([both, jnp.broadcast_to(extra[None], (S, 8, 2 * nq))], axis=1)
    keep = jnp.stack([pick(both, s), pick(both, s ^ 2)])
    give = jnp.stack([pick(both, s ^ 1), pick(both, s ^ 3)])
    pair = keep + send(give, CORE)
    here = pair[0] + send(pair[1], NEAR)
    there = send(pair[0], FAR) + send(pair[1], FAR_NEAR)
    query_total = here[block_rows : block_rows + 1, :nq]
    here, there = here[:block_rows], there[:block_rows]
    total = jnp.stack([jnp.where(f == 0, here, there), jnp.where(f == 0, there, here)])
    total = total.reshape(F, block_rows // own, own, 2 * nq).transpose(1, 0, 2, 3)
    total = total.reshape(F * block_rows, 2 * nq)
    demo_norm = jnp.sqrt(total[:, nq:] + 1e-06)
    query_norm = jnp.sqrt(query_total + 1e-06)
    return math.sqrt(K) * total[:, :nq] / (demo_norm * query_norm)


def solution(mesh):
    placed = (
        P("demo", "sketch", "fsdp"),
        P("demo", "sketch", "fsdp"),
        P("demo"),
        P("fsdp", "demo"),
        P("fsdp", "demo"),
        P("fsdp", "demo"),
        P(),
        P(),
        P("fsdp", "demo"),
        P("demo", "sketch"),
    )
    return jax.shard_map(
        shards, mesh=mesh, in_specs=placed, out_specs=P("sketch", "demo"), check_vma=False
    )
```

time: 123 us -> 114 us (0.927)
  starting transfers between devices: 54 us -> 42.1 us
  waiting for transfers between devices: 40.5 us -> 45.5 us
  Pallas kernels: 0 us -> 2.14 us
  local copies, waits for them, and re-layouts: 12.1 us -> 10.2 us
  matrix products: 9.27 us -> 7.68 us
    ppermute x31 -> x22, starting transfers between devices: 54 us -> 35.3 us  [send(): return lax.ppermute(value, AXES, moves)]
    all_to_all x0 -> x1, waiting for transfers between devices: none -> 11.5 us  [shards(): lax.all_to_all(copies, 'demo', 0, 0).reshape(Z * X * own, K // S)]
    all_to_all x0 -> x1, starting transfers between devices: none -> 6.84 us  [shards(): lax.all_to_all(copies, 'demo', 0, 0).reshape(Z * X * own, K // S)]
    ppermute x31 -> x22, waiting for transfers between devices: 40.5 us -> 34 us  [send(): return lax.ppermute(value, AXES, moves)]
    another operation x5 -> x1, local copies, waits for them, and re-layouts: 0.78 us -> 5.87 us  [side(): jnp.stack([lax.dynamic_slice_in_dim(v, which * half, half, axis=1) for v...]
    scatter x3 -> x0, local copies, waits for them, and re-layouts: 2.62 us -> none  [the longest x1 2.48 us: map_weights(): weights.at[:PROBE_ROWS, :, 12:14]]
    gather x7 -> x0, local copies, waits for them, and re-layouts: 2.53 us -> none  [the longest x3 1.3 us: map_weights(): weights = jnp.take(jnp.take(weights, z_order, axis=1), x_order, axis=2)]
    pallas_call x0 -> x1, Pallas kernels: none -> 2.14 us  [shards(): pl.pallas_call(weights_kernel, out_shape=[shape((LEFT + RIGHT, Z * X * RO...]
  transfers between devices with their start and end apart: 31 -> 23, of which waited for: 16 -> 12; matrix products, arithmetic and copies ran while one was open for 14% -> 14% of each run, Pallas kernels for 0% -> 2%
where the time goes in v3:
time: 114 us
  waiting for transfers between devices  45.5 us (40%)
  starting transfers between devices  42.1 us (37%)
  local copies, waits for them, and re-layouts  10.2 us (9%)
  matrix products  7.68 us (7%)
  other arithmetic  6.08 us (5%)
  Pallas kernels  2.14 us (2%)
    ppermute x22, starting transfers between devices, send(): return lax.ppermute(value, AXES, moves)  35.3 us
    ppermute x22, waiting for transfers between devices, send(): return lax.ppermute(value, AXES, moves)  34 us
    all_to_all x1, waiting for transfers between devices, shards(): lax.all_to_all(copies, 'demo', 0, 0).reshape(Z * X * own, K // S)  11.5 us
    all_to_all x1, starting transfers between devices, shards(): lax.all_to_all(copies, 'demo', 0, 0).reshape(Z * X * own, K // S)  6.84 us
    dot_general x5, matrix products, dot(): lax.dot_general(a, b, (contract, ((), ())), preferred_element_type=jnp.fl...  6.51 us
    another operation x1, local copies, waits for them, and re-layouts, side(): jnp.stack([lax.dynamic_slice_in_dim(v, which * half, half, axis=1) for v...  5.87 us
    another operation x2, other arithmetic, side(): jnp.stack([lax.dynamic_slice_in_dim(v, which * half, half, axis=1) for v...  4.51 us
  transfers between devices with their start and end apart: 23, of which 12 were waited for; matrix products, arithmetic and copies ran while one was open for 14% of the time, Pallas kernels for 2%

profile of v3, /device:TPU:1, one launch (start us, length us, event | category | flops | bytes accessed | tf_op | source)
XLA Modules:
  0.0 114.1 jit_solution(16738889207986682631)
XLA Ops:
  0.0 1.6 %concatenate.20 = bf16[16,4096]{1,0:T(8,128)(2,1)S(1)} concatenate(bf16[4,4096]{1,0:T(4,128)(2,1)} %bitcast.108, bf16[4,4096]{1,0:T(4,128)(2,1)} %bitcast.109, bf16[4,4096]{1,0:T(4,128)(2,1)} %bitcast.110, bf16[2,4096]{1,0:T(2,128)(2,1)} %bitcast.111, bf16[2,4096]{1,0:T(2,128)(2,1)S(1)} %broadcast_in_dim.12), dimensions={0} | concatenate | bytes 262144 | tf_op jit(solution)/shard_map/concatenate | solution.py:115
  2.3 3.3 %collective-permute-start.2 = (bf16[16,2048]{1,0:T(8,128)(2,1)S(1)}, bf16[16,2048]{1,0:T(8,128)(2,1)S(1)}, u32[]{:S(2)}, u32[]{:S(2)}) collective-permute-start(bf16[16,2048]{1,0:T(8,128)(2,1)S(1)} %get-tuple-element.30), channel_id=1, source_target_pairs={{0,24},{1,25},{2,26},{3,27},{4,28},{5,29},{6,30},{7,31},{8,0},{9,1... | collective-permute-start | bytes 196616 | tf_op jit(solution)/shard_map/ppermute | solution.py:46
  6.8 5.9 %dynamic-slice_bitcast_fusion.2 = (bf16[1,512,2048]{2,1,0:T(8,128)(2,1)S(1)}, bf16[1,512,2048]{2,1,0:T(8,128)(2,1)S(1)}, bf16[1,512,2048]{2,1,0:T(8,128)(2,1)S(1)}, bf16[1,512,2048]{2,1,0:T(8,128)(2,1)}) fusion(bf16[512,4096]{1,0:T(8,128)(2,1)} %bitcast.94, s32[]{:T(128)S(6)} %select_n.68, s32[]{:T(128)S(6)} %select_n.71, bf16[512,4096]{1,0:T(8,128)(2,1)} %bitcast.95), kind=kLoop, calls=%fused_computation.17 | loop fusion | bytes 16777224 | tf_op jit(solution)/shard_map/stack | solution.py:143
  12.7 1.7 %collective-permute-start.3 = (bf16[64,2048]{1,0:T(8,128)(2,1)S(1)}, bf16[64,2048]{1,0:T(8,128)(2,1)S(1)}, u32[]{:S(2)}, u32[]{:S(2)}) collective-permute-start(bf16[64,2048]{1,0:T(8,128)(2,1)S(1)} %pad_maximum_fusion.2), channel_id=1, source_target_pairs={{0,32},{1,33},{2,34},{3,35},{4,36},{5,37},{6,38},{7,39},{8,40},{9,... | collective-permute-start | bytes 786440 | tf_op jit(solution)/shard_map/ppermute | solution.py:46
  14.4 4.0 %collective-permute-start.4 = (bf16[64,2048]{1,0:T(8,128)(2,1)S(1)}, bf16[64,2048]{1,0:T(8,128)(2,1)S(1)}, u32[]{:S(2)}, u32[]{:S(2)}) collective-permute-start(bf16[64,2048]{1,0:T(8,128)(2,1)S(1)} %pad_maximum_fusion.2), channel_id=1, source_target_pairs={{0,224},{1,225},{2,226},{3,227},{4,228},{5,229},{6,230},{7,231},{8... | collective-permute-start | bytes 786440 | tf_op jit(solution)/shard_map/ppermute | solution.py:46
  18.4 2.4 %pad_maximum_fusion.1 = bf16[2,512,2048]{2,1,0:T(8,128)(2,1)} fusion(bf16[1,512,2048]{2,1,0:T(8,128)(2,1)S(1)} %get-tuple-element.34, bf16[1,512,2048]{2,1,0:T(8,128)(2,1)S(1)} %get-tuple-element.48), kind=kLoop, calls=%fused_computation.1 | loop fusion | flops 2097152 | bytes 8388608 | tf_op jit(solution)/shard_map/stack | solution.py:143
  20.8 2.6 %collective-permute-done.3 = bf16[64,2048]{1,0:T(8,128)(2,1)S(1)} collective-permute-done((bf16[64,2048]{1,0:T(8,128)(2,1)S(1)}, bf16[64,2048]{1,0:T(8,128)(2,1)S(1)}, u32[]{:S(2)}, u32[]{:S(2)}) %collective-permute-start.3) | collective-permute-done | bytes 262176 | tf_op jit(solution)/shard_map/ppermute | solution.py:46
  23.4 2.2 %collective-permute-start.8 = (bf16[2,512,2048]{2,1,0:T(8,128)(2,1)}, bf16[2,512,2048]{2,1,0:T(8,128)(2,1)}, u32[]{:S(2)}, u32[]{:S(2)}) collective-permute-start(bf16[2,512,2048]{2,1,0:T(8,128)(2,1)} %pad_maximum_fusion.1), channel_id=1, source_target_pairs={{0,1},{1,0},{2,3},{3,2},{4,5},{5,4},{6,7},{7,6},{8,9},{9,8},{10,11... | collective-permute-start | bytes 12582920 | tf_op jit(solution)/shard_map/ppermute | solution.py:46
  26.2 2.1 %shard_map.100 = (bf16[384,512]{1,0:T(8,128)(2,1)}, f32[8,128]{1,0:T(8,128)}) custom-call(s32[2]{0:T(128)} %pad_add_fusion.info_ref, bf16[128,128]{1,0:T(8,128)(2,1)} %contracting_ref.1, bf16[64,128]{1,0:T(8,128)(2,1)} %bitcast.112, bf16[128,2048]{1,0:T(8,128)(2,1)} %queries_ref.1), custom_call_target="tpu_custom_call" | custom-call | flops 100000000 | bytes 1000000 | tf_op jit(solution)/shard_map/pallas_call | solution.py:126
  28.4 2.1 %pad_maximum_fusion = bf16[2,512,2048]{2,1,0:T(8,128)(2,1)S(1)} fusion(bf16[1,512,2048]{2,1,0:T(8,128)(2,1)S(1)} %get-tuple-element.33, bf16[1,512,2048]{2,1,0:T(8,128)(2,1)} %get-tuple-element.49), kind=kLoop, calls=%fused_computation | loop fusion | flops 2097152 | bytes 8388608 | tf_op jit(solution)/shard_map/stack | solution.py:143
  30.6 2.9 %collective-permute-start.6 = (bf16[64,2048]{1,0:T(8,128)(2,1)S(1)}, bf16[64,2048]{1,0:T(8,128)(2,1)S(1)}, u32[]{:S(2)}, u32[]{:S(2)}) collective-permute-start(bf16[64,2048]{1,0:T(8,128)(2,1)S(1)} %collective-permute-done.4), channel_id=1, source_target_pairs={{0,224},{1,225},{2,226},{3,227},{4,228},{5,229},{6,230},{7,231},{8... | collective-permute-start | bytes 786440 | tf_op jit(solution)/shard_map/ppermute | solution.py:46
  33.5 6.4 %collective-permute-done.5 = bf16[64,2048]{1,0:T(8,128)(2,1)S(1)} collective-permute-done((bf16[64,2048]{1,0:T(8,128)(2,1)S(1)}, bf16[64,2048]{1,0:T(8,128)(2,1)S(1)}, u32[]{:S(2)}, u32[]{:S(2)}) %collective-permute-start.5) | collective-permute-done | bytes 262176 | tf_op jit(solution)/shard_map/ppermute | solution.py:46
  39.9 2.0 %collective-permute-start.7 = (bf16[64,2048]{1,0:T(8,128)(2,1)S(1)}, bf16[64,2048]{1,0:T(8,128)(2,1)S(1)}, u32[]{:S(2)}, u32[]{:S(2)}) collective-permute-start(bf16[64,2048]{1,0:T(8,128)(2,1)S(1)} %collective-permute-done.5), channel_id=1, source_target_pairs={{0,32},{1,33},{2,34},{3,35},{4,36},{5,37},{6,38},{7,39},{8,40},{9,... | collective-permute-start | bytes 786440 | tf_op jit(solution)/shard_map/ppermute | solution.py:46
  42.6 5.7 %collective-permute-done.7 = bf16[64,2048]{1,0:T(8,128)(2,1)S(1)} collective-permute-done((bf16[64,2048]{1,0:T(8,128)(2,1)S(1)}, bf16[64,2048]{1,0:T(8,128)(2,1)S(1)}, u32[]{:S(2)}, u32[]{:S(2)}) %collective-permute-start.7) | collective-permute-done | bytes 262176 | tf_op jit(solution)/shard_map/ppermute | solution.py:46
  49.5 6.1 %collective-permute-done.10 = bf16[64,2048]{1,0:T(8,128)(2,1)S(1)} collective-permute-done((bf16[64,2048]{1,0:T(8,128)(2,1)S(1)}, bf16[64,2048]{1,0:T(8,128)(2,1)S(1)}, u32[]{:S(2)}, u32[]{:S(2)}) %collective-permute-start.10) | collective-permute-done | bytes 262176 | tf_op jit(solution)/shard_map/ppermute | solution.py:46
  55.8 1.0 convolution_convert_fusion
  56.8 2.3 %fusion.4 = f32[512,128]{1,0:T(8,128)S(1)} fusion(bf16[2,512,2048]{2,1,0:T(8,128)(2,1)} %collective-permute-done.8, bf16[384,2048]{1,0:T(8,128)(2,1)S(1)} %convolution_convert_fusion), kind=kOutput, calls=%fused_computation.7 | convolution fusion | flops 268435456 | bytes 2883584 | tf_op jit(solution)/shard_map/dot_general | solution.py:50
  59.2 3.2 %collective-permute-start.11 = (f32[512,128]{1,0:T(8,128)S(1)}, f32[512,128]{1,0:T(8,128)S(1)}, u32[]{:S(2)}, u32[]{:S(2)}) collective-permute-start(f32[512,128]{1,0:T(8,128)S(1)} %fusion.4), channel_id=1, source_target_pairs={{0,1},{1,0},{2,3},{3,2},{4,5},{5,4},{6,7},{7,6},{8,9},{9,8},{10,11... | collective-permute-start | bytes 786440 | tf_op jit(solution)/shard_map/ppermute | solution.py:46
  62.3 2.4 %fusion = f32[512,256]{1,0:T(8,128)S(1)} fusion(bf16[2,512,2048]{2,1,0:T(8,128)(2,1)} %collective-permute-done.8, bf16[384,2048]{1,0:T(8,128)(2,1)S(1)} %convolution_convert_fusion), kind=kOutput, calls=%fused_computation.3 | convolution fusion | flops 536870912 | bytes 3670016 | tf_op jit(solution)/shard_map/dot_general | solution.py:50
  65.6 3.0 %collective-permute-start.12 = (f32[2,128,128]{2,1,0:T(8,128)S(1)}, f32[2,128,128]{2,1,0:T(8,128)S(1)}, u32[]{:S(2)}, u32[]{:S(2)}) collective-permute-start(f32[2,128,128]{2,1,0:T(8,128)S(1)} %dynamic-slice_bitcast_fusion.4), channel_id=1, source_target_pairs={{0,4},{1,5},{2,6},{3,7},{4,0},{5,1},{6,2},{7,3},{8,12},{9,13},{10,... | collective-permute-start | bytes 393224 | tf_op jit(solution)/shard_map/ppermute | solution.py:46
  69.6 1.1 collective-permute-start.14
  70.8 1.1 collective-permute-done.12
  72.1 6.1 %collective-permute-done.14 = f32[2,128,256]{1,2,0:T(8,128)S(1)} collective-permute-done((f32[2,128,256]{1,2,0:T(8,128)S(1)}, f32[2,128,256]{1,2,0:T(8,128)S(1)}, u32[]{:S(2)}, u32[]{:S(2)}) %collective-permute-start.14) | collective-permute-done | bytes 262176 | tf_op jit(solution)/shard_map/ppermute | solution.py:46
  79.0 2.9 %collective-permute-start.17 = (f32[2,16,128]{2,1,0:T(8,128)S(1)}, f32[2,16,128]{2,1,0:T(8,128)S(1)}, u32[]{:S(2)}, u32[]{:S(2)}) collective-permute-start(f32[2,16,128]{2,1,0:T(8,128)S(1)} %get-tuple-element.44), channel_id=1, source_target_pairs={{0,3},{1,2},{2,1},{3,0},{4,7},{5,6},{6,5},{7,4},{8,11},{9,10},{10,... | collective-permute-start | bytes 49160 | tf_op jit(solution)/shard_map/ppermute | solution.py:46
  81.8 2.0 %collective-permute-done.17 = f32[2,16,128]{2,1,0:T(8,128)S(1)} collective-permute-done((f32[2,16,128]{2,1,0:T(8,128)S(1)}, f32[2,16,128]{2,1,0:T(8,128)S(1)}, u32[]{:S(2)}, u32[]{:S(2)}) %collective-permute-start.17) | collective-permute-done | bytes 16416 | tf_op jit(solution)/shard_map/ppermute | solution.py:46
  84.7 6.8 %all-to-all-start = ((bf16[32,2,2048]{2,1,0:T(2,128)(2,1)}), bf16[32,2,2048]{2,1,0:T(2,128)(2,1)S(1)}, u32[]{:S(2)}, u32[]{:S(2)}) async-start(bf16[32,2,2048]{2,1,0:T(2,128)(2,1)} %broadcast_in_dim.14), calls=%async_computation | async-start | bytes 524288 | tf_op jit(solution)/shard_map/all_to_all | solution.py:198
  91.6 11.5 %all-to-all-done = bf16[32,2,2048]{2,1,0:T(2,128)(2,1)S(1)} async-done(((bf16[32,2,2048]{2,1,0:T(2,128)(2,1)}), bf16[32,2,2048]{2,1,0:T(2,128)(2,1)S(1)}, u32[]{:S(2)}, u32[]{:S(2)}) %all-to-all-start) | async-done | bytes 262176 | tf_op jit(solution)/shard_map/all_to_all | solution.py:198
  104.0 2.4 %collective-permute-start.18 = (f32[2,24,256]{2,1,0:T(8,128)S(1)}, f32[2,24,256]{2,1,0:T(8,128)S(1)}, u32[]{:S(2)}, u32[]{:S(2)}) collective-permute-start(f32[2,24,256]{2,1,0:T(8,128)S(1)} %pad_maximum_fusion.4), channel_id=1, source_target_pairs={{0,1},{1,0},{2,3},{3,2},{4,5},{5,4},{6,7},{7,6},{8,9},{9,8},{10,11... | collective-permute-start | bytes 147464 | tf_op jit(solution)/shard_map/ppermute | solution.py:46
  106.4 0.9 collective-permute-done.18
  107.5 1.7 %collective-permute-start.21 = (f32[24,256]{1,0:T(8,128)S(1)}, f32[24,256]{1,0:T(8,128)S(1)}, u32[]{:S(2)}, u32[]{:S(2)}) collective-permute-start(f32[24,256]{1,0:T(8,128)S(1)} %get-tuple-element.47), channel_id=1, source_target_pairs={{0,6},{1,7},{2,4},{3,5},{4,2},{5,3},{6,0},{7,1},{8,14},{9,15},{10,... | collective-permute-start | bytes 73736 | tf_op jit(solution)/shard_map/ppermute | solution.py:46
  109.2 1.5 %collective-permute-start.20 = (f32[24,256]{1,0:T(8,128)S(1)}, f32[24,256]{1,0:T(8,128)S(1)}, u32[]{:S(2)}, u32[]{:S(2)}) collective-permute-start(f32[24,256]{1,0:T(8,128)S(1)} %get-tuple-element.46), channel_id=1, source_target_pairs={{0,4},{1,5},{2,6},{3,7},{4,0},{5,1},{6,2},{7,3},{8,12},{9,13},{10,... | collective-permute-start | bytes 73736 | tf_op jit(solution)/shard_map/ppermute | solution.py:46
  111.4 2.0 %collective-permute-done.20 = f32[24,256]{1,0:T(8,128)S(1)} collective-permute-done((f32[24,256]{1,0:T(8,128)S(1)}, f32[24,256]{1,0:T(8,128)S(1)}, u32[]{:S(2)}, u32[]{:S(2)}) %collective-permute-start.20) | collective-permute-done | bytes 24608 | tf_op jit(solution)/shard_map/ppermute | solution.py:46
  (85 shorter events, 10.8 us)
Async XLA Ops:
  2.3 10.3 %collective-permute-start.2 = (bf16[16,2048]{1,0:T(8,128)(2,1)S(1)}, bf16[16,2048]{1,0:T(8,128)(2,1)S(1)}, u32[]{:S(2)}, u32[]{:S(2)}) collective-permute-start(bf16[16,2048]{1,0:T(8,128)(2,1)S(1)} %get-tuple-element.30), channel_id=1, source_target_pairs={{0,24},{1,25},{2,26},{3,27},{4,28},{5,29},{6,30},{7,31},{8,0},{9,1... | collective-permute-start | bytes 196616 | tf_op jit(solution)/shard_map/ppermute | solution.py:46
  5.6 7.0 %collective-permute-start.1 = (bf16[16,2048]{1,0:T(8,128)(2,1)S(1)}, bf16[16,2048]{1,0:T(8,128)(2,1)S(1)}, u32[]{:S(2)}, u32[]{:S(2)}) collective-permute-start(bf16[16,2048]{1,0:T(8,128)(2,1)S(1)} %get-tuple-element.30), channel_id=1, source_target_pairs={{0,16},{1,17},{2,18},{3,19},{4,20},{5,21},{6,22},{7,23},{8,24},{9,... | collective-permute-start | bytes 196616 | tf_op jit(solution)/shard_map/ppermute | solution.py:46
  6.1 6.5 %collective-permute-start = (bf16[16,2048]{1,0:T(8,128)(2,1)S(1)}, bf16[16,2048]{1,0:T(8,128)(2,1)S(1)}, u32[]{:S(2)}, u32[]{:S(2)}) collective-permute-start(bf16[16,2048]{1,0:T(8,128)(2,1)S(1)} %get-tuple-element.30), channel_id=1, source_target_pairs={{0,8},{1,9},{2,10},{3,11},{4,12},{5,13},{6,14},{7,15},{8,16},{9,17... | collective-permute-start | bytes 196616 | tf_op jit(solution)/shard_map/ppermute | solution.py:46
  12.7 10.8 %collective-permute-start.3 = (bf16[64,2048]{1,0:T(8,128)(2,1)S(1)}, bf16[64,2048]{1,0:T(8,128)(2,1)S(1)}, u32[]{:S(2)}, u32[]{:S(2)}) collective-permute-start(bf16[64,2048]{1,0:T(8,128)(2,1)S(1)} %pad_maximum_fusion.2), channel_id=1, source_target_pairs={{0,32},{1,33},{2,34},{3,35},{4,36},{5,37},{6,38},{7,39},{8,40},{9,... | collective-permute-start | bytes 786440 | tf_op jit(solution)/shard_map/ppermute | solution.py:46
  14.4 9.0 %collective-permute-start.4 = (bf16[64,2048]{1,0:T(8,128)(2,1)S(1)}, bf16[64,2048]{1,0:T(8,128)(2,1)S(1)}, u32[]{:S(2)}, u32[]{:S(2)}) collective-permute-start(bf16[64,2048]{1,0:T(8,128)(2,1)S(1)} %pad_maximum_fusion.2), channel_id=1, source_target_pairs={{0,224},{1,225},{2,226},{3,227},{4,228},{5,229},{6,230},{7,231},{8... | collective-permute-start | bytes 786440 | tf_op jit(solution)/shard_map/ppermute | solution.py:46
  18.4 7.2 %copy-start.4 = (s32[4]{0:T(128)S(1)}, s32[4]{0:T(128)}, u32[]{:S(2)}) copy-start(s32[4]{0:T(128)} %param.12) | copy-start | bytes 52
  23.4 25.2 %collective-permute-start.8 = (bf16[2,512,2048]{2,1,0:T(8,128)(2,1)}, bf16[2,512,2048]{2,1,0:T(8,128)(2,1)}, u32[]{:S(2)}, u32[]{:S(2)}) collective-permute-start(bf16[2,512,2048]{2,1,0:T(8,128)(2,1)} %pad_maximum_fusion.1), channel_id=1, source_target_pairs={{0,1},{1,0},{2,3},{3,2},{4,5},{5,4},{6,7},{7,6},{8,9},{9,8},{10,11... | collective-permute-start | bytes 12582920 | tf_op jit(solution)/shard_map/ppermute | solution.py:46
  28.4 5.1 %copy-start.2 = (bf16[512,2048]{1,0:T(8,128)(2,1)S(1)}, bf16[512,2048]{1,0:T(8,128)(2,1)}, u32[]{:S(2)}) copy-start(bf16[512,2048]{1,0:T(8,128)(2,1)} %get-tuple-element.29) | copy-start | bytes 6291460
  30.5 25.3 %copy-start.3 = (bf16[384,512]{1,0:T(8,128)(2,1)S(1)}, bf16[384,512]{1,0:T(8,128)(2,1)}, u32[]{:S(2)}) copy-start(bf16[384,512]{1,0:T(8,128)(2,1)} %get-tuple-element.22) | copy-start | bytes 1179652
  30.5 9.4 %collective-permute-start.5 = (bf16[64,2048]{1,0:T(8,128)(2,1)S(1)}, bf16[64,2048]{1,0:T(8,128)(2,1)S(1)}, u32[]{:S(2)}, u32[]{:S(2)}) collective-permute-start(bf16[64,2048]{1,0:T(8,128)(2,1)S(1)} %collective-permute-done.3), channel_id=1, source_target_pairs={{0,32},{1,33},{2,34},{3,35},{4,36},{5,37},{6,38},{7,39},{8,40},{9,... | collective-permute-start | bytes 786440 | tf_op jit(solution)/shard_map/ppermute | solution.py:46
  30.6 9.3 %collective-permute-start.6 = (bf16[64,2048]{1,0:T(8,128)(2,1)S(1)}, bf16[64,2048]{1,0:T(8,128)(2,1)S(1)}, u32[]{:S(2)}, u32[]{:S(2)}) collective-permute-start(bf16[64,2048]{1,0:T(8,128)(2,1)S(1)} %collective-permute-done.4), channel_id=1, source_target_pairs={{0,224},{1,225},{2,226},{3,227},{4,228},{5,229},{6,230},{7,231},{8... | collective-permute-start | bytes 786440 | tf_op jit(solution)/shard_map/ppermute | solution.py:46
  39.9 8.4 %collective-permute-start.7 = (bf16[64,2048]{1,0:T(8,128)(2,1)S(1)}, bf16[64,2048]{1,0:T(8,128)(2,1)S(1)}, u32[]{:S(2)}, u32[]{:S(2)}) collective-permute-start(bf16[64,2048]{1,0:T(8,128)(2,1)S(1)} %collective-permute-done.5), channel_id=1, source_target_pairs={{0,32},{1,33},{2,34},{3,35},{4,36},{5,37},{6,38},{7,39},{8,40},{9,... | collective-permute-start | bytes 786440 | tf_op jit(solution)/shard_map/ppermute | solution.py:46
  41.9 6.7 %collective-permute-start.9 = (bf16[64,2048]{1,0:T(8,128)(2,1)S(1)}, bf16[64,2048]{1,0:T(8,128)(2,1)S(1)}, u32[]{:S(2)}, u32[]{:S(2)}) collective-permute-start(bf16[64,2048]{1,0:T(8,128)(2,1)S(1)} %collective-permute-done.6), channel_id=1, source_target_pairs={{0,224},{1,225},{2,226},{3,227},{4,228},{5,229},{6,230},{7,231},{8... | collective-permute-start | bytes 786440 | tf_op jit(solution)/shard_map/ppermute | solution.py:46
  48.7 7.0 %collective-permute-start.10 = (bf16[64,2048]{1,0:T(8,128)(2,1)S(1)}, bf16[64,2048]{1,0:T(8,128)(2,1)S(1)}, u32[]{:S(2)}, u32[]{:S(2)}) collective-permute-start(bf16[64,2048]{1,0:T(8,128)(2,1)S(1)} %collective-permute-done.7), channel_id=1, source_target_pairs={{0,32},{1,33},{2,34},{3,35},{4,36},{5,37},{6,38},{7,39},{8,40},{9,... | collective-permute-start | bytes 786440 | tf_op jit(solution)/shard_map/ppermute | solution.py:46
  59.2 5.7 %collective-permute-start.11 = (f32[512,128]{1,0:T(8,128)S(1)}, f32[512,128]{1,0:T(8,128)S(1)}, u32[]{:S(2)}, u32[]{:S(2)}) collective-permute-start(f32[512,128]{1,0:T(8,128)S(1)} %fusion.4), channel_id=1, source_target_pairs={{0,1},{1,0},{2,3},{3,2},{4,5},{5,4},{6,7},{7,6},{8,9},{9,8},{10,11... | collective-permute-start | bytes 786440 | tf_op jit(solution)/shard_map/ppermute | solution.py:46
  64.8 3.9 %collective-permute-start.13 = (f32[512,256]{1,0:T(8,128)S(1)}, f32[512,256]{1,0:T(8,128)S(1)}, u32[]{:S(2)}, u32[]{:S(2)}) collective-permute-start(f32[512,256]{1,0:T(8,128)S(1)} %fusion), channel_id=1, source_target_pairs={{0,1},{1,0},{2,3},{3,2},{4,5},{5,4},{6,7},{7,6},{8,9},{9,8},{10,11... | collective-permute-start | bytes 1572872 | tf_op jit(solution)/shard_map/ppermute | solution.py:46
  65.6 6.2 %collective-permute-start.12 = (f32[2,128,128]{2,1,0:T(8,128)S(1)}, f32[2,128,128]{2,1,0:T(8,128)S(1)}, u32[]{:S(2)}, u32[]{:S(2)}) collective-permute-start(f32[2,128,128]{2,1,0:T(8,128)S(1)} %dynamic-slice_bitcast_fusion.4), channel_id=1, source_target_pairs={{0,4},{1,5},{2,6},{3,7},{4,0},{5,1},{6,2},{7,3},{8,12},{9,13},{10,... | collective-permute-start | bytes 393224 | tf_op jit(solution)/shard_map/ppermute | solution.py:46
  69.4 22.2 %copy-start.1 = (f32[8,128]{1,0:T(8,128)S(1)}, f32[8,128]{1,0:T(8,128)}, u32[]{:S(2)}) copy-start(f32[8,128]{1,0:T(8,128)} %get-tuple-element.28) | copy-start | bytes 12292
  69.4 34.1 %copy-start = (bf16[128,2048]{1,0:T(8,128)(2,1)S(1)}, bf16[128,2048]{1,0:T(8,128)(2,1)}, u32[]{:S(2)}) copy-start(bf16[128,2048]{1,0:T(8,128)(2,1)} %queries_ref.1) | copy-start | bytes 1572868
  69.6 8.7 %collective-permute-start.14 = (f32[2,128,256]{1,2,0:T(8,128)S(1)}, f32[2,128,256]{1,2,0:T(8,128)S(1)}, u32[]{:S(2)}, u32[]{:S(2)}) collective-permute-start(f32[2,128,256]{1,2,0:T(8,128)S(1)} %bitcast.101), channel_id=1, source_target_pairs={{0,4},{1,5},{2,6},{3,7},{4,0},{5,1},{6,2},{7,3},{8,12},{9,13},{10,... | collective-permute-start | bytes 786440 | tf_op jit(solution)/shard_map/ppermute | solution.py:46
  78.5 3.4 %collective-permute-start.16 = (f32[2,16,128]{2,1,0:T(8,128)S(1)}, f32[2,16,128]{2,1,0:T(8,128)S(1)}, u32[]{:S(2)}, u32[]{:S(2)}) collective-permute-start(f32[2,16,128]{2,1,0:T(8,128)S(1)} %get-tuple-element.45), channel_id=1, source_target_pairs={{0,2},{1,3},{2,0},{3,1},{4,6},{5,7},{6,4},{7,5},{8,10},{9,11},{10,... | collective-permute-start | bytes 49160 | tf_op jit(solution)/shard_map/ppermute | solution.py:46
  79.0 4.9 %collective-permute-start.17 = (f32[2,16,128]{2,1,0:T(8,128)S(1)}, f32[2,16,128]{2,1,0:T(8,128)S(1)}, u32[]{:S(2)}, u32[]{:S(2)}) collective-permute-start(f32[2,16,128]{2,1,0:T(8,128)S(1)} %get-tuple-element.44), channel_id=1, source_target_pairs={{0,3},{1,2},{2,1},{3,0},{4,7},{5,6},{6,5},{7,4},{8,11},{9,10},{10,... | collective-permute-start | bytes 49160 | tf_op jit(solution)/shard_map/ppermute | solution.py:46
  81.8 2.0 %collective-permute-start.15 = (f32[2,16,128]{2,1,0:T(8,128)S(1)}, f32[2,16,128]{2,1,0:T(8,128)S(1)}, u32[]{:S(2)}, u32[]{:S(2)}) collective-permute-start(f32[2,16,128]{2,1,0:T(8,128)S(1)} %get-tuple-element.43), channel_id=1, source_target_pairs={{0,1},{1,0},{2,3},{3,2},{4,5},{5,4},{6,7},{7,6},{8,9},{9,8},{10,11... | collective-permute-start | bytes 49160 | tf_op jit(solution)/shard_map/ppermute | solution.py:46
  84.7 18.4 %all-to-all-start = ((bf16[32,2,2048]{2,1,0:T(2,128)(2,1)}), bf16[32,2,2048]{2,1,0:T(2,128)(2,1)S(1)}, u32[]{:S(2)}, u32[]{:S(2)}) async-start(bf16[32,2,2048]{2,1,0:T(2,128)(2,1)} %broadcast_in_dim.14), calls=%async_computation | async-start | bytes 524288 | tf_op jit(solution)/shard_map/all_to_all | solution.py:198
  104.0 3.3 %collective-permute-start.18 = (f32[2,24,256]{2,1,0:T(8,128)S(1)}, f32[2,24,256]{2,1,0:T(8,128)S(1)}, u32[]{:S(2)}, u32[]{:S(2)}) collective-permute-start(f32[2,24,256]{2,1,0:T(8,128)S(1)} %pad_maximum_fusion.4), channel_id=1, source_target_pairs={{0,1},{1,0},{2,3},{3,2},{4,5},{5,4},{6,7},{7,6},{8,9},{9,8},{10,11... | collective-permute-start | bytes 147464 | tf_op jit(solution)/shard_map/ppermute | solution.py:46
  107.3 3.3 %collective-permute-start.19 = (f32[24,256]{1,0:T(8,128)S(1)}, f32[24,256]{1,0:T(8,128)S(1)}, u32[]{:S(2)}, u32[]{:S(2)}) collective-permute-start(f32[24,256]{1,0:T(8,128)S(1)} %get-tuple-element.47), channel_id=1, source_target_pairs={{0,2},{1,3},{2,0},{3,1},{4,6},{5,7},{6,4},{7,5},{8,10},{9,11},{10,... | collective-permute-start | bytes 73736 | tf_op jit(solution)/shard_map/ppermute | solution.py:46
  107.5 3.9 %collective-permute-start.21 = (f32[24,256]{1,0:T(8,128)S(1)}, f32[24,256]{1,0:T(8,128)S(1)}, u32[]{:S(2)}, u32[]{:S(2)}) collective-permute-start(f32[24,256]{1,0:T(8,128)S(1)} %get-tuple-element.47), channel_id=1, source_target_pairs={{0,6},{1,7},{2,4},{3,5},{4,2},{5,3},{6,0},{7,1},{8,14},{9,15},{10,... | collective-permute-start | bytes 73736 | tf_op jit(solution)/shard_map/ppermute | solution.py:46
  109.2 4.2 %collective-permute-start.20 = (f32[24,256]{1,0:T(8,128)S(1)}, f32[24,256]{1,0:T(8,128)S(1)}, u32[]{:S(2)}, u32[]{:S(2)}) collective-permute-start(f32[24,256]{1,0:T(8,128)S(1)} %get-tuple-element.46), channel_id=1, source_target_pairs={{0,4},{1,5},{2,6},{3,7},{4,0},{5,1},{6,2},{7,3},{8,12},{9,13},{10,... | collective-permute-start | bytes 73736 | tf_op jit(solution)/shard_map/ppermute | solution.py:46

commit v4 on v3

--- a/solution.py
+++ b/solution.py
@@ -12,7 +12,8 @@
 K = 8192
 AXES = ("demo", "fsdp", "sketch")
 Z, X, F, S = 8, 4, 2, 4
-ROWS = 16
+ROWS = 14
+Z_BACK = (0, 1, 2, 6, 7, 3, 4, 5)
 LEFT = 2 * PROBE_ROWS
 RIGHT = 2 * PROBE_COLUMNS
 LAST = ((1,), (1,))
@@ -61,9 +62,15 @@
 def weights_kernel(info_ref, contracting_ref, expanding_ref, queries_ref, weights_ref, squares_ref):
     columns = Z * X * ROWS
     column = lax.broadcasted_iota(jnp.int32, (1, columns), 1)
-    kind = column % ROWS
-    z_from = (info_ref[0] + Z - column // (X * ROWS)) % Z
-    x_from = (info_ref[1] + X - (column // ROWS) % X) % X
+    block = jnp.zeros_like(column)
+    for k in range(1, Z * X):
+        block += jnp.where(column >= k * ROWS, 1, 0)
+    kind = column - block * ROWS
+    z_back = jnp.zeros_like(column)
+    for k, back in enumerate(Z_BACK):
+        z_back += jnp.where(block // X == k, back, 0)
+    z_from = (info_ref[0] + Z - z_back) % Z
+    x_from = (info_ref[1] + X - block % X) % X
     place = z_from * X + x_from
 
     def chosen(count, width, start):
@@ -114,15 +121,15 @@
 
     block = jnp.concatenate(
         [
-            lowrank_contract_matrix.T,
-            lowrank_expand_matrix.T,
-            output_feature_sketch.T,
-            input_feature_sketch.T,
-            jnp.zeros((2, feat), jnp.bfloat16),
-        ],
-        axis=0,
-    )
-    block = lax.dynamic_slice_in_dim(block, core * half, half, axis=1)
+            lax.dynamic_slice_in_dim(part.T, core * half, half, axis=1)
+            for part in (
+                lowrank_contract_matrix,
+                lowrank_expand_matrix,
+                output_feature_sketch,
+                input_feature_sketch,
+            )
+        ]
+    )
     weights, query_squares = pl.pallas_call(
         weights_kernel,
         out_shape=[shape((LEFT + RIGHT, Z * X * ROWS), jnp.bfloat16), shape((8, 128))],
@@ -136,44 +143,35 @@
         latent_random_map_expanding.T,
         queries,
     )
-    act = activations.reshape(tokens, feat)
-    cot = cotangents.reshape(tokens, feat)
-
-    def side(which):
-        return jnp.stack(
-            [lax.dynamic_slice_in_dim(v, which * half, half, axis=1) for v in (act, cot)]
-        )
-
     line = jnp.concatenate([block] + [send(block, shift(0, k)) for k in range(1, X)])
-    got = [line] + [None] * (Z - 1)
-    up = down = line
+    line, weights, query_squares = lax.optimization_barrier((line, weights, query_squares))
+    up, down = [line], [line]
     for k in range(1, Z // 2 + 1):
-        up = send(up, shift(1, 0))
-        got[k] = up
+        up.append(send(up[-1], shift(1, 0)))
         if k < Z // 2:
-            down = send(down, shift(-1, 0))
-            got[Z - k] = down
-        if k == 1:
-            give = side(1 - core)
-            give, up, down = lax.optimization_barrier((give, up, down))
-            theirs = send(give, CORE)
+            down.append(send(down[-1], shift(-1, 0)))
         if k == 2:
-            mine = side(core)
-            mine, weights, query_squares, up, down = lax.optimization_barrier(
-                (mine, weights, query_squares, up, down)
-            )
-        if k == 3:
-            theirs, up, down = lax.optimization_barrier((theirs, up, down))
-    rows = jnp.concatenate(got)
-    maps = jnp.dot(weights, rows, preferred_element_type=jnp.float32).astype(jnp.bfloat16)
+            early = jnp.concatenate([up[0], up[1], up[2], down[2], down[1]])
+            other_early = send(early, CORE)
+    late = jnp.concatenate([up[3], up[4], down[3]])
+    other_late = send(late, CORE)
+    rows = jnp.concatenate([early, late])
+    other = jnp.concatenate([other_early, other_late])
+    maps = jnp.concatenate(
+        [
+            jnp.dot(
+                weights, jnp.where(core == k, rows, other), preferred_element_type=jnp.float32
+            ).astype(jnp.bfloat16)
+            for k in (0, 1)
+        ],
+        axis=1,
+    )
     left_map, right_map = maps[:LEFT], maps[LEFT:]
-
-    right_away = send(dot(theirs[1], right_map, LAST), CORE)
-    right = dot(mine[1], right_map, LAST) + right_away
+    right = dot(cotangents.reshape(tokens, feat), right_map, LAST)
     right = right.reshape(F, own, tok_local, RIGHT)
-    right_sum = pick(right, f) + send(pick(right, 1 - f), FAR)
-    left_away = send(dot(theirs[0], left_map, LAST), CORE)
-    left = dot(mine[0], left_map, LAST) + left_away
+    give_right, left_map = lax.optimization_barrier((pick(right, 1 - f), left_map))
+    right_sum = pick(right, f) + send(give_right, FAR)
+    left = dot(activations.reshape(tokens, feat), left_map, LAST)
     left = left.reshape(F, own, tok_local, LEFT)
     left_sum = pick(left, f) + send(pick(left, 1 - f), FAR)
 

time: 114 us -> 107 us (0.939)
  waiting for transfers between devices: 45.5 us -> 39.7 us
  starting transfers between devices: 42.1 us -> 46.7 us
  other arithmetic: 6.08 us -> 1.74 us
  local copies, waits for them, and re-layouts: 10.2 us -> 8.17 us
    another operation x1 -> x0, local copies, waits for them, and re-layouts: 5.87 us -> none  [side(): jnp.stack([lax.dynamic_slice_in_dim(v, which * half, half, axis=1) for v...]
    ppermute x22 -> x21, starting transfers between devices: 35.3 us -> 40.1 us  [send(): return lax.ppermute(value, AXES, moves)]
    ppermute x22 -> x21, waiting for transfers between devices: 34 us -> 29.3 us  [send(): return lax.ppermute(value, AXES, moves)]
    another operation x2 -> x0, other arithmetic: 4.51 us -> none  [side(): jnp.stack([lax.dynamic_slice_in_dim(v, which * half, half, axis=1) for v...]
    unnamed x21 -> x18, local copies, waits for them, and re-layouts: 0.82 us -> 3.16 us
    dynamic_slice x0 -> x3, local copies, waits for them, and re-layouts: none -> 1.47 us  [shards(): lax.dynamic_slice_in_dim(part.T, core * half, half, axis=1)]
    dot_general x5 -> x3, matrix products: 6.51 us -> 5.3 us  [dot(): lax.dot_general(a, b, (contract, ((), ())), preferred_element_type=jnp.fl...]
  transfers between devices with their start and end apart: 23 -> 22, of which waited for: 12 -> 12; matrix products, arithmetic and copies ran while one was open for 14% -> 2% of each run, Pallas kernels for 2% -> 2%
where the time goes in v4:
time: 107 us; the launch traced here: 106 us
  starting transfers between devices  46.7 us (44%)
  waiting for transfers between devices  39.7 us (37%)
  local copies, waits for them, and re-layouts  8.17 us (8%)
  matrix products  7.44 us (7%)
  Pallas kernels  2.14 us (2%)
  other arithmetic  1.74 us (2%)
    ppermute x21, starting transfers between devices, send(): return lax.ppermute(value, AXES, moves)  40.1 us
    ppermute x21, waiting for transfers between devices, send(): return lax.ppermute(value, AXES, moves)  29.3 us
    all_to_all x1, waiting for transfers between devices, shards(): lax.all_to_all(copies, 'demo', 0, 0).reshape(Z * X * own, K // S)  10.4 us
    all_to_all x1, starting transfers between devices, shards(): lax.all_to_all(copies, 'demo', 0, 0).reshape(Z * X * own, K // S)  6.65 us
    dot_general x3, matrix products, dot(): lax.dot_general(a, b, (contract, ((), ())), preferred_element_type=jnp.fl...  5.3 us
    unnamed x18, local copies, waits for them, and re-layouts  3.16 us
  transfers between devices with their start and end apart: 22, of which 12 were waited for; matrix products, arithmetic and copies ran while one was open for 2% of the time, Pallas kernels for 2%

profile of v4, /device:TPU:1, one launch (start us, length us, event | category | flops | bytes accessed | tf_op | source)
XLA Modules:
  0.0 106.4 jit_solution(18111275500447986226)
XLA Ops:
  2.3 2.1 %collective-permute-start = (bf16[14,2048]{1,0:T(8,128)(2,1)S(1)}, bf16[14,2048]{1,0:T(8,128)(2,1)S(1)}, u32[]{:S(2)}, u32[]{:S(2)}) collective-permute-start(bf16[14,2048]{1,0:T(8,128)(2,1)S(1)} %pad_maximum_fusion.2), channel_id=1, source_target_pairs={{0,8},{1,9},{2,10},{3,11},{4,12},{5,13},{6,14},{7,15},{8,16},{9,17... | collective-permute-start | bytes 172040 | tf_op jit(solution)/shard_map/ppermute | solution.py:47
  4.4 2.5 %collective-permute-start.1 = (bf16[14,2048]{1,0:T(8,128)(2,1)S(1)}, bf16[14,2048]{1,0:T(8,128)(2,1)S(1)}, u32[]{:S(2)}, u32[]{:S(2)}) collective-permute-start(bf16[14,2048]{1,0:T(8,128)(2,1)S(1)} %pad_maximum_fusion.2), channel_id=1, source_target_pairs={{0,16},{1,17},{2,18},{3,19},{4,20},{5,21},{6,22},{7,23},{8,24},{9,... | collective-permute-start | bytes 172040 | tf_op jit(solution)/shard_map/ppermute | solution.py:47
  6.9 1.2 %collective-permute-start.2 = (bf16[14,2048]{1,0:T(8,128)(2,1)S(1)}, bf16[14,2048]{1,0:T(8,128)(2,1)S(1)}, u32[]{:S(2)}, u32[]{:S(2)}) collective-permute-start(bf16[14,2048]{1,0:T(8,128)(2,1)S(1)} %pad_maximum_fusion.2), channel_id=1, source_target_pairs={{0,24},{1,25},{2,26},{3,27},{4,28},{5,29},{6,30},{7,31},{8,0},{9,1... | collective-permute-start | bytes 172040 | tf_op jit(solution)/shard_map/ppermute | solution.py:47
  9.3 2.1 %shard_map.100 = (bf16[384,448]{1,0:T(8,128)(2,1)}, f32[8,128]{1,0:T(8,128)}) custom-call(s32[2]{0:T(128)} %pad_add_fusion.info_ref, bf16[128,128]{1,0:T(8,128)(2,1)} %contracting_ref.1, bf16[64,128]{1,0:T(8,128)(2,1)} %bitcast.96, bf16[128,2048]{1,0:T(8,128)(2,1)} %queries_ref.1), custom_call_target="tpu_custom_call" | custom-call | flops 100000000 | bytes 1000000 | tf_op jit(solution)/shard_map/pallas_call | solution.py:133
  12.1 1.7 %collective-permute-start.3 = (bf16[56,2048]{1,0:T(8,128)(2,1)S(1)}, bf16[56,2048]{1,0:T(8,128)(2,1)S(1)}, u32[]{:S(2)}, u32[]{:S(2)}) collective-permute-start(bf16[56,2048]{1,0:T(8,128)(2,1)S(1)} %concatenate.34), channel_id=1, source_target_pairs={{0,32},{1,33},{2,34},{3,35},{4,36},{5,37},{6,38},{7,39},{8,40},{9,... | collective-permute-start | bytes 688136 | tf_op jit(solution)/shard_map/ppermute | solution.py:47
  13.8 4.0 %collective-permute-start.5 = (bf16[56,2048]{1,0:T(8,128)(2,1)S(1)}, bf16[56,2048]{1,0:T(8,128)(2,1)S(1)}, u32[]{:S(2)}, u32[]{:S(2)}) collective-permute-start(bf16[56,2048]{1,0:T(8,128)(2,1)S(1)} %concatenate.34), channel_id=1, source_target_pairs={{0,224},{1,225},{2,226},{3,227},{4,228},{5,229},{6,230},{7,231},{8... | collective-permute-start | bytes 688136 | tf_op jit(solution)/shard_map/ppermute | solution.py:47
  17.9 4.3 %collective-permute-done.3 = bf16[56,2048]{1,0:T(8,128)(2,1)S(1)} collective-permute-done((bf16[56,2048]{1,0:T(8,128)(2,1)S(1)}, bf16[56,2048]{1,0:T(8,128)(2,1)S(1)}, u32[]{:S(2)}, u32[]{:S(2)}) %collective-permute-start.3) | collective-permute-done | bytes 229408 | tf_op jit(solution)/shard_map/ppermute | solution.py:47
  22.2 2.7 %collective-permute-start.6 = (bf16[56,2048]{1,0:T(8,128)(2,1)S(1)}, bf16[56,2048]{1,0:T(8,128)(2,1)S(1)}, u32[]{:S(2)}, u32[]{:S(2)}) collective-permute-start(bf16[56,2048]{1,0:T(8,128)(2,1)S(1)} %collective-permute-done.5), channel_id=1, source_target_pairs={{0,224},{1,225},{2,226},{3,227},{4,228},{5,229},{6,230},{7,231},{8... | collective-permute-start | bytes 688136 | tf_op jit(solution)/shard_map/ppermute | solution.py:47
  24.9 3.4 %collective-permute-done.4 = bf16[56,2048]{1,0:T(8,128)(2,1)S(1)} collective-permute-done((bf16[56,2048]{1,0:T(8,128)(2,1)S(1)}, bf16[56,2048]{1,0:T(8,128)(2,1)S(1)}, u32[]{:S(2)}, u32[]{:S(2)}) %collective-permute-start.4) | collective-permute-done | bytes 229408 | tf_op jit(solution)/shard_map/ppermute | solution.py:47
  28.4 3.4 %collective-permute-start.10 = (bf16[280,2048]{1,0:T(8,128)(2,1)S(1)}, bf16[280,2048]{1,0:T(8,128)(2,1)S(1)}, u32[]{:S(2)}, u32[]{:S(2)}) collective-permute-start(bf16[280,2048]{1,0:T(8,128)(2,1)S(1)} %get-tuple-element.21), channel_id=1, source_target_pairs={{0,1},{1,0},{2,3},{3,2},{4,5},{5,4},{6,7},{7,6},{8,9},{9,8},{10,11... | collective-permute-start | bytes 3440648 | tf_op jit(solution)/shard_map/ppermute | solution.py:47
  31.8 3.0 %collective-permute-start.9 = (bf16[56,2048]{1,0:T(8,128)(2,1)S(1)}, bf16[56,2048]{1,0:T(8,128)(2,1)S(1)}, u32[]{:S(2)}, u32[]{:S(2)}) collective-permute-start(bf16[56,2048]{1,0:T(8,128)(2,1)S(1)} %collective-permute-done.6), channel_id=1, source_target_pairs={{0,224},{1,225},{2,226},{3,227},{4,228},{5,229},{6,230},{7,231},{8... | collective-permute-start | bytes 688136 | tf_op jit(solution)/shard_map/ppermute | solution.py:47
  34.8 5.0 %collective-permute-done.9 = bf16[56,2048]{1,0:T(8,128)(2,1)S(1)} collective-permute-done((bf16[56,2048]{1,0:T(8,128)(2,1)S(1)}, bf16[56,2048]{1,0:T(8,128)(2,1)S(1)}, u32[]{:S(2)}, u32[]{:S(2)}) %collective-permute-start.9) | collective-permute-done | bytes 229408 | tf_op jit(solution)/shard_map/ppermute | solution.py:47
  39.8 1.1 %collective-permute-done.8 = bf16[56,2048]{1,0:T(8,128)(2,1)S(1)} collective-permute-done((bf16[56,2048]{1,0:T(8,128)(2,1)S(1)}, bf16[56,2048]{1,0:T(8,128)(2,1)S(1)}, u32[]{:S(2)}, u32[]{:S(2)}) %collective-permute-start.8) | collective-permute-done | bytes 229408 | tf_op jit(solution)/shard_map/ppermute | solution.py:47
  40.9 5.4 %collective-permute-start.11 = (bf16[168,2048]{1,0:T(8,128)(2,1)S(1)}, bf16[168,2048]{1,0:T(8,128)(2,1)S(1)}, u32[]{:S(2)}, u32[]{:S(2)}) collective-permute-start(bf16[168,2048]{1,0:T(8,128)(2,1)S(1)} %pad_maximum_fusion.1), channel_id=1, source_target_pairs={{0,1},{1,0},{2,3},{3,2},{4,5},{5,4},{6,7},{7,6},{8,9},{9,8},{10,11... | collective-permute-start | bytes 2064392 | tf_op jit(solution)/shard_map/ppermute | solution.py:47
  46.5 1.6 %collective-permute-done.11 = bf16[168,2048]{1,0:T(8,128)(2,1)S(1)} collective-permute-done((bf16[168,2048]{1,0:T(8,128)(2,1)S(1)}, bf16[168,2048]{1,0:T(8,128)(2,1)S(1)}, u32[]{:S(2)}, u32[]{:S(2)}) %collective-permute-start.11) | collective-permute-done | bytes 688160 | tf_op jit(solution)/shard_map/ppermute | solution.py:47
  50.3 2.1 %copy-done.3 = bf16[4,128,4096]{2,1,0:T(8,128)(2,1)S(1)} copy-done((bf16[4,128,4096]{2,1,0:T(8,128)(2,1)S(1)}, bf16[4,128,4096]{2,1,0:T(8,128)(2,1)}, u32[]{:S(2)}) %copy-start.3) | copy-done | bytes 4194328
  52.4 1.3 %fusion.7 = f32[512,256]{0,1:T(8,128)S(1)} fusion(bf16[512,4096]{1,0:T(8,128)(2,1)S(1)} %bitcast.97, bf16[384,2048]{1,0:T(8,128)(2,1)S(1)} %convolution_convert_fusion.1, bf16[384,2048]{1,0:T(8,128)(2,1)S(1)} %convolution_convert_fusion), kind=kOutput, calls=%fused_computation.10 | convolution fusion | flops 1077936128 | bytes 7864320 | tf_op jit(solution)/shard_map/dot_general | solution.py:51
  54.2 3.7 %convolution_bitcast_fusion = f32[512,128]{0,1:T(8,128)S(1)} fusion(bf16[128,4096]{1,0:T(8,128)(2,1)S(1)} %pad_maximum_fusion, bf16[512,4096]{1,0:T(8,128)(2,1)} %bitcast.84), kind=kOutput, calls=%fused_computation.11 | convolution fusion | flops 536870912 | bytes 5505024 | tf_op jit(solution)/shard_map/dot_general | solution.py:51
  58.1 3.0 %collective-permute-start.12 = (f32[2,128,128]{2,1,0:T(8,128)S(1)}, f32[2,128,128]{2,1,0:T(8,128)S(1)}, u32[]{:S(2)}, u32[]{:S(2)}) collective-permute-start(f32[2,128,128]{2,1,0:T(8,128)S(1)} %dynamic-slice_bitcast_fusion), channel_id=1, source_target_pairs={{0,4},{1,5},{2,6},{3,7},{4,0},{5,1},{6,2},{7,3},{8,12},{9,13},{10,... | collective-permute-start | bytes 393224 | tf_op jit(solution)/shard_map/ppermute | solution.py:47
  61.3 3.1 %collective-permute-done.12 = f32[2,128,128]{2,1,0:T(8,128)S(1)} collective-permute-done((f32[2,128,128]{2,1,0:T(8,128)S(1)}, f32[2,128,128]{2,1,0:T(8,128)S(1)}, u32[]{:S(2)}, u32[]{:S(2)}) %collective-permute-start.12) | collective-permute-done | bytes 131104 | tf_op jit(solution)/shard_map/ppermute | solution.py:47
  64.6 5.2 %collective-permute-done.13 = f32[2,128,256]{1,2,0:T(8,128)S(1)} collective-permute-done((f32[2,128,256]{1,2,0:T(8,128)S(1)}, f32[2,128,256]{1,2,0:T(8,128)S(1)}, u32[]{:S(2)}, u32[]{:S(2)}) %collective-permute-start.13) | collective-permute-done | bytes 262176 | tf_op jit(solution)/shard_map/ppermute | solution.py:47
  70.0 1.6 %collective-permute-start.15 = (f32[2,16,128]{2,1,0:T(8,128)S(1)}, f32[2,16,128]{2,1,0:T(8,128)S(1)}, u32[]{:S(2)}, u32[]{:S(2)}) collective-permute-start(f32[2,16,128]{2,1,0:T(8,128)S(1)} %get-tuple-element.39), channel_id=1, source_target_pairs={{0,2},{1,3},{2,0},{3,1},{4,6},{5,7},{6,4},{7,5},{8,10},{9,11},{10,... | collective-permute-start | bytes 49160 | tf_op jit(solution)/shard_map/ppermute | solution.py:47
  71.7 1.6 %collective-permute-start.16 = (f32[2,16,128]{2,1,0:T(8,128)S(1)}, f32[2,16,128]{2,1,0:T(8,128)S(1)}, u32[]{:S(2)}, u32[]{:S(2)}) collective-permute-start(f32[2,16,128]{2,1,0:T(8,128)S(1)} %get-tuple-element.38), channel_id=1, source_target_pairs={{0,3},{1,2},{2,1},{3,0},{4,7},{5,6},{6,5},{7,4},{8,11},{9,10},{10,... | collective-permute-start | bytes 49160 | tf_op jit(solution)/shard_map/ppermute | solution.py:47
  73.3 1.7 %collective-permute-done.16 = f32[2,16,128]{2,1,0:T(8,128)S(1)} collective-permute-done((f32[2,16,128]{2,1,0:T(8,128)S(1)}, f32[2,16,128]{2,1,0:T(8,128)S(1)}, u32[]{:S(2)}, u32[]{:S(2)}) %collective-permute-start.16) | collective-permute-done | bytes 16416 | tf_op jit(solution)/shard_map/ppermute | solution.py:47
  75.9 6.7 %all-to-all-start = ((bf16[32,2,2048]{2,1,0:T(2,128)(2,1)}), bf16[32,2,2048]{2,1,0:T(2,128)(2,1)S(1)}, u32[]{:S(2)}, u32[]{:S(2)}) async-start(bf16[32,2,2048]{2,1,0:T(2,128)(2,1)} %broadcast_in_dim.11), calls=%async_computation | async-start | bytes 524288 | tf_op jit(solution)/shard_map/all_to_all | solution.py:196
  82.5 10.4 %all-to-all-done = bf16[32,2,2048]{2,1,0:T(2,128)(2,1)S(1)} async-done(((bf16[32,2,2048]{2,1,0:T(2,128)(2,1)}), bf16[32,2,2048]{2,1,0:T(2,128)(2,1)S(1)}, u32[]{:S(2)}, u32[]{:S(2)}) %all-to-all-start) | async-done | bytes 262176 | tf_op jit(solution)/shard_map/all_to_all | solution.py:196
  93.9 3.6 %collective-permute-start.17 = (f32[2,24,256]{2,1,0:T(8,128)S(1)}, f32[2,24,256]{2,1,0:T(8,128)S(1)}, u32[]{:S(2)}, u32[]{:S(2)}) collective-permute-start(f32[2,24,256]{2,1,0:T(8,128)S(1)} %pad_maximum_fusion.4), channel_id=1, source_target_pairs={{0,1},{1,0},{2,3},{3,2},{4,5},{5,4},{6,7},{7,6},{8,9},{9,8},{10,11... | collective-permute-start | bytes 147464 | tf_op jit(solution)/shard_map/ppermute | solution.py:47
  98.4 1.4 %collective-permute-start.18 = (f32[24,256]{1,0:T(8,128)S(1)}, f32[24,256]{1,0:T(8,128)S(1)}, u32[]{:S(2)}, u32[]{:S(2)}) collective-permute-start(f32[24,256]{1,0:T(8,128)S(1)} %get-tuple-element.41), channel_id=1, source_target_pairs={{0,2},{1,3},{2,0},{3,1},{4,6},{5,7},{6,4},{7,5},{8,10},{9,11},{10,... | collective-permute-start | bytes 73736 | tf_op jit(solution)/shard_map/ppermute | solution.py:47
  99.7 1.7 %collective-permute-start.20 = (f32[24,256]{1,0:T(8,128)S(1)}, f32[24,256]{1,0:T(8,128)S(1)}, u32[]{:S(2)}, u32[]{:S(2)}) collective-permute-start(f32[24,256]{1,0:T(8,128)S(1)} %get-tuple-element.41), channel_id=1, source_target_pairs={{0,6},{1,7},{2,4},{3,5},{4,2},{5,3},{6,0},{7,1},{8,14},{9,15},{10,... | collective-permute-start | bytes 73736 | tf_op jit(solution)/shard_map/ppermute | solution.py:47
  101.5 1.1 %collective-permute-start.19 = (f32[24,256]{1,0:T(8,128)S(1)}, f32[24,256]{1,0:T(8,128)S(1)}, u32[]{:S(2)}, u32[]{:S(2)}) collective-permute-start(f32[24,256]{1,0:T(8,128)S(1)} %get-tuple-element.40), channel_id=1, source_target_pairs={{0,4},{1,5},{2,6},{3,7},{4,0},{5,1},{6,2},{7,3},{8,12},{9,13},{10,... | collective-permute-start | bytes 73736 | tf_op jit(solution)/shard_map/ppermute | solution.py:47
  102.6 1.0 collective-permute-done.20
  103.6 2.0 %collective-permute-done.19 = f32[24,256]{1,0:T(8,128)S(1)} collective-permute-done((f32[24,256]{1,0:T(8,128)S(1)}, f32[24,256]{1,0:T(8,128)S(1)}, u32[]{:S(2)}, u32[]{:S(2)}) %collective-permute-start.19) | collective-permute-done | bytes 24608 | tf_op jit(solution)/shard_map/ppermute | solution.py:47
  (83 shorter events, 11.3 us)
Async XLA Ops:
  0.0 0.8 copy-start
  2.3 9.2 %collective-permute-start = (bf16[14,2048]{1,0:T(8,128)(2,1)S(1)}, bf16[14,2048]{1,0:T(8,128)(2,1)S(1)}, u32[]{:S(2)}, u32[]{:S(2)}) collective-permute-start(bf16[14,2048]{1,0:T(8,128)(2,1)S(1)} %pad_maximum_fusion.2), channel_id=1, source_target_pairs={{0,8},{1,9},{2,10},{3,11},{4,12},{5,13},{6,14},{7,15},{8,16},{9,17... | collective-permute-start | bytes 172040 | tf_op jit(solution)/shard_map/ppermute | solution.py:47
  4.4 7.1 %collective-permute-start.1 = (bf16[14,2048]{1,0:T(8,128)(2,1)S(1)}, bf16[14,2048]{1,0:T(8,128)(2,1)S(1)}, u32[]{:S(2)}, u32[]{:S(2)}) collective-permute-start(bf16[14,2048]{1,0:T(8,128)(2,1)S(1)} %pad_maximum_fusion.2), channel_id=1, source_target_pairs={{0,16},{1,17},{2,18},{3,19},{4,20},{5,21},{6,22},{7,23},{8,24},{9,... | collective-permute-start | bytes 172040 | tf_op jit(solution)/shard_map/ppermute | solution.py:47
  6.9 4.6 %collective-permute-start.2 = (bf16[14,2048]{1,0:T(8,128)(2,1)S(1)}, bf16[14,2048]{1,0:T(8,128)(2,1)S(1)}, u32[]{:S(2)}, u32[]{:S(2)}) collective-permute-start(bf16[14,2048]{1,0:T(8,128)(2,1)S(1)} %pad_maximum_fusion.2), channel_id=1, source_target_pairs={{0,24},{1,25},{2,26},{3,27},{4,28},{5,29},{6,30},{7,31},{8,0},{9,1... | collective-permute-start | bytes 172040 | tf_op jit(solution)/shard_map/ppermute | solution.py:47
  12.1 10.1 %collective-permute-start.3 = (bf16[56,2048]{1,0:T(8,128)(2,1)S(1)}, bf16[56,2048]{1,0:T(8,128)(2,1)S(1)}, u32[]{:S(2)}, u32[]{:S(2)}) collective-permute-start(bf16[56,2048]{1,0:T(8,128)(2,1)S(1)} %concatenate.34), channel_id=1, source_target_pairs={{0,32},{1,33},{2,34},{3,35},{4,36},{5,37},{6,38},{7,39},{8,40},{9,... | collective-permute-start | bytes 688136 | tf_op jit(solution)/shard_map/ppermute | solution.py:47
  13.8 8.3 %collective-permute-start.5 = (bf16[56,2048]{1,0:T(8,128)(2,1)S(1)}, bf16[56,2048]{1,0:T(8,128)(2,1)S(1)}, u32[]{:S(2)}, u32[]{:S(2)}) collective-permute-start(bf16[56,2048]{1,0:T(8,128)(2,1)S(1)} %concatenate.34), channel_id=1, source_target_pairs={{0,224},{1,225},{2,226},{3,227},{4,228},{5,229},{6,230},{7,231},{8... | collective-permute-start | bytes 688136 | tf_op jit(solution)/shard_map/ppermute | solution.py:47
  22.2 6.1 %collective-permute-start.4 = (bf16[56,2048]{1,0:T(8,128)(2,1)S(1)}, bf16[56,2048]{1,0:T(8,128)(2,1)S(1)}, u32[]{:S(2)}, u32[]{:S(2)}) collective-permute-start(bf16[56,2048]{1,0:T(8,128)(2,1)S(1)} %collective-permute-done.3), channel_id=1, source_target_pairs={{0,32},{1,33},{2,34},{3,35},{4,36},{5,37},{6,38},{7,39},{8,40},{9,... | collective-permute-start | bytes 688136 | tf_op jit(solution)/shard_map/ppermute | solution.py:47
  22.2 6.1 %collective-permute-start.6 = (bf16[56,2048]{1,0:T(8,128)(2,1)S(1)}, bf16[56,2048]{1,0:T(8,128)(2,1)S(1)}, u32[]{:S(2)}, u32[]{:S(2)}) collective-permute-start(bf16[56,2048]{1,0:T(8,128)(2,1)S(1)} %collective-permute-done.5), channel_id=1, source_target_pairs={{0,224},{1,225},{2,226},{3,227},{4,228},{5,229},{6,230},{7,231},{8... | collective-permute-start | bytes 688136 | tf_op jit(solution)/shard_map/ppermute | solution.py:47
  28.2 6.6 %collective-permute-start.7 = (bf16[56,2048]{1,0:T(8,128)(2,1)S(1)}, bf16[56,2048]{1,0:T(8,128)(2,1)S(1)}, u32[]{:S(2)}, u32[]{:S(2)}) collective-permute-start(bf16[56,2048]{1,0:T(8,128)(2,1)S(1)} %collective-permute-done.4), channel_id=1, source_target_pairs={{0,32},{1,33},{2,34},{3,35},{4,36},{5,37},{6,38},{7,39},{8,40},{9,... | collective-permute-start | bytes 688136 | tf_op jit(solution)/shard_map/ppermute | solution.py:47
  28.4 18.0 %collective-permute-start.10 = (bf16[280,2048]{1,0:T(8,128)(2,1)S(1)}, bf16[280,2048]{1,0:T(8,128)(2,1)S(1)}, u32[]{:S(2)}, u32[]{:S(2)}) collective-permute-start(bf16[280,2048]{1,0:T(8,128)(2,1)S(1)} %get-tuple-element.21), channel_id=1, source_target_pairs={{0,1},{1,0},{2,3},{3,2},{4,5},{5,4},{6,7},{7,6},{8,9},{9,8},{10,11... | collective-permute-start | bytes 3440648 | tf_op jit(solution)/shard_map/ppermute | solution.py:47
  31.8 8.0 %collective-permute-start.9 = (bf16[56,2048]{1,0:T(8,128)(2,1)S(1)}, bf16[56,2048]{1,0:T(8,128)(2,1)S(1)}, u32[]{:S(2)}, u32[]{:S(2)}) collective-permute-start(bf16[56,2048]{1,0:T(8,128)(2,1)S(1)} %collective-permute-done.6), channel_id=1, source_target_pairs={{0,224},{1,225},{2,226},{3,227},{4,228},{5,229},{6,230},{7,231},{8... | collective-permute-start | bytes 688136 | tf_op jit(solution)/shard_map/ppermute | solution.py:47
  34.8 6.1 %collective-permute-start.8 = (bf16[56,2048]{1,0:T(8,128)(2,1)S(1)}, bf16[56,2048]{1,0:T(8,128)(2,1)S(1)}, u32[]{:S(2)}, u32[]{:S(2)}) collective-permute-start(bf16[56,2048]{1,0:T(8,128)(2,1)S(1)} %collective-permute-done.7), channel_id=1, source_target_pairs={{0,32},{1,33},{2,34},{3,35},{4,36},{5,37},{6,38},{7,39},{8,40},{9,... | collective-permute-start | bytes 688136 | tf_op jit(solution)/shard_map/ppermute | solution.py:47
  40.9 7.2 %collective-permute-start.11 = (bf16[168,2048]{1,0:T(8,128)(2,1)S(1)}, bf16[168,2048]{1,0:T(8,128)(2,1)S(1)}, u32[]{:S(2)}, u32[]{:S(2)}) collective-permute-start(bf16[168,2048]{1,0:T(8,128)(2,1)S(1)} %pad_maximum_fusion.1), channel_id=1, source_target_pairs={{0,1},{1,0},{2,3},{3,2},{4,5},{5,4},{6,7},{7,6},{8,9},{9,8},{10,11... | collective-permute-start | bytes 2064392 | tf_op jit(solution)/shard_map/ppermute | solution.py:47
  46.4 1.8 %copy-start.4 = (bf16[384,448]{1,0:T(8,128)(2,1)S(1)}, bf16[384,448]{1,0:T(8,128)(2,1)}, u32[]{:S(2)}) copy-start(bf16[384,448]{1,0:T(8,128)(2,1)} %get-tuple-element.14) | copy-start | bytes 1032196
  50.2 2.2 %copy-start.3 = (bf16[4,128,4096]{2,1,0:T(8,128)(2,1)S(1)}, bf16[4,128,4096]{2,1,0:T(8,128)(2,1)}, u32[]{:S(2)}) copy-start(bf16[4,128,4096]{2,1,0:T(8,128)(2,1)} %param.11) | copy-start | bytes 12582916
  58.0 24.6 %copy-start.2 = (f32[8,128]{1,0:T(8,128)S(1)}, f32[8,128]{1,0:T(8,128)}, u32[]{:S(2)}) copy-start(f32[8,128]{1,0:T(8,128)} %get-tuple-element.18) | copy-start | bytes 12292
  58.1 35.3 %copy-start.1 = (bf16[128,2048]{1,0:T(8,128)(2,1)S(1)}, bf16[128,2048]{1,0:T(8,128)(2,1)}, u32[]{:S(2)}) copy-start(bf16[128,2048]{1,0:T(8,128)(2,1)} %queries_ref.1) | copy-start | bytes 1572868
  58.1 6.3 %collective-permute-start.12 = (f32[2,128,128]{2,1,0:T(8,128)S(1)}, f32[2,128,128]{2,1,0:T(8,128)S(1)}, u32[]{:S(2)}, u32[]{:S(2)}) collective-permute-start(f32[2,128,128]{2,1,0:T(8,128)S(1)} %dynamic-slice_bitcast_fusion), channel_id=1, source_target_pairs={{0,4},{1,5},{2,6},{3,7},{4,0},{5,1},{6,2},{7,3},{8,12},{9,13},{10,... | collective-permute-start | bytes 393224 | tf_op jit(solution)/shard_map/ppermute | solution.py:47
  61.1 8.7 %collective-permute-start.13 = (f32[2,128,256]{1,2,0:T(8,128)S(1)}, f32[2,128,256]{1,2,0:T(8,128)S(1)}, u32[]{:S(2)}, u32[]{:S(2)}) collective-permute-start(f32[2,128,256]{1,2,0:T(8,128)S(1)} %bitcast.89), channel_id=1, source_target_pairs={{0,4},{1,5},{2,6},{3,7},{4,0},{5,1},{6,2},{7,3},{8,12},{9,13},{10,... | collective-permute-start | bytes 786440 | tf_op jit(solution)/shard_map/ppermute | solution.py:47
  70.0 3.3 %collective-permute-start.15 = (f32[2,16,128]{2,1,0:T(8,128)S(1)}, f32[2,16,128]{2,1,0:T(8,128)S(1)}, u32[]{:S(2)}, u32[]{:S(2)}) collective-permute-start(f32[2,16,128]{2,1,0:T(8,128)S(1)} %get-tuple-element.39), channel_id=1, source_target_pairs={{0,2},{1,3},{2,0},{3,1},{4,6},{5,7},{6,4},{7,5},{8,10},{9,11},{10,... | collective-permute-start | bytes 49160 | tf_op jit(solution)/shard_map/ppermute | solution.py:47
  71.7 3.3 %collective-permute-start.16 = (f32[2,16,128]{2,1,0:T(8,128)S(1)}, f32[2,16,128]{2,1,0:T(8,128)S(1)}, u32[]{:S(2)}, u32[]{:S(2)}) collective-permute-start(f32[2,16,128]{2,1,0:T(8,128)S(1)} %get-tuple-element.38), channel_id=1, source_target_pairs={{0,3},{1,2},{2,1},{3,0},{4,7},{5,6},{6,5},{7,4},{8,11},{9,10},{10,... | collective-permute-start | bytes 49160 | tf_op jit(solution)/shard_map/ppermute | solution.py:47
  73.3 1.7 %collective-permute-start.14 = (f32[2,16,128]{2,1,0:T(8,128)S(1)}, f32[2,16,128]{2,1,0:T(8,128)S(1)}, u32[]{:S(2)}, u32[]{:S(2)}) collective-permute-start(f32[2,16,128]{2,1,0:T(8,128)S(1)} %get-tuple-element.37), channel_id=1, source_target_pairs={{0,1},{1,0},{2,3},{3,2},{4,5},{5,4},{6,7},{7,6},{8,9},{9,8},{10,11... | collective-permute-start | bytes 49160 | tf_op jit(solution)/shard_map/ppermute | solution.py:47
  75.9 17.1 %all-to-all-start = ((bf16[32,2,2048]{2,1,0:T(2,128)(2,1)}), bf16[32,2,2048]{2,1,0:T(2,128)(2,1)S(1)}, u32[]{:S(2)}, u32[]{:S(2)}) async-start(bf16[32,2,2048]{2,1,0:T(2,128)(2,1)} %broadcast_in_dim.11), calls=%async_computation | async-start | bytes 524288 | tf_op jit(solution)/shard_map/all_to_all | solution.py:196
  93.9 4.5 %collective-permute-start.17 = (f32[2,24,256]{2,1,0:T(8,128)S(1)}, f32[2,24,256]{2,1,0:T(8,128)S(1)}, u32[]{:S(2)}, u32[]{:S(2)}) collective-permute-start(f32[2,24,256]{2,1,0:T(8,128)S(1)} %pad_maximum_fusion.4), channel_id=1, source_target_pairs={{0,1},{1,0},{2,3},{3,2},{4,5},{5,4},{6,7},{7,6},{8,9},{9,8},{10,11... | collective-permute-start | bytes 147464 | tf_op jit(solution)/shard_map/ppermute | solution.py:47
  98.4 4.2 %collective-permute-start.18 = (f32[24,256]{1,0:T(8,128)S(1)}, f32[24,256]{1,0:T(8,128)S(1)}, u32[]{:S(2)}, u32[]{:S(2)}) collective-permute-start(f32[24,256]{1,0:T(8,128)S(1)} %get-tuple-element.41), channel_id=1, source_target_pairs={{0,2},{1,3},{2,0},{3,1},{4,6},{5,7},{6,4},{7,5},{8,10},{9,11},{10,... | collective-permute-start | bytes 73736 | tf_op jit(solution)/shard_map/ppermute | solution.py:47
  99.7 3.9 %collective-permute-start.20 = (f32[24,256]{1,0:T(8,128)S(1)}, f32[24,256]{1,0:T(8,128)S(1)}, u32[]{:S(2)}, u32[]{:S(2)}) collective-permute-start(f32[24,256]{1,0:T(8,128)S(1)} %get-tuple-element.41), channel_id=1, source_target_pairs={{0,6},{1,7},{2,4},{3,5},{4,2},{5,3},{6,0},{7,1},{8,14},{9,15},{10,... | collective-permute-start | bytes 73736 | tf_op jit(solution)/shard_map/ppermute | solution.py:47
  101.5 4.2 %collective-permute-start.19 = (f32[24,256]{1,0:T(8,128)S(1)}, f32[24,256]{1,0:T(8,128)S(1)}, u32[]{:S(2)}, u32[]{:S(2)}) collective-permute-start(f32[24,256]{1,0:T(8,128)S(1)} %get-tuple-element.40), channel_id=1, source_target_pairs={{0,4},{1,5},{2,6},{3,7},{4,0},{5,1},{6,2},{7,3},{8,12},{9,13},{10,... | collective-permute-start | bytes 73736 | tf_op jit(solution)/shard_map/ppermute | solution.py:47

commit v5 on v4

--- a/solution.py
+++ b/solution.py
@@ -13,7 +13,7 @@
 AXES = ("demo", "fsdp", "sketch")
 Z, X, F, S = 8, 4, 2, 4
 ROWS = 14
-Z_BACK = (0, 1, 2, 6, 7, 3, 4, 5)
+Z_BACK = (0, 1, 2, 3, 5, 6, 7, 4)
 LEFT = 2 * PROBE_ROWS
 RIGHT = 2 * PROBE_COLUMNS
 LAST = ((1,), (1,))
@@ -150,10 +150,9 @@
         up.append(send(up[-1], shift(1, 0)))
         if k < Z // 2:
             down.append(send(down[-1], shift(-1, 0)))
-        if k == 2:
-            early = jnp.concatenate([up[0], up[1], up[2], down[2], down[1]])
-            other_early = send(early, CORE)
-    late = jnp.concatenate([up[3], up[4], down[3]])
+    early = jnp.concatenate(up[:4] + down[:0:-1])
+    other_early = send(early, CORE)
+    late = up[4]
     other_late = send(late, CORE)
     rows = jnp.concatenate([early, late])
     other = jnp.concatenate([other_early, other_late])
@@ -169,8 +168,7 @@
     left_map, right_map = maps[:LEFT], maps[LEFT:]
     right = dot(cotangents.reshape(tokens, feat), right_map, LAST)
     right = right.reshape(F, own, tok_local, RIGHT)
-    give_right, left_map = lax.optimization_barrier((pick(right, 1 - f), left_map))
-    right_sum = pick(right, f) + send(give_right, FAR)
+    right_sum = pick(right, f) + send(pick(right, 1 - f), FAR)
     left = dot(activations.reshape(tokens, feat), left_map, LAST)
     left = left.reshape(F, own, tok_local, LEFT)
     left_sum = pick(left, f) + send(pick(left, 1 - f), FAR)

time: 107 us -> 110 us (1.028)
  local copies, waits for them, and re-layouts: 8.17 us -> 15.1 us
  starting transfers between devices: 46.7 us -> 42.3 us
    unnamed x18 -> x28, local copies, waits for them, and re-layouts: 3.16 us -> 9.38 us
    ppermute x21, starting transfers between devices: 40.1 us -> 35 us  [send(): return lax.ppermute(value, AXES, moves)]
    all_to_all x1, waiting for transfers between devices: 10.4 us -> 11.5 us  [shards(): lax.all_to_all(copies, 'demo', 0, 0).reshape(Z * X * own, K // S)]
  transfers between devices with their start and end apart: 22 -> 22, of which waited for: 12 -> 11; matrix products, arithmetic and copies ran while one was open for 2% -> 8% of each run, Pallas kernels for 2% -> 2%
where the time goes in v5:
time: 110 us; the launch traced here: 109 us
  starting transfers between devices  42.3 us (38%)
  waiting for transfers between devices  40.3 us (37%)
  local copies, waits for them, and re-layouts  15.1 us (14%)
  matrix products  7.46 us (7%)
  Pallas kernels  2.14 us (2%)
  other arithmetic  1.64 us (1%)
    ppermute x21, starting transfers between devices, send(): return lax.ppermute(value, AXES, moves)  35 us
    ppermute x21, waiting for transfers between devices, send(): return lax.ppermute(value, AXES, moves)  28.8 us
    all_to_all x1, waiting for transfers between devices, shards(): lax.all_to_all(copies, 'demo', 0, 0).reshape(Z * X * own, K // S)  11.5 us
    unnamed x28, local copies, waits for them, and re-layouts  9.38 us
    all_to_all x1, starting transfers between devices, shards(): lax.all_to_all(copies, 'demo', 0, 0).reshape(Z * X * own, K // S)  7.37 us
    dot_general x3, matrix products, dot(): lax.dot_general(a, b, (contract, ((), ())), preferred_element_type=jnp.fl...  5.33 us
  transfers between devices with their start and end apart: 22, of which 11 were waited for; matrix products, arithmetic and copies ran while one was open for 8% of the time, Pallas kernels for 2%

profile of v5, /device:TPU:1, one launch (start us, length us, event | category | flops | bytes accessed | tf_op | source)
XLA Modules:
  0.0 109.4 jit_solution(14165432287356145978)
XLA Ops:
  2.3 2.1 %collective-permute-start = (bf16[14,2048]{1,0:T(8,128)(2,1)S(1)}, bf16[14,2048]{1,0:T(8,128)(2,1)S(1)}, u32[]{:S(2)}, u32[]{:S(2)}) collective-permute-start(bf16[14,2048]{1,0:T(8,128)(2,1)S(1)} %pad_maximum_fusion.4), channel_id=1, source_target_pairs={{0,8},{1,9},{2,10},{3,11},{4,12},{5,13},{6,14},{7,15},{8,16},{9,17... | collective-permute-start | bytes 172040 | tf_op jit(solution)/shard_map/ppermute | solution.py:47
  4.4 2.5 %collective-permute-start.1 = (bf16[14,2048]{1,0:T(8,128)(2,1)S(1)}, bf16[14,2048]{1,0:T(8,128)(2,1)S(1)}, u32[]{:S(2)}, u32[]{:S(2)}) collective-permute-start(bf16[14,2048]{1,0:T(8,128)(2,1)S(1)} %pad_maximum_fusion.4), channel_id=1, source_target_pairs={{0,16},{1,17},{2,18},{3,19},{4,20},{5,21},{6,22},{7,23},{8,24},{9,... | collective-permute-start | bytes 172040 | tf_op jit(solution)/shard_map/ppermute | solution.py:47
  6.9 1.2 %collective-permute-start.2 = (bf16[14,2048]{1,0:T(8,128)(2,1)S(1)}, bf16[14,2048]{1,0:T(8,128)(2,1)S(1)}, u32[]{:S(2)}, u32[]{:S(2)}) collective-permute-start(bf16[14,2048]{1,0:T(8,128)(2,1)S(1)} %pad_maximum_fusion.4), channel_id=1, source_target_pairs={{0,24},{1,25},{2,26},{3,27},{4,28},{5,29},{6,30},{7,31},{8,0},{9,1... | collective-permute-start | bytes 172040 | tf_op jit(solution)/shard_map/ppermute | solution.py:47
  8.6 2.1 %shard_map.100 = (bf16[384,448]{1,0:T(8,128)(2,1)}, f32[8,128]{1,0:T(8,128)}) custom-call(s32[2]{0:T(128)} %pad_add_fusion.info_ref, bf16[128,128]{1,0:T(8,128)(2,1)} %contracting_ref.1, bf16[64,128]{1,0:T(8,128)(2,1)} %bitcast.95, bf16[128,2048]{1,0:T(8,128)(2,1)} %queries_ref.1), custom_call_target="tpu_custom_call" | custom-call | flops 100000000 | bytes 1000000 | tf_op jit(solution)/shard_map/pallas_call | solution.py:133
  11.4 1.7 %collective-permute-start.3 = (bf16[56,2048]{1,0:T(8,128)(2,1)S(1)}, bf16[56,2048]{1,0:T(8,128)(2,1)S(1)}, u32[]{:S(2)}, u32[]{:S(2)}) collective-permute-start(bf16[56,2048]{1,0:T(8,128)(2,1)S(1)} %concatenate.31), channel_id=1, source_target_pairs={{0,32},{1,33},{2,34},{3,35},{4,36},{5,37},{6,38},{7,39},{8,40},{9,... | collective-permute-start | bytes 688136 | tf_op jit(solution)/shard_map/ppermute | solution.py:47
  13.1 4.0 %collective-permute-start.6 = (bf16[56,2048]{1,0:T(8,128)(2,1)S(1)}, bf16[56,2048]{1,0:T(8,128)(2,1)S(1)}, u32[]{:S(2)}, u32[]{:S(2)}) collective-permute-start(bf16[56,2048]{1,0:T(8,128)(2,1)S(1)} %concatenate.31), channel_id=1, source_target_pairs={{0,224},{1,225},{2,226},{3,227},{4,228},{5,229},{6,230},{7,231},{8... | collective-permute-start | bytes 688136 | tf_op jit(solution)/shard_map/ppermute | solution.py:47
  17.8 3.5 %collective-permute-done.3 = bf16[56,2048]{1,0:T(8,128)(2,1)S(1)} collective-permute-done((bf16[56,2048]{1,0:T(8,128)(2,1)S(1)}, bf16[56,2048]{1,0:T(8,128)(2,1)S(1)}, u32[]{:S(2)}, u32[]{:S(2)}) %collective-permute-start.3) | collective-permute-done | bytes 229408 | tf_op jit(solution)/shard_map/ppermute | solution.py:47
  21.4 2.7 %collective-permute-start.7 = (bf16[56,2048]{1,0:T(8,128)(2,1)S(1)}, bf16[56,2048]{1,0:T(8,128)(2,1)S(1)}, u32[]{:S(2)}, u32[]{:S(2)}) collective-permute-start(bf16[56,2048]{1,0:T(8,128)(2,1)S(1)} %collective-permute-done.6), channel_id=1, source_target_pairs={{0,224},{1,225},{2,226},{3,227},{4,228},{5,229},{6,230},{7,231},{8... | collective-permute-start | bytes 688136 | tf_op jit(solution)/shard_map/ppermute | solution.py:47
  24.8 2.7 %collective-permute-done.4 = bf16[56,2048]{1,0:T(8,128)(2,1)S(1)} collective-permute-done((bf16[56,2048]{1,0:T(8,128)(2,1)S(1)}, bf16[56,2048]{1,0:T(8,128)(2,1)S(1)}, u32[]{:S(2)}, u32[]{:S(2)}) %collective-permute-start.4) | collective-permute-done | bytes 229408 | tf_op jit(solution)/shard_map/ppermute | solution.py:47
  27.5 2.7 %collective-permute-start.8 = (bf16[56,2048]{1,0:T(8,128)(2,1)S(1)}, bf16[56,2048]{1,0:T(8,128)(2,1)S(1)}, u32[]{:S(2)}, u32[]{:S(2)}) collective-permute-start(bf16[56,2048]{1,0:T(8,128)(2,1)S(1)} %collective-permute-done.7), channel_id=1, source_target_pairs={{0,224},{1,225},{2,226},{3,227},{4,228},{5,229},{6,230},{7,231},{8... | collective-permute-start | bytes 688136 | tf_op jit(solution)/shard_map/ppermute | solution.py:47
  30.9 2.7 %collective-permute-done.5 = bf16[56,2048]{1,0:T(8,128)(2,1)S(1)} collective-permute-done((bf16[56,2048]{1,0:T(8,128)(2,1)S(1)}, bf16[56,2048]{1,0:T(8,128)(2,1)S(1)}, u32[]{:S(2)}, u32[]{:S(2)}) %collective-permute-start.5) | collective-permute-done | bytes 229408 | tf_op jit(solution)/shard_map/ppermute | solution.py:47
  36.5 1.3 %copy-done.4 = bf16[448,2048]{1,0:T(8,128)(2,1)} copy-done((bf16[448,2048]{1,0:T(8,128)(2,1)}, bf16[448,2048]{1,0:T(8,128)(2,1)S(1)}, u32[]{:S(2)}) %copy-start.4) | copy-done | bytes 1835032
  37.7 4.5 %collective-permute-start.10 = (bf16[392,2048]{1,0:T(8,128)(2,1)}, bf16[392,2048]{1,0:T(8,128)(2,1)S(1)}, u32[]{:S(2)}, u32[]{:S(2)}) collective-permute-start(bf16[392,2048]{1,0:T(8,128)(2,1)} %get-tuple-element.17), channel_id=1, source_target_pairs={{0,1},{1,0},{2,3},{3,2},{4,5},{5,4},{6,7},{7,6},{8,9},{9,8},{10,11... | collective-permute-start | bytes 4816904 | tf_op jit(solution)/shard_map/ppermute | solution.py:47
  42.4 8.3 %collective-permute-done.9 = bf16[56,2048]{1,0:T(8,128)(2,1)S(1)} collective-permute-done((bf16[56,2048]{1,0:T(8,128)(2,1)S(1)}, bf16[56,2048]{1,0:T(8,128)(2,1)S(1)}, u32[]{:S(2)}, u32[]{:S(2)}) %collective-permute-start.9) | collective-permute-done | bytes 229408 | tf_op jit(solution)/shard_map/ppermute | solution.py:47
  52.6 1.1 copy-done.5
  53.7 1.0 convolution_convert_fusion.1
  54.7 1.0 convolution_convert_fusion
  55.7 1.2 %copy-done.2 = bf16[384,2048]{1,0:T(8,128)(2,1)} copy-done((bf16[384,2048]{1,0:T(8,128)(2,1)}, bf16[384,2048]{1,0:T(8,128)(2,1)S(1)}, u32[]{:S(2)}) %copy-start.2) | copy-done | bytes 1572888
  57.5 1.3 %fusion.6 = f32[512,256]{0,1:T(8,128)S(1)} fusion(bf16[512,4096]{1,0:T(8,128)(2,1)S(1)} %bitcast.96, bf16[384,2048]{1,0:T(8,128)(2,1)S(1)} %convolution_convert_fusion, bf16[384,2048]{1,0:T(8,128)(2,1)S(1)} %convolution_convert_fusion.1), kind=kOutput, calls=%fused_computation.9 | convolution fusion | flops 1077936128 | bytes 7864320 | tf_op jit(solution)/shard_map/dot_general | solution.py:51
  59.4 3.0 %collective-permute-start.13 = (f32[2,128,256]{1,2,0:T(8,128)S(1)}, f32[2,128,256]{1,2,0:T(8,128)S(1)}, u32[]{:S(2)}, u32[]{:S(2)}) collective-permute-start(f32[2,128,256]{1,2,0:T(8,128)S(1)} %bitcast.88), channel_id=1, source_target_pairs={{0,4},{1,5},{2,6},{3,7},{4,0},{5,1},{6,2},{7,3},{8,12},{9,13},{10,... | collective-permute-start | bytes 786440 | tf_op jit(solution)/shard_map/ppermute | solution.py:47
  62.4 3.7 %convolution_bitcast_fusion = f32[512,128]{0,1:T(8,128)S(1)} fusion(bf16[512,4096]{1,0:T(8,128)(2,1)} %bitcast.83, bf16[384,2048]{1,0:T(8,128)(2,1)S(1)} %copy-done.3, bf16[384,2048]{1,0:T(8,128)(2,1)S(1)} %convolution_convert_fusion.1), kind=kOutput, calls=%fused_computation.10 | convolution fusion | flops 538968064 | bytes 7602176 | tf_op jit(solution)/shard_map/dot_general | solution.py:51
  66.3 1.2 %collective-permute-start.12 = (f32[2,128,128]{2,1,0:T(8,128)S(1)}, f32[2,128,128]{2,1,0:T(8,128)S(1)}, u32[]{:S(2)}, u32[]{:S(2)}) collective-permute-start(f32[2,128,128]{2,1,0:T(8,128)S(1)} %dynamic-slice_bitcast_fusion), channel_id=1, source_target_pairs={{0,4},{1,5},{2,6},{3,7},{4,0},{5,1},{6,2},{7,3},{8,12},{9,13},{10,... | collective-permute-start | bytes 393224 | tf_op jit(solution)/shard_map/ppermute | solution.py:47
  67.5 5.2 %collective-permute-done.12 = f32[2,128,128]{2,1,0:T(8,128)S(1)} collective-permute-done((f32[2,128,128]{2,1,0:T(8,128)S(1)}, f32[2,128,128]{2,1,0:T(8,128)S(1)}, u32[]{:S(2)}, u32[]{:S(2)}) %collective-permute-start.12) | collective-permute-done | bytes 131104 | tf_op jit(solution)/shard_map/ppermute | solution.py:47
  73.1 1.2 %collective-permute-start.14 = (f32[2,16,128]{2,1,0:T(8,128)S(1)}, f32[2,16,128]{2,1,0:T(8,128)S(1)}, u32[]{:S(2)}, u32[]{:S(2)}) collective-permute-start(f32[2,16,128]{2,1,0:T(8,128)S(1)} %get-tuple-element.37), channel_id=1, source_target_pairs={{0,1},{1,0},{2,3},{3,2},{4,5},{5,4},{6,7},{7,6},{8,9},{9,8},{10,11... | collective-permute-start | bytes 49160 | tf_op jit(solution)/shard_map/ppermute | solution.py:47
  74.7 1.3 %collective-permute-start.16 = (f32[2,16,128]{2,1,0:T(8,128)S(1)}, f32[2,16,128]{2,1,0:T(8,128)S(1)}, u32[]{:S(2)}, u32[]{:S(2)}) collective-permute-start(f32[2,16,128]{2,1,0:T(8,128)S(1)} %get-tuple-element.38), channel_id=1, source_target_pairs={{0,3},{1,2},{2,1},{3,0},{4,7},{5,6},{6,5},{7,4},{8,11},{9,10},{10,... | collective-permute-start | bytes 49160 | tf_op jit(solution)/shard_map/ppermute | solution.py:47
  76.9 1.0 collective-permute-done.16
  78.7 7.4 %all-to-all-start = ((bf16[32,2,2048]{2,1,0:T(2,128)(2,1)}), bf16[32,2,2048]{2,1,0:T(2,128)(2,1)S(1)}, u32[]{:S(2)}, u32[]{:S(2)}) async-start(bf16[32,2,2048]{2,1,0:T(2,128)(2,1)} %broadcast_in_dim.11), calls=%async_computation | async-start | bytes 524288 | tf_op jit(solution)/shard_map/all_to_all | solution.py:194
  86.1 11.5 %all-to-all-done = bf16[32,2,2048]{2,1,0:T(2,128)(2,1)S(1)} async-done(((bf16[32,2,2048]{2,1,0:T(2,128)(2,1)}), bf16[32,2,2048]{2,1,0:T(2,128)(2,1)S(1)}, u32[]{:S(2)}, u32[]{:S(2)}) %all-to-all-start) | async-done | bytes 262176 | tf_op jit(solution)/shard_map/all_to_all | solution.py:194
  98.6 2.4 %collective-permute-start.17 = (f32[2,24,256]{2,1,0:T(8,128)S(1)}, f32[2,24,256]{2,1,0:T(8,128)S(1)}, u32[]{:S(2)}, u32[]{:S(2)}) collective-permute-start(f32[2,24,256]{2,1,0:T(8,128)S(1)} %pad_maximum_fusion.6), channel_id=1, source_target_pairs={{0,1},{1,0},{2,3},{3,2},{4,5},{5,4},{6,7},{7,6},{8,9},{9,8},{10,11... | collective-permute-start | bytes 147464 | tf_op jit(solution)/shard_map/ppermute | solution.py:47
  101.9 1.1 %collective-permute-start.18 = (f32[24,256]{1,0:T(8,128)S(1)}, f32[24,256]{1,0:T(8,128)S(1)}, u32[]{:S(2)}, u32[]{:S(2)}) collective-permute-start(f32[24,256]{1,0:T(8,128)S(1)} %get-tuple-element.41), channel_id=1, source_target_pairs={{0,2},{1,3},{2,0},{3,1},{4,6},{5,7},{6,4},{7,5},{8,10},{9,11},{10,... | collective-permute-start | bytes 73736 | tf_op jit(solution)/shard_map/ppermute | solution.py:47
  103.0 1.4 %collective-permute-start.20 = (f32[24,256]{1,0:T(8,128)S(1)}, f32[24,256]{1,0:T(8,128)S(1)}, u32[]{:S(2)}, u32[]{:S(2)}) collective-permute-start(f32[24,256]{1,0:T(8,128)S(1)} %get-tuple-element.41), channel_id=1, source_target_pairs={{0,6},{1,7},{2,4},{3,5},{4,2},{5,3},{6,0},{7,1},{8,14},{9,15},{10,... | collective-permute-start | bytes 73736 | tf_op jit(solution)/shard_map/ppermute | solution.py:47
  105.3 3.4 %collective-permute-done.19 = f32[24,256]{1,0:T(8,128)S(1)} collective-permute-done((f32[24,256]{1,0:T(8,128)S(1)}, f32[24,256]{1,0:T(8,128)S(1)}, u32[]{:S(2)}, u32[]{:S(2)}) %collective-permute-start.19) | collective-permute-done | bytes 24608 | tf_op jit(solution)/shard_map/ppermute | solution.py:47
  (91 shorter events, 17.8 us)
Async XLA Ops:
  0.0 0.8 copy-start
  2.3 8.5 %collective-permute-start = (bf16[14,2048]{1,0:T(8,128)(2,1)S(1)}, bf16[14,2048]{1,0:T(8,128)(2,1)S(1)}, u32[]{:S(2)}, u32[]{:S(2)}) collective-permute-start(bf16[14,2048]{1,0:T(8,128)(2,1)S(1)} %pad_maximum_fusion.4), channel_id=1, source_target_pairs={{0,8},{1,9},{2,10},{3,11},{4,12},{5,13},{6,14},{7,15},{8,16},{9,17... | collective-permute-start | bytes 172040 | tf_op jit(solution)/shard_map/ppermute | solution.py:47
  4.4 6.3 %collective-permute-start.1 = (bf16[14,2048]{1,0:T(8,128)(2,1)S(1)}, bf16[14,2048]{1,0:T(8,128)(2,1)S(1)}, u32[]{:S(2)}, u32[]{:S(2)}) collective-permute-start(bf16[14,2048]{1,0:T(8,128)(2,1)S(1)} %pad_maximum_fusion.4), channel_id=1, source_target_pairs={{0,16},{1,17},{2,18},{3,19},{4,20},{5,21},{6,22},{7,23},{8,24},{9,... | collective-permute-start | bytes 172040 | tf_op jit(solution)/shard_map/ppermute | solution.py:47
  6.9 3.9 %collective-permute-start.2 = (bf16[14,2048]{1,0:T(8,128)(2,1)S(1)}, bf16[14,2048]{1,0:T(8,128)(2,1)S(1)}, u32[]{:S(2)}, u32[]{:S(2)}) collective-permute-start(bf16[14,2048]{1,0:T(8,128)(2,1)S(1)} %pad_maximum_fusion.4), channel_id=1, source_target_pairs={{0,24},{1,25},{2,26},{3,27},{4,28},{5,29},{6,30},{7,31},{8,0},{9,1... | collective-permute-start | bytes 172040 | tf_op jit(solution)/shard_map/ppermute | solution.py:47
  11.4 10.0 %collective-permute-start.3 = (bf16[56,2048]{1,0:T(8,128)(2,1)S(1)}, bf16[56,2048]{1,0:T(8,128)(2,1)S(1)}, u32[]{:S(2)}, u32[]{:S(2)}) collective-permute-start(bf16[56,2048]{1,0:T(8,128)(2,1)S(1)} %concatenate.31), channel_id=1, source_target_pairs={{0,32},{1,33},{2,34},{3,35},{4,36},{5,37},{6,38},{7,39},{8,40},{9,... | collective-permute-start | bytes 688136 | tf_op jit(solution)/shard_map/ppermute | solution.py:47
  13.1 8.3 %collective-permute-start.6 = (bf16[56,2048]{1,0:T(8,128)(2,1)S(1)}, bf16[56,2048]{1,0:T(8,128)(2,1)S(1)}, u32[]{:S(2)}, u32[]{:S(2)}) collective-permute-start(bf16[56,2048]{1,0:T(8,128)(2,1)S(1)} %concatenate.31), channel_id=1, source_target_pairs={{0,224},{1,225},{2,226},{3,227},{4,228},{5,229},{6,230},{7,231},{8... | collective-permute-start | bytes 688136 | tf_op jit(solution)/shard_map/ppermute | solution.py:47
  21.4 6.1 %collective-permute-start.4 = (bf16[56,2048]{1,0:T(8,128)(2,1)S(1)}, bf16[56,2048]{1,0:T(8,128)(2,1)S(1)}, u32[]{:S(2)}, u32[]{:S(2)}) collective-permute-start(bf16[56,2048]{1,0:T(8,128)(2,1)S(1)} %collective-permute-done.3), channel_id=1, source_target_pairs={{0,32},{1,33},{2,34},{3,35},{4,36},{5,37},{6,38},{7,39},{8,40},{9,... | collective-permute-start | bytes 688136 | tf_op jit(solution)/shard_map/ppermute | solution.py:47
  21.4 6.1 %collective-permute-start.7 = (bf16[56,2048]{1,0:T(8,128)(2,1)S(1)}, bf16[56,2048]{1,0:T(8,128)(2,1)S(1)}, u32[]{:S(2)}, u32[]{:S(2)}) collective-permute-start(bf16[56,2048]{1,0:T(8,128)(2,1)S(1)} %collective-permute-done.6), channel_id=1, source_target_pairs={{0,224},{1,225},{2,226},{3,227},{4,228},{5,229},{6,230},{7,231},{8... | collective-permute-start | bytes 688136 | tf_op jit(solution)/shard_map/ppermute | solution.py:47
  24.8 17.5 %copy-start.9 = (s32[4]{0:T(128)S(1)}, s32[4]{0:T(128)}, u32[]{:S(2)}) copy-start(s32[4]{0:T(128)} %param.12) | copy-start | bytes 52
  27.4 6.1 %collective-permute-start.5 = (bf16[56,2048]{1,0:T(8,128)(2,1)S(1)}, bf16[56,2048]{1,0:T(8,128)(2,1)S(1)}, u32[]{:S(2)}, u32[]{:S(2)}) collective-permute-start(bf16[56,2048]{1,0:T(8,128)(2,1)S(1)} %collective-permute-done.4), channel_id=1, source_target_pairs={{0,32},{1,33},{2,34},{3,35},{4,36},{5,37},{6,38},{7,39},{8,40},{9,... | collective-permute-start | bytes 688136 | tf_op jit(solution)/shard_map/ppermute | solution.py:47
  27.5 6.8 %collective-permute-start.8 = (bf16[56,2048]{1,0:T(8,128)(2,1)S(1)}, bf16[56,2048]{1,0:T(8,128)(2,1)S(1)}, u32[]{:S(2)}, u32[]{:S(2)}) collective-permute-start(bf16[56,2048]{1,0:T(8,128)(2,1)S(1)} %collective-permute-done.7), channel_id=1, source_target_pairs={{0,224},{1,225},{2,226},{3,227},{4,228},{5,229},{6,230},{7,231},{8... | collective-permute-start | bytes 688136 | tf_op jit(solution)/shard_map/ppermute | solution.py:47
  36.5 1.3 %copy-start.4 = (bf16[448,2048]{1,0:T(8,128)(2,1)}, bf16[448,2048]{1,0:T(8,128)(2,1)S(1)}, u32[]{:S(2)}) copy-start(bf16[448,2048]{1,0:T(8,128)(2,1)S(1)} %get-tuple-element.18) | copy-start | bytes 5505028
  37.7 14.5 %collective-permute-start.10 = (bf16[392,2048]{1,0:T(8,128)(2,1)}, bf16[392,2048]{1,0:T(8,128)(2,1)S(1)}, u32[]{:S(2)}, u32[]{:S(2)}) collective-permute-start(bf16[392,2048]{1,0:T(8,128)(2,1)} %get-tuple-element.17), channel_id=1, source_target_pairs={{0,1},{1,0},{2,3},{3,2},{4,5},{5,4},{6,7},{7,6},{8,9},{9,8},{10,11... | collective-permute-start | bytes 4816904 | tf_op jit(solution)/shard_map/ppermute | solution.py:47
  42.3 8.4 %collective-permute-start.9 = (bf16[56,2048]{1,0:T(8,128)(2,1)S(1)}, bf16[56,2048]{1,0:T(8,128)(2,1)S(1)}, u32[]{:S(2)}, u32[]{:S(2)}) collective-permute-start(bf16[56,2048]{1,0:T(8,128)(2,1)S(1)} %collective-permute-done.5), channel_id=1, source_target_pairs={{0,32},{1,33},{2,34},{3,35},{4,36},{5,37},{6,38},{7,39},{8,40},{9,... | collective-permute-start | bytes 688136 | tf_op jit(solution)/shard_map/ppermute | solution.py:47
  50.7 1.9 %collective-permute-start.11 = (bf16[56,2048]{1,0:T(8,128)(2,1)S(1)}, bf16[56,2048]{1,0:T(8,128)(2,1)S(1)}, u32[]{:S(2)}, u32[]{:S(2)}) collective-permute-start(bf16[56,2048]{1,0:T(8,128)(2,1)S(1)} %collective-permute-done.9), channel_id=1, source_target_pairs={{0,1},{1,0},{2,3},{3,2},{4,5},{5,4},{6,7},{7,6},{8,9},{9,8},{10,11... | collective-permute-start | bytes 688136 | tf_op jit(solution)/shard_map/ppermute | solution.py:47
  52.2 1.5 %copy-start.5 = (bf16[448,2048]{1,0:T(8,128)(2,1)S(1)}, bf16[448,2048]{1,0:T(8,128)(2,1)}, u32[]{:S(2)}) copy-start(bf16[448,2048]{1,0:T(8,128)(2,1)} %constant_dynamic-update-slice_fusion) | copy-start | bytes 5505028
  52.2 1.5 %copy-start.8 = (bf16[384,448]{1,0:T(8,128)(2,1)S(1)}, bf16[384,448]{1,0:T(8,128)(2,1)}, u32[]{:S(2)}) copy-start(bf16[384,448]{1,0:T(8,128)(2,1)} %get-tuple-element.12) | copy-start | bytes 1032196
  54.7 2.8 %copy-start.7 = (bf16[4,128,4096]{2,1,0:T(8,128)(2,1)S(1)}, bf16[4,128,4096]{2,1,0:T(8,128)(2,1)}, u32[]{:S(2)}) copy-start(bf16[4,128,4096]{2,1,0:T(8,128)(2,1)} %param.11) | copy-start | bytes 12582916
  55.7 1.2 %copy-start.2 = (bf16[384,2048]{1,0:T(8,128)(2,1)}, bf16[384,2048]{1,0:T(8,128)(2,1)S(1)}, u32[]{:S(2)}) copy-start(bf16[384,2048]{1,0:T(8,128)(2,1)S(1)} %convolution_convert_fusion) | copy-start | bytes 4718596
  59.1 3.2 %copy-start.3 = (bf16[384,2048]{1,0:T(8,128)(2,1)S(1)}, bf16[384,2048]{1,0:T(8,128)(2,1)}, u32[]{:S(2)}) copy-start(bf16[384,2048]{1,0:T(8,128)(2,1)} %copy-done.2) | copy-start | bytes 4718596
  59.4 13.5 %collective-permute-start.13 = (f32[2,128,256]{1,2,0:T(8,128)S(1)}, f32[2,128,256]{1,2,0:T(8,128)S(1)}, u32[]{:S(2)}, u32[]{:S(2)}) collective-permute-start(f32[2,128,256]{1,2,0:T(8,128)S(1)} %bitcast.88), channel_id=1, source_target_pairs={{0,4},{1,5},{2,6},{3,7},{4,0},{5,1},{6,2},{7,3},{8,12},{9,13},{10,... | collective-permute-start | bytes 786440 | tf_op jit(solution)/shard_map/ppermute | solution.py:47
  66.1 20.0 %copy-start.6 = (f32[8,128]{1,0:T(8,128)S(1)}, f32[8,128]{1,0:T(8,128)}, u32[]{:S(2)}) copy-start(f32[8,128]{1,0:T(8,128)} %get-tuple-element.14) | copy-start | bytes 12292
  66.1 31.7 %copy-start.1 = (bf16[128,2048]{1,0:T(8,128)(2,1)S(1)}, bf16[128,2048]{1,0:T(8,128)(2,1)}, u32[]{:S(2)}) copy-start(bf16[128,2048]{1,0:T(8,128)(2,1)} %queries_ref.1) | copy-start | bytes 1572868
  66.3 6.4 %collective-permute-start.12 = (f32[2,128,128]{2,1,0:T(8,128)S(1)}, f32[2,128,128]{2,1,0:T(8,128)S(1)}, u32[]{:S(2)}, u32[]{:S(2)}) collective-permute-start(f32[2,128,128]{2,1,0:T(8,128)S(1)} %dynamic-slice_bitcast_fusion), channel_id=1, source_target_pairs={{0,4},{1,5},{2,6},{3,7},{4,0},{5,1},{6,2},{7,3},{8,12},{9,13},{10,... | collective-permute-start | bytes 393224 | tf_op jit(solution)/shard_map/ppermute | solution.py:47
  73.1 2.9 %collective-permute-start.14 = (f32[2,16,128]{2,1,0:T(8,128)S(1)}, f32[2,16,128]{2,1,0:T(8,128)S(1)}, u32[]{:S(2)}, u32[]{:S(2)}) collective-permute-start(f32[2,16,128]{2,1,0:T(8,128)S(1)} %get-tuple-element.37), channel_id=1, source_target_pairs={{0,1},{1,0},{2,3},{3,2},{4,5},{5,4},{6,7},{7,6},{8,9},{9,8},{10,11... | collective-permute-start | bytes 49160 | tf_op jit(solution)/shard_map/ppermute | solution.py:47
  74.3 2.6 %collective-permute-start.15 = (f32[2,16,128]{2,1,0:T(8,128)S(1)}, f32[2,16,128]{2,1,0:T(8,128)S(1)}, u32[]{:S(2)}, u32[]{:S(2)}) collective-permute-start(f32[2,16,128]{2,1,0:T(8,128)S(1)} %get-tuple-element.39), channel_id=1, source_target_pairs={{0,2},{1,3},{2,0},{3,1},{4,6},{5,7},{6,4},{7,5},{8,10},{9,11},{10,... | collective-permute-start | bytes 49160 | tf_op jit(solution)/shard_map/ppermute | solution.py:47
  74.7 3.2 %collective-permute-start.16 = (f32[2,16,128]{2,1,0:T(8,128)S(1)}, f32[2,16,128]{2,1,0:T(8,128)S(1)}, u32[]{:S(2)}, u32[]{:S(2)}) collective-permute-start(f32[2,16,128]{2,1,0:T(8,128)S(1)} %get-tuple-element.38), channel_id=1, source_target_pairs={{0,3},{1,2},{2,1},{3,0},{4,7},{5,6},{6,5},{7,4},{8,11},{9,10},{10,... | collective-permute-start | bytes 49160 | tf_op jit(solution)/shard_map/ppermute | solution.py:47
  78.7 18.9 %all-to-all-start = ((bf16[32,2,2048]{2,1,0:T(2,128)(2,1)}), bf16[32,2,2048]{2,1,0:T(2,128)(2,1)S(1)}, u32[]{:S(2)}, u32[]{:S(2)}) async-start(bf16[32,2,2048]{2,1,0:T(2,128)(2,1)} %broadcast_in_dim.11), calls=%async_computation | async-start | bytes 524288 | tf_op jit(solution)/shard_map/all_to_all | solution.py:194
  98.6 3.3 %collective-permute-start.17 = (f32[2,24,256]{2,1,0:T(8,128)S(1)}, f32[2,24,256]{2,1,0:T(8,128)S(1)}, u32[]{:S(2)}, u32[]{:S(2)}) collective-permute-start(f32[2,24,256]{2,1,0:T(8,128)S(1)} %pad_maximum_fusion.6), channel_id=1, source_target_pairs={{0,1},{1,0},{2,3},{3,2},{4,5},{5,4},{6,7},{7,6},{8,9},{9,8},{10,11... | collective-permute-start | bytes 147464 | tf_op jit(solution)/shard_map/ppermute | solution.py:47
  101.9 3.3 %collective-permute-start.18 = (f32[24,256]{1,0:T(8,128)S(1)}, f32[24,256]{1,0:T(8,128)S(1)}, u32[]{:S(2)}, u32[]{:S(2)}) collective-permute-start(f32[24,256]{1,0:T(8,128)S(1)} %get-tuple-element.41), channel_id=1, source_target_pairs={{0,2},{1,3},{2,0},{3,1},{4,6},{5,7},{6,4},{7,5},{8,10},{9,11},{10,... | collective-permute-start | bytes 73736 | tf_op jit(solution)/shard_map/ppermute | solution.py:47
  103.0 5.6 %collective-permute-start.20 = (f32[24,256]{1,0:T(8,128)S(1)}, f32[24,256]{1,0:T(8,128)S(1)}, u32[]{:S(2)}, u32[]{:S(2)}) collective-permute-start(f32[24,256]{1,0:T(8,128)S(1)} %get-tuple-element.41), channel_id=1, source_target_pairs={{0,6},{1,7},{2,4},{3,5},{4,2},{5,3},{6,0},{7,1},{8,14},{9,15},{10,... | collective-permute-start | bytes 73736 | tf_op jit(solution)/shard_map/ppermute | solution.py:47
  104.5 4.2 %collective-permute-start.19 = (f32[24,256]{1,0:T(8,128)S(1)}, f32[24,256]{1,0:T(8,128)S(1)}, u32[]{:S(2)}, u32[]{:S(2)}) collective-permute-start(f32[24,256]{1,0:T(8,128)S(1)} %get-tuple-element.40), channel_id=1, source_target_pairs={{0,4},{1,5},{2,6},{3,7},{4,0},{5,1},{6,2},{7,3},{8,12},{9,13},{10,... | collective-permute-start | bytes 73736 | tf_op jit(solution)/shard_map/ppermute | solution.py:47

commit v6 on v4

--- a/solution.py
+++ b/solution.py
@@ -13,7 +13,7 @@
 AXES = ("demo", "fsdp", "sketch")
 Z, X, F, S = 8, 4, 2, 4
 ROWS = 14
-Z_BACK = (0, 1, 2, 6, 7, 3, 4, 5)
+Z_BACK = (0, 1, 2, 6, 7, 3, 5, 4)
 LEFT = 2 * PROBE_ROWS
 RIGHT = 2 * PROBE_COLUMNS
 LAST = ((1,), (1,))
@@ -36,7 +36,6 @@
 NEAR = pairs(lambda z, x, f, s: (z, x, f, s ^ 2))
 CORE_NEAR = pairs(lambda z, x, f, s: (z, x, f, s ^ 3))
 FAR = pairs(lambda z, x, f, s: (z, x, f ^ 1, s))
-FAR_NEAR = pairs(lambda z, x, f, s: (z, x, f ^ 1, s ^ 2))
 
 
 def shift(dz, dx):
@@ -146,14 +145,15 @@
     line = jnp.concatenate([block] + [send(block, shift(0, k)) for k in range(1, X)])
     line, weights, query_squares = lax.optimization_barrier((line, weights, query_squares))
     up, down = [line], [line]
-    for k in range(1, Z // 2 + 1):
+    for k in range(1, Z // 2):
         up.append(send(up[-1], shift(1, 0)))
-        if k < Z // 2:
-            down.append(send(down[-1], shift(-1, 0)))
+        down.append(send(down[-1], shift(-1, 0)))
         if k == 2:
             early = jnp.concatenate([up[0], up[1], up[2], down[2], down[1]])
             other_early = send(early, CORE)
-    late = jnp.concatenate([up[3], up[4], down[3]])
+    cut = 32
+    farthest = [send(up[3][:cut], shift(1, 0)), send(down[3][cut:], shift(-1, 0))]
+    late = jnp.concatenate([up[3], down[3], *farthest])
     other_late = send(late, CORE)
     rows = jnp.concatenate([early, late])
     other = jnp.concatenate([other_early, other_late])
@@ -169,8 +169,7 @@
     left_map, right_map = maps[:LEFT], maps[LEFT:]
     right = dot(cotangents.reshape(tokens, feat), right_map, LAST)
     right = right.reshape(F, own, tok_local, RIGHT)
-    give_right, left_map = lax.optimization_barrier((pick(right, 1 - f), left_map))
-    right_sum = pick(right, f) + send(give_right, FAR)
+    right_sum = pick(right, f) + send(pick(right, 1 - f), FAR)
     left = dot(activations.reshape(tokens, feat), left_map, LAST)
     left = left.reshape(F, own, tok_local, LEFT)
     left_sum = pick(left, f) + send(pick(left, 1 - f), FAR)
@@ -205,10 +204,11 @@
     keep = jnp.stack([pick(both, s), pick(both, s ^ 2)])
     give = jnp.stack([pick(both, s ^ 1), pick(both, s ^ 3)])
     pair = keep + send(give, CORE)
-    here = pair[0] + send(pair[1], NEAR)
-    there = send(pair[0], FAR) + send(pair[1], FAR_NEAR)
-    query_total = here[block_rows : block_rows + 1, :nq]
-    here, there = here[:block_rows], there[:block_rows]
+    far = send(pair, FAR)
+    wide = jnp.concatenate([pair, far[:, :block_rows]], axis=1)
+    wide = wide[0] + send(wide[1], NEAR)
+    query_total = wide[block_rows : block_rows + 1, :nq]
+    here, there = wide[:block_rows], wide[block_rows + 8 :]
     total = jnp.stack([jnp.where(f == 0, here, there), jnp.where(f == 0, there, here)])
     total = total.reshape(F, block_rows // own, own, 2 * nq).transpose(1, 0, 2, 3)
     total = total.reshape(F * block_rows, 2 * nq)

time: 107 us -> 110 us (1.028)
  local copies, waits for them, and re-layouts: 8.17 us -> 9.89 us
  starting transfers between devices: 46.7 us -> 45.1 us
  matrix products: 7.44 us -> 8.93 us
    ppermute x21, starting transfers between devices: 40.1 us -> 38 us  [send(): return lax.ppermute(value, AXES, moves)]
    dot_general x3, matrix products: 5.3 us -> 6.79 us  [dot(): lax.dot_general(a, b, (contract, ((), ())), preferred_element_type=jnp.fl...]
    all_to_all x1, waiting for transfers between devices: 10.4 us -> 11.5 us  [shards(): lax.all_to_all(copies, 'demo', 0, 0).reshape(Z * X * own, K // S)]
    unnamed x18 -> x19, local copies, waits for them, and re-layouts: 3.16 us -> 2.24 us
  transfers between devices with their start and end apart: 22 -> 22, of which waited for: 12 -> 11; matrix products, arithmetic and copies ran while one was open for 2% -> 8% of each run, Pallas kernels for 2% -> 2%
where the time goes in v6:
time: 110 us; the launch traced here: 109 us
  starting transfers between devices  45.1 us (41%)
  waiting for transfers between devices  40.3 us (37%)
  local copies, waits for them, and re-layouts  9.89 us (9%)
  matrix products  8.93 us (8%)
  other arithmetic  2.57 us (2%)
  Pallas kernels  2.13 us (2%)
    ppermute x21, starting transfers between devices, send(): return lax.ppermute(value, AXES, moves)  38 us
    ppermute x21, waiting for transfers between devices, send(): return lax.ppermute(value, AXES, moves)  28.8 us
    all_to_all x1, waiting for transfers between devices, shards(): lax.all_to_all(copies, 'demo', 0, 0).reshape(Z * X * own, K // S)  11.5 us
    all_to_all x1, starting transfers between devices, shards(): lax.all_to_all(copies, 'demo', 0, 0).reshape(Z * X * own, K // S)  7.16 us
    dot_general x3, matrix products, dot(): lax.dot_general(a, b, (contract, ((), ())), preferred_element_type=jnp.fl...  6.79 us
    unnamed x19, local copies, waits for them, and re-layouts  2.24 us
  transfers between devices with their start and end apart: 22, of which 11 were waited for; matrix products, arithmetic and copies ran while one was open for 8% of the time, Pallas kernels for 2%

profile of v6, /device:TPU:1, one launch (start us, length us, event | category | flops | bytes accessed | tf_op | source)
XLA Modules:
  0.0 109.4 jit_solution(13485987777246149752)
XLA Ops:
  2.3 2.1 %collective-permute-start = (bf16[14,2048]{1,0:T(8,128)(2,1)S(1)}, bf16[14,2048]{1,0:T(8,128)(2,1)S(1)}, u32[]{:S(2)}, u32[]{:S(2)}) collective-permute-start(bf16[14,2048]{1,0:T(8,128)(2,1)S(1)} %pad_maximum_fusion.5), channel_id=1, source_target_pairs={{0,8},{1,9},{2,10},{3,11},{4,12},{5,13},{6,14},{7,15},{8,16},{9,17... | collective-permute-start | bytes 172040 | tf_op jit(solution)/shard_map/ppermute | solution.py:46
  4.4 2.5 %collective-permute-start.1 = (bf16[14,2048]{1,0:T(8,128)(2,1)S(1)}, bf16[14,2048]{1,0:T(8,128)(2,1)S(1)}, u32[]{:S(2)}, u32[]{:S(2)}) collective-permute-start(bf16[14,2048]{1,0:T(8,128)(2,1)S(1)} %pad_maximum_fusion.5), channel_id=1, source_target_pairs={{0,16},{1,17},{2,18},{3,19},{4,20},{5,21},{6,22},{7,23},{8,24},{9,... | collective-permute-start | bytes 172040 | tf_op jit(solution)/shard_map/ppermute | solution.py:46
  6.9 1.2 %collective-permute-start.2 = (bf16[14,2048]{1,0:T(8,128)(2,1)S(1)}, bf16[14,2048]{1,0:T(8,128)(2,1)S(1)}, u32[]{:S(2)}, u32[]{:S(2)}) collective-permute-start(bf16[14,2048]{1,0:T(8,128)(2,1)S(1)} %pad_maximum_fusion.5), channel_id=1, source_target_pairs={{0,24},{1,25},{2,26},{3,27},{4,28},{5,29},{6,30},{7,31},{8,0},{9,1... | collective-permute-start | bytes 172040 | tf_op jit(solution)/shard_map/ppermute | solution.py:46
  9.3 2.1 %shard_map.100 = (bf16[384,448]{1,0:T(8,128)(2,1)}, f32[8,128]{1,0:T(8,128)}) custom-call(s32[2]{0:T(128)} %pad_add_fusion.info_ref, bf16[128,128]{1,0:T(8,128)(2,1)} %contracting_ref.1, bf16[64,128]{1,0:T(8,128)(2,1)} %bitcast.95, bf16[128,2048]{1,0:T(8,128)(2,1)} %queries_ref.1), custom_call_target="tpu_custom_call" | custom-call | flops 100000000 | bytes 1000000 | tf_op jit(solution)/shard_map/pallas_call | solution.py:132
  12.1 1.7 %collective-permute-start.3 = (bf16[56,2048]{1,0:T(8,128)(2,1)S(1)}, bf16[56,2048]{1,0:T(8,128)(2,1)S(1)}, u32[]{:S(2)}, u32[]{:S(2)}) collective-permute-start(bf16[56,2048]{1,0:T(8,128)(2,1)S(1)} %concatenate.37), channel_id=1, source_target_pairs={{0,32},{1,33},{2,34},{3,35},{4,36},{5,37},{6,38},{7,39},{8,40},{9,... | collective-permute-start | bytes 688136 | tf_op jit(solution)/shard_map/ppermute | solution.py:46
  13.8 4.0 %collective-permute-start.5 = (bf16[56,2048]{1,0:T(8,128)(2,1)S(1)}, bf16[56,2048]{1,0:T(8,128)(2,1)S(1)}, u32[]{:S(2)}, u32[]{:S(2)}) collective-permute-start(bf16[56,2048]{1,0:T(8,128)(2,1)S(1)} %concatenate.37), channel_id=1, source_target_pairs={{0,224},{1,225},{2,226},{3,227},{4,228},{5,229},{6,230},{7,231},{8... | collective-permute-start | bytes 688136 | tf_op jit(solution)/shard_map/ppermute | solution.py:46
  17.9 4.3 %collective-permute-done.3 = bf16[56,2048]{1,0:T(8,128)(2,1)S(1)} collective-permute-done((bf16[56,2048]{1,0:T(8,128)(2,1)S(1)}, bf16[56,2048]{1,0:T(8,128)(2,1)S(1)}, u32[]{:S(2)}, u32[]{:S(2)}) %collective-permute-start.3) | collective-permute-done | bytes 229408 | tf_op jit(solution)/shard_map/ppermute | solution.py:46
  22.1 2.7 %collective-permute-start.6 = (bf16[56,2048]{1,0:T(8,128)(2,1)S(1)}, bf16[56,2048]{1,0:T(8,128)(2,1)S(1)}, u32[]{:S(2)}, u32[]{:S(2)}) collective-permute-start(bf16[56,2048]{1,0:T(8,128)(2,1)S(1)} %collective-permute-done.5), channel_id=1, source_target_pairs={{0,224},{1,225},{2,226},{3,227},{4,228},{5,229},{6,230},{7,231},{8... | collective-permute-start | bytes 688136 | tf_op jit(solution)/shard_map/ppermute | solution.py:46
  24.9 3.4 %collective-permute-done.4 = bf16[56,2048]{1,0:T(8,128)(2,1)S(1)} collective-permute-done((bf16[56,2048]{1,0:T(8,128)(2,1)S(1)}, bf16[56,2048]{1,0:T(8,128)(2,1)S(1)}, u32[]{:S(2)}, u32[]{:S(2)}) %collective-permute-start.4) | collective-permute-done | bytes 229408 | tf_op jit(solution)/shard_map/ppermute | solution.py:46
  28.2 2.7 %collective-permute-start.8 = (bf16[56,2048]{1,0:T(8,128)(2,1)S(1)}, bf16[56,2048]{1,0:T(8,128)(2,1)S(1)}, u32[]{:S(2)}, u32[]{:S(2)}) collective-permute-start(bf16[56,2048]{1,0:T(8,128)(2,1)S(1)} %collective-permute-done.6), channel_id=1, source_target_pairs={{0,224},{1,225},{2,226},{3,227},{4,228},{5,229},{6,230},{7,231},{8... | collective-permute-start | bytes 688136 | tf_op jit(solution)/shard_map/ppermute | solution.py:46
  31.0 4.0 %collective-permute-start.11 = (bf16[280,2048]{1,0:T(8,128)(2,1)S(1)}, bf16[280,2048]{1,0:T(8,128)(2,1)S(1)}, u32[]{:S(2)}, u32[]{:S(2)}) collective-permute-start(bf16[280,2048]{1,0:T(8,128)(2,1)S(1)} %get-tuple-element.17), channel_id=1, source_target_pairs={{0,1},{1,0},{2,3},{3,2},{4,5},{5,4},{6,7},{7,6},{8,9},{9,8},{10,11... | collective-permute-start | bytes 3440648 | tf_op jit(solution)/shard_map/ppermute | solution.py:46
  35.1 2.7 %collective-permute-start.10 = (bf16[24,2048]{1,0:T(8,128)(2,1)S(1)}, bf16[24,2048]{1,0:T(8,128)(2,1)S(1)}, u32[]{:S(2)}, u32[]{:S(2)}) collective-permute-start(bf16[24,2048]{1,0:T(8,128)(2,1)S(1)} %slice.49), channel_id=1, source_target_pairs={{0,224},{1,225},{2,226},{3,227},{4,228},{5,229},{6,230},{7,231},{8... | collective-permute-start | bytes 294920 | tf_op jit(solution)/shard_map/ppermute | solution.py:46
  37.9 1.6 %collective-permute-done.10 = bf16[24,2048]{1,0:T(8,128)(2,1)S(1)} collective-permute-done((bf16[24,2048]{1,0:T(8,128)(2,1)S(1)}, bf16[24,2048]{1,0:T(8,128)(2,1)S(1)}, u32[]{:S(2)}, u32[]{:S(2)}) %collective-permute-start.10) | collective-permute-done | bytes 98336 | tf_op jit(solution)/shard_map/ppermute | solution.py:46
  40.2 5.2 %collective-permute-start.12 = (bf16[168,2048]{1,0:T(8,128)(2,1)S(1)}, bf16[168,2048]{1,0:T(8,128)(2,1)S(1)}, u32[]{:S(2)}, u32[]{:S(2)}) collective-permute-start(bf16[168,2048]{1,0:T(8,128)(2,1)S(1)} %pad_maximum_fusion.4), channel_id=1, source_target_pairs={{0,1},{1,0},{2,3},{3,2},{4,5},{5,4},{6,7},{7,6},{8,9},{9,8},{10,11... | collective-permute-start | bytes 2064392 | tf_op jit(solution)/shard_map/ppermute | solution.py:46
  45.5 1.6 %collective-permute-done.12 = bf16[168,2048]{1,0:T(8,128)(2,1)S(1)} collective-permute-done((bf16[168,2048]{1,0:T(8,128)(2,1)S(1)}, bf16[168,2048]{1,0:T(8,128)(2,1)S(1)}, u32[]{:S(2)}, u32[]{:S(2)}) %collective-permute-start.12) | collective-permute-done | bytes 688160 | tf_op jit(solution)/shard_map/ppermute | solution.py:46
  47.2 1.0 convolution_convert_fusion
  48.2 1.0 convolution_convert_fusion.1
  49.2 1.2 %copy-done.1 = bf16[4,128,4096]{2,1,0:T(8,128)(2,1)S(1)} copy-done((bf16[4,128,4096]{2,1,0:T(8,128)(2,1)S(1)}, bf16[4,128,4096]{2,1,0:T(8,128)(2,1)}, u32[]{:S(2)}) %copy-start.1) | copy-done | bytes 4194328
  50.4 2.2 %convolution_bitcast_fusion = f32[512,128]{0,1:T(8,128)} fusion(bf16[512,4096]{1,0:T(8,128)(2,1)S(1)} %bitcast.83, bf16[384,2048]{1,0:T(8,128)(2,1)S(1)} %convolution_convert_fusion, bf16[384,2048]{1,0:T(8,128)(2,1)S(1)} %convolution_convert_fusion.1), kind=kOutput, calls=%fused_computation.10 | convolution fusion | flops 538968064 | bytes 7602176 | tf_op jit(solution)/shard_map/dot_general | solution.py:50
  52.6 1.1 copy.70
  54.4 2.9 %collective-permute-start.13 = (f32[2,128,128]{2,1,0:T(8,128)}, f32[2,128,128]{2,1,0:T(8,128)}, u32[]{:S(2)}, u32[]{:S(2)}) collective-permute-start(f32[2,128,128]{2,1,0:T(8,128)} %dynamic-slice_bitcast_fusion), channel_id=1, source_target_pairs={{0,4},{1,5},{2,6},{3,7},{4,0},{5,1},{6,2},{7,3},{8,12},{9,13},{10,... | collective-permute-start | bytes 393224 | tf_op jit(solution)/shard_map/ppermute | solution.py:46
  57.3 4.3 %fusion.6 = f32[512,256]{0,1:T(8,128)} fusion(bf16[512,4096]{1,0:T(8,128)(2,1)} %bitcast.96, bf16[384,2048]{1,0:T(8,128)(2,1)S(1)} %convolution_convert_fusion, bf16[384,2048]{1,0:T(8,128)(2,1)S(1)} %convolution_convert_fusion.1), kind=kOutput, calls=%fused_computation.9 | convolution fusion | flops 1077936128 | bytes 7864320 | tf_op jit(solution)/shard_map/dot_general | solution.py:50
  61.6 1.4 %reshape.84 = f32[2,2,128,256]{2,1,0,3:T(2,128)S(1)} reshape(f32[512,256]{0,1:T(8,128)} %fusion.6) | data formatting | bytes 1048576 | tf_op jit(solution)/shard_map/reshape | solution.py:171
  63.4 0.9 fusion.12
  64.4 7.5 %collective-permute-done.14 = f32[2,128,256]{1,2,0:T(8,128)S(1)} collective-permute-done((f32[2,128,256]{1,2,0:T(8,128)S(1)}, f32[2,128,256]{1,2,0:T(8,128)S(1)}, u32[]{:S(2)}, u32[]{:S(2)}) %collective-permute-start.14) | collective-permute-done | bytes 262176 | tf_op jit(solution)/shard_map/ppermute | solution.py:46
  72.7 2.8 %collective-permute-start.17 = (f32[2,16,128]{2,1,0:T(8,128)S(1)}, f32[2,16,128]{2,1,0:T(8,128)S(1)}, u32[]{:S(2)}, u32[]{:S(2)}) collective-permute-start(f32[2,16,128]{2,1,0:T(8,128)S(1)} %get-tuple-element.32), channel_id=1, source_target_pairs={{0,3},{1,2},{2,1},{3,0},{4,7},{5,6},{6,5},{7,4},{8,11},{9,10},{10,... | collective-permute-start | bytes 49160 | tf_op jit(solution)/shard_map/ppermute | solution.py:46
  75.4 2.0 %collective-permute-done.17 = f32[2,16,128]{2,1,0:T(8,128)S(1)} collective-permute-done((f32[2,16,128]{2,1,0:T(8,128)S(1)}, f32[2,16,128]{2,1,0:T(8,128)S(1)}, u32[]{:S(2)}, u32[]{:S(2)}) %collective-permute-start.17) | collective-permute-done | bytes 16416 | tf_op jit(solution)/shard_map/ppermute | solution.py:46
  78.3 7.2 %all-to-all-start = ((bf16[32,2,2048]{2,1,0:T(2,128)(2,1)}), bf16[32,2,2048]{2,1,0:T(2,128)(2,1)S(1)}, u32[]{:S(2)}, u32[]{:S(2)}) async-start(bf16[32,2,2048]{2,1,0:T(2,128)(2,1)} %broadcast_in_dim.11), calls=%async_computation | async-start | bytes 524288 | tf_op jit(solution)/shard_map/all_to_all | solution.py:195
  85.5 11.5 %all-to-all-done = bf16[32,2,2048]{2,1,0:T(2,128)(2,1)S(1)} async-done(((bf16[32,2,2048]{2,1,0:T(2,128)(2,1)}), bf16[32,2,2048]{2,1,0:T(2,128)(2,1)S(1)}, u32[]{:S(2)}, u32[]{:S(2)}) %all-to-all-start) | async-done | bytes 262176 | tf_op jit(solution)/shard_map/all_to_all | solution.py:195
  97.9 2.4 %collective-permute-start.18 = (f32[2,24,256]{2,1,0:T(8,128)S(1)}, f32[2,24,256]{2,1,0:T(8,128)S(1)}, u32[]{:S(2)}, u32[]{:S(2)}) collective-permute-start(f32[2,24,256]{2,1,0:T(8,128)S(1)} %pad_maximum_fusion.7), channel_id=1, source_target_pairs={{0,1},{1,0},{2,3},{3,2},{4,5},{5,4},{6,7},{7,6},{8,9},{9,8},{10,11... | collective-permute-start | bytes 147464 | tf_op jit(solution)/shard_map/ppermute | solution.py:46
  101.5 4.2 %collective-permute-done.19 = f32[2,24,256]{2,1,0:T(8,128)S(1)} collective-permute-done((f32[2,24,256]{2,1,0:T(8,128)S(1)}, f32[2,24,256]{2,1,0:T(8,128)S(1)}, u32[]{:S(2)}, u32[]{:S(2)}) %collective-permute-start.19) | collective-permute-done | bytes 49184 | tf_op jit(solution)/shard_map/ppermute | solution.py:46
  105.9 2.7 %collective-permute-done.20 = f32[40,256]{1,0:T(8,128)S(1)} collective-permute-done((f32[40,256]{1,0:T(8,128)S(1)}, f32[40,256]{1,0:T(8,128)S(1)}, u32[]{:S(2)}, u32[]{:S(2)}) %collective-permute-start.20) | collective-permute-done | bytes 40992 | tf_op jit(solution)/shard_map/ppermute | solution.py:46
  (86 shorter events, 11.1 us)
Async XLA Ops:
  0.0 0.8 copy-start
  2.3 9.2 %collective-permute-start = (bf16[14,2048]{1,0:T(8,128)(2,1)S(1)}, bf16[14,2048]{1,0:T(8,128)(2,1)S(1)}, u32[]{:S(2)}, u32[]{:S(2)}) collective-permute-start(bf16[14,2048]{1,0:T(8,128)(2,1)S(1)} %pad_maximum_fusion.5), channel_id=1, source_target_pairs={{0,8},{1,9},{2,10},{3,11},{4,12},{5,13},{6,14},{7,15},{8,16},{9,17... | collective-permute-start | bytes 172040 | tf_op jit(solution)/shard_map/ppermute | solution.py:46
  4.4 7.0 %collective-permute-start.1 = (bf16[14,2048]{1,0:T(8,128)(2,1)S(1)}, bf16[14,2048]{1,0:T(8,128)(2,1)S(1)}, u32[]{:S(2)}, u32[]{:S(2)}) collective-permute-start(bf16[14,2048]{1,0:T(8,128)(2,1)S(1)} %pad_maximum_fusion.5), channel_id=1, source_target_pairs={{0,16},{1,17},{2,18},{3,19},{4,20},{5,21},{6,22},{7,23},{8,24},{9,... | collective-permute-start | bytes 172040 | tf_op jit(solution)/shard_map/ppermute | solution.py:46
  6.9 4.6 %collective-permute-start.2 = (bf16[14,2048]{1,0:T(8,128)(2,1)S(1)}, bf16[14,2048]{1,0:T(8,128)(2,1)S(1)}, u32[]{:S(2)}, u32[]{:S(2)}) collective-permute-start(bf16[14,2048]{1,0:T(8,128)(2,1)S(1)} %pad_maximum_fusion.5), channel_id=1, source_target_pairs={{0,24},{1,25},{2,26},{3,27},{4,28},{5,29},{6,30},{7,31},{8,0},{9,1... | collective-permute-start | bytes 172040 | tf_op jit(solution)/shard_map/ppermute | solution.py:46
  12.1 10.1 %collective-permute-start.3 = (bf16[56,2048]{1,0:T(8,128)(2,1)S(1)}, bf16[56,2048]{1,0:T(8,128)(2,1)S(1)}, u32[]{:S(2)}, u32[]{:S(2)}) collective-permute-start(bf16[56,2048]{1,0:T(8,128)(2,1)S(1)} %concatenate.37), channel_id=1, source_target_pairs={{0,32},{1,33},{2,34},{3,35},{4,36},{5,37},{6,38},{7,39},{8,40},{9,... | collective-permute-start | bytes 688136 | tf_op jit(solution)/shard_map/ppermute | solution.py:46
  13.8 8.3 %collective-permute-start.5 = (bf16[56,2048]{1,0:T(8,128)(2,1)S(1)}, bf16[56,2048]{1,0:T(8,128)(2,1)S(1)}, u32[]{:S(2)}, u32[]{:S(2)}) collective-permute-start(bf16[56,2048]{1,0:T(8,128)(2,1)S(1)} %concatenate.37), channel_id=1, source_target_pairs={{0,224},{1,225},{2,226},{3,227},{4,228},{5,229},{6,230},{7,231},{8... | collective-permute-start | bytes 688136 | tf_op jit(solution)/shard_map/ppermute | solution.py:46
  22.1 6.1 %collective-permute-start.4 = (bf16[56,2048]{1,0:T(8,128)(2,1)S(1)}, bf16[56,2048]{1,0:T(8,128)(2,1)S(1)}, u32[]{:S(2)}, u32[]{:S(2)}) collective-permute-start(bf16[56,2048]{1,0:T(8,128)(2,1)S(1)} %collective-permute-done.3), channel_id=1, source_target_pairs={{0,32},{1,33},{2,34},{3,35},{4,36},{5,37},{6,38},{7,39},{8,40},{9,... | collective-permute-start | bytes 688136 | tf_op jit(solution)/shard_map/ppermute | solution.py:46
  22.1 6.1 %collective-permute-start.6 = (bf16[56,2048]{1,0:T(8,128)(2,1)S(1)}, bf16[56,2048]{1,0:T(8,128)(2,1)S(1)}, u32[]{:S(2)}, u32[]{:S(2)}) collective-permute-start(bf16[56,2048]{1,0:T(8,128)(2,1)S(1)} %collective-permute-done.5), channel_id=1, source_target_pairs={{0,224},{1,225},{2,226},{3,227},{4,228},{5,229},{6,230},{7,231},{8... | collective-permute-start | bytes 688136 | tf_op jit(solution)/shard_map/ppermute | solution.py:46
  28.2 6.8 %collective-permute-start.7 = (bf16[56,2048]{1,0:T(8,128)(2,1)S(1)}, bf16[56,2048]{1,0:T(8,128)(2,1)S(1)}, u32[]{:S(2)}, u32[]{:S(2)}) collective-permute-start(bf16[56,2048]{1,0:T(8,128)(2,1)S(1)} %collective-permute-done.4), channel_id=1, source_target_pairs={{0,32},{1,33},{2,34},{3,35},{4,36},{5,37},{6,38},{7,39},{8,40},{9,... | collective-permute-start | bytes 688136 | tf_op jit(solution)/shard_map/ppermute | solution.py:46
  28.2 6.9 %collective-permute-start.8 = (bf16[56,2048]{1,0:T(8,128)(2,1)S(1)}, bf16[56,2048]{1,0:T(8,128)(2,1)S(1)}, u32[]{:S(2)}, u32[]{:S(2)}) collective-permute-start(bf16[56,2048]{1,0:T(8,128)(2,1)S(1)} %collective-permute-done.6), channel_id=1, source_target_pairs={{0,224},{1,225},{2,226},{3,227},{4,228},{5,229},{6,230},{7,231},{8... | collective-permute-start | bytes 688136 | tf_op jit(solution)/shard_map/ppermute | solution.py:46
  31.0 14.4 %collective-permute-start.11 = (bf16[280,2048]{1,0:T(8,128)(2,1)S(1)}, bf16[280,2048]{1,0:T(8,128)(2,1)S(1)}, u32[]{:S(2)}, u32[]{:S(2)}) collective-permute-start(bf16[280,2048]{1,0:T(8,128)(2,1)S(1)} %get-tuple-element.17), channel_id=1, source_target_pairs={{0,1},{1,0},{2,3},{3,2},{4,5},{5,4},{6,7},{7,6},{8,9},{9,8},{10,11... | collective-permute-start | bytes 3440648 | tf_op jit(solution)/shard_map/ppermute | solution.py:46
  35.0 5.1 %collective-permute-start.9 = (bf16[32,2048]{1,0:T(8,128)(2,1)S(1)}, bf16[32,2048]{1,0:T(8,128)(2,1)S(1)}, u32[]{:S(2)}, u32[]{:S(2)}) collective-permute-start(bf16[32,2048]{1,0:T(8,128)(2,1)S(1)} %slice.48), channel_id=1, source_target_pairs={{0,32},{1,33},{2,34},{3,35},{4,36},{5,37},{6,38},{7,39},{8,40},{9,... | collective-permute-start | bytes 393224 | tf_op jit(solution)/shard_map/ppermute | solution.py:46
  35.1 4.4 %collective-permute-start.10 = (bf16[24,2048]{1,0:T(8,128)(2,1)S(1)}, bf16[24,2048]{1,0:T(8,128)(2,1)S(1)}, u32[]{:S(2)}, u32[]{:S(2)}) collective-permute-start(bf16[24,2048]{1,0:T(8,128)(2,1)S(1)} %slice.49), channel_id=1, source_target_pairs={{0,224},{1,225},{2,226},{3,227},{4,228},{5,229},{6,230},{7,231},{8... | collective-permute-start | bytes 294920 | tf_op jit(solution)/shard_map/ppermute | solution.py:46
  40.2 7.0 %collective-permute-start.12 = (bf16[168,2048]{1,0:T(8,128)(2,1)S(1)}, bf16[168,2048]{1,0:T(8,128)(2,1)S(1)}, u32[]{:S(2)}, u32[]{:S(2)}) collective-permute-start(bf16[168,2048]{1,0:T(8,128)(2,1)S(1)} %pad_maximum_fusion.4), channel_id=1, source_target_pairs={{0,1},{1,0},{2,3},{3,2},{4,5},{5,4},{6,7},{7,6},{8,9},{9,8},{10,11... | collective-permute-start | bytes 2064392 | tf_op jit(solution)/shard_map/ppermute | solution.py:46
  45.4 1.8 %copy-start.4 = (bf16[384,448]{1,0:T(8,128)(2,1)S(1)}, bf16[384,448]{1,0:T(8,128)(2,1)}, u32[]{:S(2)}) copy-start(bf16[384,448]{1,0:T(8,128)(2,1)} %get-tuple-element.12) | copy-start | bytes 1032196
  48.2 2.2 %copy-start.1 = (bf16[4,128,4096]{2,1,0:T(8,128)(2,1)S(1)}, bf16[4,128,4096]{2,1,0:T(8,128)(2,1)}, u32[]{:S(2)}) copy-start(bf16[4,128,4096]{2,1,0:T(8,128)(2,1)} %param.10) | copy-start | bytes 12582916
  54.4 9.0 %collective-permute-start.13 = (f32[2,128,128]{2,1,0:T(8,128)}, f32[2,128,128]{2,1,0:T(8,128)}, u32[]{:S(2)}, u32[]{:S(2)}) collective-permute-start(f32[2,128,128]{2,1,0:T(8,128)} %dynamic-slice_bitcast_fusion), channel_id=1, source_target_pairs={{0,4},{1,5},{2,6},{3,7},{4,0},{5,1},{6,2},{7,3},{8,12},{9,13},{10,... | collective-permute-start | bytes 393224 | tf_op jit(solution)/shard_map/ppermute | solution.py:46
  62.9 22.5 %copy-start.3 = (f32[8,128]{1,0:T(8,128)S(1)}, f32[8,128]{1,0:T(8,128)}, u32[]{:S(2)}) copy-start(f32[8,128]{1,0:T(8,128)} %get-tuple-element.14) | copy-start | bytes 12292
  63.1 34.3 %copy-start.2 = (bf16[128,2048]{1,0:T(8,128)(2,1)S(1)}, bf16[128,2048]{1,0:T(8,128)(2,1)}, u32[]{:S(2)}) copy-start(bf16[128,2048]{1,0:T(8,128)(2,1)} %queries_ref.1) | copy-start | bytes 1572868
  63.2 8.8 %collective-permute-start.14 = (f32[2,128,256]{1,2,0:T(8,128)S(1)}, f32[2,128,256]{1,2,0:T(8,128)S(1)}, u32[]{:S(2)}, u32[]{:S(2)}) collective-permute-start(f32[2,128,256]{1,2,0:T(8,128)S(1)} %bitcast.88), channel_id=1, source_target_pairs={{0,4},{1,5},{2,6},{3,7},{4,0},{5,1},{6,2},{7,3},{8,12},{9,13},{10,... | collective-permute-start | bytes 786440 | tf_op jit(solution)/shard_map/ppermute | solution.py:46
  72.2 3.2 %collective-permute-start.16 = (f32[2,16,128]{2,1,0:T(8,128)S(1)}, f32[2,16,128]{2,1,0:T(8,128)S(1)}, u32[]{:S(2)}, u32[]{:S(2)}) collective-permute-start(f32[2,16,128]{2,1,0:T(8,128)S(1)} %get-tuple-element.33), channel_id=1, source_target_pairs={{0,2},{1,3},{2,0},{3,1},{4,6},{5,7},{6,4},{7,5},{8,10},{9,11},{10,... | collective-permute-start | bytes 49160 | tf_op jit(solution)/shard_map/ppermute | solution.py:46
  72.7 4.7 %collective-permute-start.17 = (f32[2,16,128]{2,1,0:T(8,128)S(1)}, f32[2,16,128]{2,1,0:T(8,128)S(1)}, u32[]{:S(2)}, u32[]{:S(2)}) collective-permute-start(f32[2,16,128]{2,1,0:T(8,128)S(1)} %get-tuple-element.32), channel_id=1, source_target_pairs={{0,3},{1,2},{2,1},{3,0},{4,7},{5,6},{6,5},{7,4},{8,11},{9,10},{10,... | collective-permute-start | bytes 49160 | tf_op jit(solution)/shard_map/ppermute | solution.py:46
  75.4 2.0 %collective-permute-start.15 = (f32[2,16,128]{2,1,0:T(8,128)S(1)}, f32[2,16,128]{2,1,0:T(8,128)S(1)}, u32[]{:S(2)}, u32[]{:S(2)}) collective-permute-start(f32[2,16,128]{2,1,0:T(8,128)S(1)} %get-tuple-element.31), channel_id=1, source_target_pairs={{0,1},{1,0},{2,3},{3,2},{4,5},{5,4},{6,7},{7,6},{8,9},{9,8},{10,11... | collective-permute-start | bytes 49160 | tf_op jit(solution)/shard_map/ppermute | solution.py:46
  78.3 18.7 %all-to-all-start = ((bf16[32,2,2048]{2,1,0:T(2,128)(2,1)}), bf16[32,2,2048]{2,1,0:T(2,128)(2,1)S(1)}, u32[]{:S(2)}, u32[]{:S(2)}) async-start(bf16[32,2,2048]{2,1,0:T(2,128)(2,1)} %broadcast_in_dim.11), calls=%async_computation | async-start | bytes 524288 | tf_op jit(solution)/shard_map/all_to_all | solution.py:195
  97.9 3.3 %collective-permute-start.18 = (f32[2,24,256]{2,1,0:T(8,128)S(1)}, f32[2,24,256]{2,1,0:T(8,128)S(1)}, u32[]{:S(2)}, u32[]{:S(2)}) collective-permute-start(f32[2,24,256]{2,1,0:T(8,128)S(1)} %pad_maximum_fusion.7), channel_id=1, source_target_pairs={{0,1},{1,0},{2,3},{3,2},{4,5},{5,4},{6,7},{7,6},{8,9},{9,8},{10,11... | collective-permute-start | bytes 147464 | tf_op jit(solution)/shard_map/ppermute | solution.py:46
  101.2 4.5 %collective-permute-start.19 = (f32[2,24,256]{2,1,0:T(8,128)S(1)}, f32[2,24,256]{2,1,0:T(8,128)S(1)}, u32[]{:S(2)}, u32[]{:S(2)}) collective-permute-start(f32[2,24,256]{2,1,0:T(8,128)S(1)} %maximum_add_fusion), channel_id=1, source_target_pairs={{0,4},{1,5},{2,6},{3,7},{4,0},{5,1},{6,2},{7,3},{8,12},{9,13},{10,... | collective-permute-start | bytes 147464 | tf_op jit(solution)/shard_map/ppermute | solution.py:46
  105.7 2.9 %collective-permute-start.20 = (f32[40,256]{1,0:T(8,128)S(1)}, f32[40,256]{1,0:T(8,128)S(1)}, u32[]{:S(2)}, u32[]{:S(2)}) collective-permute-start(f32[40,256]{1,0:T(8,128)S(1)} %fusion.16), channel_id=1, source_target_pairs={{0,2},{1,3},{2,0},{3,1},{4,6},{5,7},{6,4},{7,5},{8,10},{9,11},{10,... | collective-permute-start | bytes 122888 | tf_op jit(solution)/shard_map/ppermute | solution.py:46

commit v7 on v6

--- a/solution.py
+++ b/solution.py
@@ -36,6 +36,7 @@
 NEAR = pairs(lambda z, x, f, s: (z, x, f, s ^ 2))
 CORE_NEAR = pairs(lambda z, x, f, s: (z, x, f, s ^ 3))
 FAR = pairs(lambda z, x, f, s: (z, x, f ^ 1, s))
+FAR_NEAR = pairs(lambda z, x, f, s: (z, x, f ^ 1, s ^ 2))
 
 
 def shift(dz, dx):
@@ -157,22 +158,27 @@
     other_late = send(late, CORE)
     rows = jnp.concatenate([early, late])
     other = jnp.concatenate([other_early, other_late])
-    maps = jnp.concatenate(
-        [
-            jnp.dot(
-                weights, jnp.where(core == k, rows, other), preferred_element_type=jnp.float32
-            ).astype(jnp.bfloat16)
-            for k in (0, 1)
-        ],
-        axis=1,
-    )
-    left_map, right_map = maps[:LEFT], maps[LEFT:]
-    right = dot(cotangents.reshape(tokens, feat), right_map, LAST)
-    right = right.reshape(F, own, tok_local, RIGHT)
-    right_sum = pick(right, f) + send(pick(right, 1 - f), FAR)
-    left = dot(activations.reshape(tokens, feat), left_map, LAST)
-    left = left.reshape(F, own, tok_local, LEFT)
-    left_sum = pick(left, f) + send(pick(left, 1 - f), FAR)
+    sides = [jnp.where(core == k, rows, other) for k in (0, 1)]
+
+    def build(part):
+        return jnp.concatenate(
+            [
+                jnp.dot(part, side, preferred_element_type=jnp.float32).astype(jnp.bfloat16)
+                for side in sides
+            ],
+            axis=1,
+        )
+
+    left_map, right_map = build(weights[:LEFT]), build(weights[LEFT:])
+    cot = cotangents.reshape(F, tokens // F, feat)
+    act = activations.reshape(F, tokens // F, feat)
+    right_away = send(dot(pick(cot, 1 - f), right_map, LAST), FAR)
+    left_away = send(dot(pick(act, 1 - f), left_map, LAST), FAR)
+    right_here = dot(pick(cot, f), right_map, LAST)
+    left_here = dot(pick(act, f), left_map, LAST)
+    right_here, left_here = lax.optimization_barrier((right_here, left_here))
+    right_sum = (right_here + right_away).reshape(own, tok_local, RIGHT)
+    left_sum = (left_here + left_away).reshape(own, tok_local, LEFT)
 
     positions = s * tok_local + jnp.arange(tok_local, dtype=jnp.int32)
     own_lengths = pick(lengths.reshape(F, own), f)
@@ -188,7 +194,8 @@
     def part(k):
         return lax.dynamic_index_in_dim(parts, s ^ k, 1, keepdims=False)
 
-    summed = (part(0) + send(part(1), CORE)) + (send(part(2), NEAR) + send(part(3), CORE_NEAR))
+    halves = jnp.stack([part(0), part(2)]) + send(jnp.stack([part(1), part(3)]), CORE)
+    summed = halves[0] + send(halves[1], NEAR)
     demo_sketch = summed.astype(jnp.bfloat16).reshape(own, K // S)
 
     copies = jnp.broadcast_to(demo_sketch[None], (Z * X, own, K // S))
@@ -204,11 +211,10 @@
     keep = jnp.stack([pick(both, s), pick(both, s ^ 2)])
     give = jnp.stack([pick(both, s ^ 1), pick(both, s ^ 3)])
     pair = keep + send(give, CORE)
-    far = send(pair, FAR)
-    wide = jnp.concatenate([pair, far[:, :block_rows]], axis=1)
-    wide = wide[0] + send(wide[1], NEAR)
-    query_total = wide[block_rows : block_rows + 1, :nq]
-    here, there = wide[:block_rows], wide[block_rows + 8 :]
+    here = pair[0] + send(pair[1], NEAR)
+    there = send(pair[0], FAR) + send(pair[1], FAR_NEAR)
+    query_total = here[block_rows : block_rows + 1, :nq]
+    here, there = here[:block_rows], there[:block_rows]
     total = jnp.stack([jnp.where(f == 0, here, there), jnp.where(f == 0, there, here)])
     total = total.reshape(F, block_rows // own, own, 2 * nq).transpose(1, 0, 2, 3)
     total = total.reshape(F * block_rows, 2 * nq)

time: 110 us -> 101 us (0.918)
  waiting for transfers between devices: 40.3 us -> 35.4 us
  starting transfers between devices: 45.1 us -> 48.8 us
  local copies, waits for them, and re-layouts: 9.89 us -> 6.4 us
  matrix products: 8.93 us -> 6.09 us
    ppermute x21, waiting for transfers between devices: 28.8 us -> 25 us  [send(): return lax.ppermute(value, AXES, moves)]
    ppermute x21, starting transfers between devices: 38 us -> 41.8 us  [send(): return lax.ppermute(value, AXES, moves)]
    dot_general x3 -> x5, matrix products: 6.79 us -> 3.19 us  [dot(): lax.dot_general(a, b, (contract, ((), ())), preferred_element_type=jnp.fl...]
    reshape x2 -> x1, local copies, waits for them, and re-layouts: 2.44 us -> 0.14 us  [shards(): right_sum = (right_here + right_away).reshape(own, tok_local, RIGHT)]
    all_to_all x1, waiting for transfers between devices: 11.5 us -> 10.4 us  [shards(): lax.all_to_all(copies, 'demo', 0, 0).reshape(Z * X * own, K // S)]
    dot_general x2 -> x4, matrix products: 1.99 us -> 2.64 us  [build(): jnp.dot(part, side, preferred_element_type=jnp.float32).astype(jnp.bfloat16)]
    unnamed x19 -> x21, local copies, waits for them, and re-layouts: 2.24 us -> 1.93 us
  transfers between devices with their start and end apart: 22 -> 22, of which waited for: 11 -> 12; matrix products, arithmetic and copies ran while one was open for 8% -> 4% of each run, Pallas kernels for 2% -> 2%
where the time goes in v7:
time: 101 us
  starting transfers between devices  48.8 us (48%)
  waiting for transfers between devices  35.4 us (35%)
  local copies, waits for them, and re-layouts  6.4 us (6%)
  matrix products  6.09 us (6%)
  Pallas kernels  2.14 us (2%)
  other arithmetic  1.7 us (2%)
    ppermute x21, starting transfers between devices, send(): return lax.ppermute(value, AXES, moves)  41.8 us
    ppermute x21, waiting for transfers between devices, send(): return lax.ppermute(value, AXES, moves)  25 us
    all_to_all x1, waiting for transfers between devices, shards(): lax.all_to_all(copies, 'demo', 0, 0).reshape(Z * X * own, K // S)  10.4 us
    all_to_all x1, starting transfers between devices, shards(): lax.all_to_all(copies, 'demo', 0, 0).reshape(Z * X * own, K // S)  7.06 us
    dot_general x5, matrix products, dot(): lax.dot_general(a, b, (contract, ((), ())), preferred_element_type=jnp.fl...  3.19 us
    dot_general x4, matrix products, build(): jnp.dot(part, side, preferred_element_type=jnp.float32).astype(jnp.bfloat16)  2.64 us
    pallas_call x1, Pallas kernels, shards(): pl.pallas_call(weights_kernel, out_shape=[shape((LEFT + RIGHT, Z * X * RO...  2.14 us
  transfers between devices with their start and end apart: 22, of which 12 were waited for; matrix products, arithmetic and copies ran while one was open for 4% of the time, Pallas kernels for 2%

profile of v7, /device:TPU:1, one launch (start us, length us, event | category | flops | bytes accessed | tf_op | source)
XLA Modules:
  0.0 101.0 jit_solution(14581035827041754049)
XLA Ops:
  0.0 0.8 copy-done
  2.3 2.1 %collective-permute-start = (bf16[14,2048]{1,0:T(8,128)(2,1)S(1)}, bf16[14,2048]{1,0:T(8,128)(2,1)S(1)}, u32[]{:S(2)}, u32[]{:S(2)}) collective-permute-start(bf16[14,2048]{1,0:T(8,128)(2,1)S(1)} %pad_maximum_fusion.7), channel_id=1, source_target_pairs={{0,8},{1,9},{2,10},{3,11},{4,12},{5,13},{6,14},{7,15},{8,16},{9,17... | collective-permute-start | bytes 172040 | tf_op jit(solution)/shard_map/ppermute | solution.py:47
  4.4 2.5 %collective-permute-start.1 = (bf16[14,2048]{1,0:T(8,128)(2,1)S(1)}, bf16[14,2048]{1,0:T(8,128)(2,1)S(1)}, u32[]{:S(2)}, u32[]{:S(2)}) collective-permute-start(bf16[14,2048]{1,0:T(8,128)(2,1)S(1)} %pad_maximum_fusion.7), channel_id=1, source_target_pairs={{0,16},{1,17},{2,18},{3,19},{4,20},{5,21},{6,22},{7,23},{8,24},{9,... | collective-permute-start | bytes 172040 | tf_op jit(solution)/shard_map/ppermute | solution.py:47
  6.9 1.2 %collective-permute-start.2 = (bf16[14,2048]{1,0:T(8,128)(2,1)S(1)}, bf16[14,2048]{1,0:T(8,128)(2,1)S(1)}, u32[]{:S(2)}, u32[]{:S(2)}) collective-permute-start(bf16[14,2048]{1,0:T(8,128)(2,1)S(1)} %pad_maximum_fusion.7), channel_id=1, source_target_pairs={{0,24},{1,25},{2,26},{3,27},{4,28},{5,29},{6,30},{7,31},{8,0},{9,1... | collective-permute-start | bytes 172040 | tf_op jit(solution)/shard_map/ppermute | solution.py:47
  9.4 2.1 %shard_map.100 = (bf16[384,448]{1,0:T(8,128)(2,1)}, f32[8,128]{1,0:T(8,128)}) custom-call(s32[2]{0:T(128)} %pad_add_fusion.info_ref, bf16[128,128]{1,0:T(8,128)(2,1)} %contracting_ref.1, bf16[64,128]{1,0:T(8,128)(2,1)} %bitcast.74, bf16[128,2048]{1,0:T(8,128)(2,1)} %queries_ref.1), custom_call_target="tpu_custom_call" | custom-call | flops 100000000 | bytes 1000000 | tf_op jit(solution)/shard_map/pallas_call | solution.py:133
  12.2 1.7 %collective-permute-start.3 = (bf16[56,2048]{1,0:T(8,128)(2,1)S(1)}, bf16[56,2048]{1,0:T(8,128)(2,1)S(1)}, u32[]{:S(2)}, u32[]{:S(2)}) collective-permute-start(bf16[56,2048]{1,0:T(8,128)(2,1)S(1)} %concatenate.37), channel_id=1, source_target_pairs={{0,32},{1,33},{2,34},{3,35},{4,36},{5,37},{6,38},{7,39},{8,40},{9,... | collective-permute-start | bytes 688136 | tf_op jit(solution)/shard_map/ppermute | solution.py:47
  13.9 4.0 %collective-permute-start.5 = (bf16[56,2048]{1,0:T(8,128)(2,1)S(1)}, bf16[56,2048]{1,0:T(8,128)(2,1)S(1)}, u32[]{:S(2)}, u32[]{:S(2)}) collective-permute-start(bf16[56,2048]{1,0:T(8,128)(2,1)S(1)} %concatenate.37), channel_id=1, source_target_pairs={{0,224},{1,225},{2,226},{3,227},{4,228},{5,229},{6,230},{7,231},{8... | collective-permute-start | bytes 688136 | tf_op jit(solution)/shard_map/ppermute | solution.py:47
  18.0 4.3 %collective-permute-done.3 = bf16[56,2048]{1,0:T(8,128)(2,1)S(1)} collective-permute-done((bf16[56,2048]{1,0:T(8,128)(2,1)S(1)}, bf16[56,2048]{1,0:T(8,128)(2,1)S(1)}, u32[]{:S(2)}, u32[]{:S(2)}) %collective-permute-start.3) | collective-permute-done | bytes 229408 | tf_op jit(solution)/shard_map/ppermute | solution.py:47
  22.2 2.7 %collective-permute-start.6 = (bf16[56,2048]{1,0:T(8,128)(2,1)S(1)}, bf16[56,2048]{1,0:T(8,128)(2,1)S(1)}, u32[]{:S(2)}, u32[]{:S(2)}) collective-permute-start(bf16[56,2048]{1,0:T(8,128)(2,1)S(1)} %collective-permute-done.5), channel_id=1, source_target_pairs={{0,224},{1,225},{2,226},{3,227},{4,228},{5,229},{6,230},{7,231},{8... | collective-permute-start | bytes 688136 | tf_op jit(solution)/shard_map/ppermute | solution.py:47
  25.0 3.4 %collective-permute-done.4 = bf16[56,2048]{1,0:T(8,128)(2,1)S(1)} collective-permute-done((bf16[56,2048]{1,0:T(8,128)(2,1)S(1)}, bf16[56,2048]{1,0:T(8,128)(2,1)S(1)}, u32[]{:S(2)}, u32[]{:S(2)}) %collective-permute-start.4) | collective-permute-done | bytes 229408 | tf_op jit(solution)/shard_map/ppermute | solution.py:47
  28.3 2.7 %collective-permute-start.8 = (bf16[56,2048]{1,0:T(8,128)(2,1)S(1)}, bf16[56,2048]{1,0:T(8,128)(2,1)S(1)}, u32[]{:S(2)}, u32[]{:S(2)}) collective-permute-start(bf16[56,2048]{1,0:T(8,128)(2,1)S(1)} %collective-permute-done.6), channel_id=1, source_target_pairs={{0,224},{1,225},{2,226},{3,227},{4,228},{5,229},{6,230},{7,231},{8... | collective-permute-start | bytes 688136 | tf_op jit(solution)/shard_map/ppermute | solution.py:47
  31.1 4.0 %collective-permute-start.11 = (bf16[280,2048]{1,0:T(8,128)(2,1)S(1)}, bf16[280,2048]{1,0:T(8,128)(2,1)S(1)}, u32[]{:S(2)}, u32[]{:S(2)}) collective-permute-start(bf16[280,2048]{1,0:T(8,128)(2,1)S(1)} %get-tuple-element.19), channel_id=1, source_target_pairs={{0,1},{1,0},{2,3},{3,2},{4,5},{5,4},{6,7},{7,6},{8,9},{9,8},{10,11... | collective-permute-start | bytes 3440648 | tf_op jit(solution)/shard_map/ppermute | solution.py:47
  35.2 2.7 %collective-permute-start.10 = (bf16[24,2048]{1,0:T(8,128)(2,1)S(1)}, bf16[24,2048]{1,0:T(8,128)(2,1)S(1)}, u32[]{:S(2)}, u32[]{:S(2)}) collective-permute-start(bf16[24,2048]{1,0:T(8,128)(2,1)S(1)} %slice.55), channel_id=1, source_target_pairs={{0,224},{1,225},{2,226},{3,227},{4,228},{5,229},{6,230},{7,231},{8... | collective-permute-start | bytes 294920 | tf_op jit(solution)/shard_map/ppermute | solution.py:47
  38.0 1.6 %collective-permute-done.10 = bf16[24,2048]{1,0:T(8,128)(2,1)S(1)} collective-permute-done((bf16[24,2048]{1,0:T(8,128)(2,1)S(1)}, bf16[24,2048]{1,0:T(8,128)(2,1)S(1)}, u32[]{:S(2)}, u32[]{:S(2)}) %collective-permute-start.10) | collective-permute-done | bytes 98336 | tf_op jit(solution)/shard_map/ppermute | solution.py:47
  40.3 5.2 %collective-permute-start.12 = (bf16[168,2048]{1,0:T(8,128)(2,1)S(1)}, bf16[168,2048]{1,0:T(8,128)(2,1)S(1)}, u32[]{:S(2)}, u32[]{:S(2)}) collective-permute-start(bf16[168,2048]{1,0:T(8,128)(2,1)S(1)} %pad_maximum_fusion.4), channel_id=1, source_target_pairs={{0,1},{1,0},{2,3},{3,2},{4,5},{5,4},{6,7},{7,6},{8,9},{9,8},{10,11... | collective-permute-start | bytes 2064392 | tf_op jit(solution)/shard_map/ppermute | solution.py:47
  45.6 1.6 %collective-permute-done.12 = bf16[168,2048]{1,0:T(8,128)(2,1)S(1)} collective-permute-done((bf16[168,2048]{1,0:T(8,128)(2,1)S(1)}, bf16[168,2048]{1,0:T(8,128)(2,1)S(1)}, u32[]{:S(2)}, u32[]{:S(2)}) %collective-permute-start.12) | collective-permute-done | bytes 688160 | tf_op jit(solution)/shard_map/ppermute | solution.py:47
  47.9 0.8 convolution_convert_fusion.1
  49.2 0.8 convolution_convert_fusion
  50.0 0.8 copy-done.4
  51.6 3.0 %collective-permute-start.13 = (f32[256,128]{1,0:T(8,128)S(1)}, f32[256,128]{1,0:T(8,128)S(1)}, u32[]{:S(2)}, u32[]{:S(2)}) collective-permute-start(f32[256,128]{1,0:T(8,128)S(1)} %fusion.2), channel_id=1, source_target_pairs={{0,4},{1,5},{2,6},{3,7},{4,0},{5,1},{6,2},{7,3},{8,12},{9,13},{10,... | collective-permute-start | bytes 393224 | tf_op jit(solution)/shard_map/ppermute | solution.py:47
  58.0 6.8 %collective-permute-done.14 = f32[256,256]{1,0:T(8,128)S(1)} collective-permute-done((f32[256,256]{1,0:T(8,128)S(1)}, f32[256,256]{1,0:T(8,128)S(1)}, u32[]{:S(2)}, u32[]{:S(2)}) %collective-permute-start.14) | collective-permute-done | bytes 262176 | tf_op jit(solution)/shard_map/ppermute | solution.py:47
  65.3 1.6 %collective-permute-start.15 = (f32[2,2,16,128]{3,2,1,0:T(8,128)S(1)}, f32[2,2,16,128]{3,2,1,0:T(8,128)S(1)}, u32[]{:S(2)}, u32[]{:S(2)}) collective-permute-start(f32[2,2,16,128]{3,2,1,0:T(8,128)S(1)} %pad_maximum_fusion.10), channel_id=1, source_target_pairs={{0,1},{1,0},{2,3},{3,2},{4,5},{5,4},{6,7},{7,6},{8,9},{9,8},{10,11... | collective-permute-start | bytes 98312 | tf_op jit(solution)/shard_map/ppermute | solution.py:47
  66.9 0.9 collective-permute-done.15
  68.3 2.2 %collective-permute-done.16 = f32[2,16,128]{2,1,0:T(8,128)S(1)} collective-permute-done((f32[2,16,128]{2,1,0:T(8,128)S(1)}, f32[2,16,128]{2,1,0:T(8,128)S(1)}, u32[]{:S(2)}, u32[]{:S(2)}) %collective-permute-start.16) | collective-permute-done | bytes 16416 | tf_op jit(solution)/shard_map/ppermute | solution.py:47
  70.5 0.8 broadcast_in_dim.11
  71.3 7.1 %all-to-all-start = ((bf16[32,2,2048]{2,1,0:T(2,128)(2,1)}), bf16[32,2,2048]{2,1,0:T(2,128)(2,1)S(1)}, u32[]{:S(2)}, u32[]{:S(2)}) async-start(bf16[32,2,2048]{2,1,0:T(2,128)(2,1)} %broadcast_in_dim.11), calls=%async_computation | async-start | bytes 524288 | tf_op jit(solution)/shard_map/all_to_all | solution.py:202
  78.4 10.4 %all-to-all-done = bf16[32,2,2048]{2,1,0:T(2,128)(2,1)S(1)} async-done(((bf16[32,2,2048]{2,1,0:T(2,128)(2,1)}), bf16[32,2,2048]{2,1,0:T(2,128)(2,1)S(1)}, u32[]{:S(2)}, u32[]{:S(2)}) %all-to-all-start) | async-done | bytes 262176 | tf_op jit(solution)/shard_map/all_to_all | solution.py:202
  89.7 3.8 %collective-permute-start.17 = (f32[2,24,256]{2,1,0:T(8,128)S(1)}, f32[2,24,256]{2,1,0:T(8,128)S(1)}, u32[]{:S(2)}, u32[]{:S(2)}) collective-permute-start(f32[2,24,256]{2,1,0:T(8,128)S(1)} %pad_maximum_fusion.9), channel_id=1, source_target_pairs={{0,1},{1,0},{2,3},{3,2},{4,5},{5,4},{6,7},{7,6},{8,9},{9,8},{10,11... | collective-permute-start | bytes 147464 | tf_op jit(solution)/shard_map/ppermute | solution.py:47
  93.6 0.9 collective-permute-done.17
  95.0 1.1 %collective-permute-start.20 = (f32[24,256]{1,0:T(8,128)S(1)}, f32[24,256]{1,0:T(8,128)S(1)}, u32[]{:S(2)}, u32[]{:S(2)}) collective-permute-start(f32[24,256]{1,0:T(8,128)S(1)} %get-tuple-element.40), channel_id=1, source_target_pairs={{0,6},{1,7},{2,4},{3,5},{4,2},{5,3},{6,0},{7,1},{8,14},{9,15},{10,... | collective-permute-start | bytes 73736 | tf_op jit(solution)/shard_map/ppermute | solution.py:47
  96.1 1.7 %collective-permute-start.19 = (f32[24,256]{1,0:T(8,128)S(1)}, f32[24,256]{1,0:T(8,128)S(1)}, u32[]{:S(2)}, u32[]{:S(2)}) collective-permute-start(f32[24,256]{1,0:T(8,128)S(1)} %get-tuple-element.39), channel_id=1, source_target_pairs={{0,4},{1,5},{2,6},{3,7},{4,0},{5,1},{6,2},{7,3},{8,12},{9,13},{10,... | collective-permute-start | bytes 73736 | tf_op jit(solution)/shard_map/ppermute | solution.py:47
  97.8 2.4 %collective-permute-done.19 = f32[24,256]{1,0:T(8,128)S(1)} collective-permute-done((f32[24,256]{1,0:T(8,128)S(1)}, f32[24,256]{1,0:T(8,128)S(1)}, u32[]{:S(2)}, u32[]{:S(2)}) %collective-permute-start.19) | collective-permute-done | bytes 24608 | tf_op jit(solution)/shard_map/ppermute | solution.py:47
  (90 shorter events, 13.0 us)
Async XLA Ops:
  0.0 0.8 copy-start
  2.3 9.3 %collective-permute-start = (bf16[14,2048]{1,0:T(8,128)(2,1)S(1)}, bf16[14,2048]{1,0:T(8,128)(2,1)S(1)}, u32[]{:S(2)}, u32[]{:S(2)}) collective-permute-start(bf16[14,2048]{1,0:T(8,128)(2,1)S(1)} %pad_maximum_fusion.7), channel_id=1, source_target_pairs={{0,8},{1,9},{2,10},{3,11},{4,12},{5,13},{6,14},{7,15},{8,16},{9,17... | collective-permute-start | bytes 172040 | tf_op jit(solution)/shard_map/ppermute | solution.py:47
  4.4 7.2 %collective-permute-start.1 = (bf16[14,2048]{1,0:T(8,128)(2,1)S(1)}, bf16[14,2048]{1,0:T(8,128)(2,1)S(1)}, u32[]{:S(2)}, u32[]{:S(2)}) collective-permute-start(bf16[14,2048]{1,0:T(8,128)(2,1)S(1)} %pad_maximum_fusion.7), channel_id=1, source_target_pairs={{0,16},{1,17},{2,18},{3,19},{4,20},{5,21},{6,22},{7,23},{8,24},{9,... | collective-permute-start | bytes 172040 | tf_op jit(solution)/shard_map/ppermute | solution.py:47
  6.9 4.7 %collective-permute-start.2 = (bf16[14,2048]{1,0:T(8,128)(2,1)S(1)}, bf16[14,2048]{1,0:T(8,128)(2,1)S(1)}, u32[]{:S(2)}, u32[]{:S(2)}) collective-permute-start(bf16[14,2048]{1,0:T(8,128)(2,1)S(1)} %pad_maximum_fusion.7), channel_id=1, source_target_pairs={{0,24},{1,25},{2,26},{3,27},{4,28},{5,29},{6,30},{7,31},{8,0},{9,1... | collective-permute-start | bytes 172040 | tf_op jit(solution)/shard_map/ppermute | solution.py:47
  12.2 10.1 %collective-permute-start.3 = (bf16[56,2048]{1,0:T(8,128)(2,1)S(1)}, bf16[56,2048]{1,0:T(8,128)(2,1)S(1)}, u32[]{:S(2)}, u32[]{:S(2)}) collective-permute-start(bf16[56,2048]{1,0:T(8,128)(2,1)S(1)} %concatenate.37), channel_id=1, source_target_pairs={{0,32},{1,33},{2,34},{3,35},{4,36},{5,37},{6,38},{7,39},{8,40},{9,... | collective-permute-start | bytes 688136 | tf_op jit(solution)/shard_map/ppermute | solution.py:47
  13.9 8.3 %collective-permute-start.5 = (bf16[56,2048]{1,0:T(8,128)(2,1)S(1)}, bf16[56,2048]{1,0:T(8,128)(2,1)S(1)}, u32[]{:S(2)}, u32[]{:S(2)}) collective-permute-start(bf16[56,2048]{1,0:T(8,128)(2,1)S(1)} %concatenate.37), channel_id=1, source_target_pairs={{0,224},{1,225},{2,226},{3,227},{4,228},{5,229},{6,230},{7,231},{8... | collective-permute-start | bytes 688136 | tf_op jit(solution)/shard_map/ppermute | solution.py:47
  22.2 6.1 %collective-permute-start.4 = (bf16[56,2048]{1,0:T(8,128)(2,1)S(1)}, bf16[56,2048]{1,0:T(8,128)(2,1)S(1)}, u32[]{:S(2)}, u32[]{:S(2)}) collective-permute-start(bf16[56,2048]{1,0:T(8,128)(2,1)S(1)} %collective-permute-done.3), channel_id=1, source_target_pairs={{0,32},{1,33},{2,34},{3,35},{4,36},{5,37},{6,38},{7,39},{8,40},{9,... | collective-permute-start | bytes 688136 | tf_op jit(solution)/shard_map/ppermute | solution.py:47
  22.2 6.1 %collective-permute-start.6 = (bf16[56,2048]{1,0:T(8,128)(2,1)S(1)}, bf16[56,2048]{1,0:T(8,128)(2,1)S(1)}, u32[]{:S(2)}, u32[]{:S(2)}) collective-permute-start(bf16[56,2048]{1,0:T(8,128)(2,1)S(1)} %collective-permute-done.5), channel_id=1, source_target_pairs={{0,224},{1,225},{2,226},{3,227},{4,228},{5,229},{6,230},{7,231},{8... | collective-permute-start | bytes 688136 | tf_op jit(solution)/shard_map/ppermute | solution.py:47
  28.3 6.8 %collective-permute-start.7 = (bf16[56,2048]{1,0:T(8,128)(2,1)S(1)}, bf16[56,2048]{1,0:T(8,128)(2,1)S(1)}, u32[]{:S(2)}, u32[]{:S(2)}) collective-permute-start(bf16[56,2048]{1,0:T(8,128)(2,1)S(1)} %collective-permute-done.4), channel_id=1, source_target_pairs={{0,32},{1,33},{2,34},{3,35},{4,36},{5,37},{6,38},{7,39},{8,40},{9,... | collective-permute-start | bytes 688136 | tf_op jit(solution)/shard_map/ppermute | solution.py:47
  28.3 6.9 %collective-permute-start.8 = (bf16[56,2048]{1,0:T(8,128)(2,1)S(1)}, bf16[56,2048]{1,0:T(8,128)(2,1)S(1)}, u32[]{:S(2)}, u32[]{:S(2)}) collective-permute-start(bf16[56,2048]{1,0:T(8,128)(2,1)S(1)} %collective-permute-done.6), channel_id=1, source_target_pairs={{0,224},{1,225},{2,226},{3,227},{4,228},{5,229},{6,230},{7,231},{8... | collective-permute-start | bytes 688136 | tf_op jit(solution)/shard_map/ppermute | solution.py:47
  31.1 14.4 %collective-permute-start.11 = (bf16[280,2048]{1,0:T(8,128)(2,1)S(1)}, bf16[280,2048]{1,0:T(8,128)(2,1)S(1)}, u32[]{:S(2)}, u32[]{:S(2)}) collective-permute-start(bf16[280,2048]{1,0:T(8,128)(2,1)S(1)} %get-tuple-element.19), channel_id=1, source_target_pairs={{0,1},{1,0},{2,3},{3,2},{4,5},{5,4},{6,7},{7,6},{8,9},{9,8},{10,11... | collective-permute-start | bytes 3440648 | tf_op jit(solution)/shard_map/ppermute | solution.py:47
  35.1 5.1 %collective-permute-start.9 = (bf16[32,2048]{1,0:T(8,128)(2,1)S(1)}, bf16[32,2048]{1,0:T(8,128)(2,1)S(1)}, u32[]{:S(2)}, u32[]{:S(2)}) collective-permute-start(bf16[32,2048]{1,0:T(8,128)(2,1)S(1)} %slice.54), channel_id=1, source_target_pairs={{0,32},{1,33},{2,34},{3,35},{4,36},{5,37},{6,38},{7,39},{8,40},{9,... | collective-permute-start | bytes 393224 | tf_op jit(solution)/shard_map/ppermute | solution.py:47
  35.2 4.4 %collective-permute-start.10 = (bf16[24,2048]{1,0:T(8,128)(2,1)S(1)}, bf16[24,2048]{1,0:T(8,128)(2,1)S(1)}, u32[]{:S(2)}, u32[]{:S(2)}) collective-permute-start(bf16[24,2048]{1,0:T(8,128)(2,1)S(1)} %slice.55), channel_id=1, source_target_pairs={{0,224},{1,225},{2,226},{3,227},{4,228},{5,229},{6,230},{7,231},{8... | collective-permute-start | bytes 294920 | tf_op jit(solution)/shard_map/ppermute | solution.py:47
  40.3 7.0 %collective-permute-start.12 = (bf16[168,2048]{1,0:T(8,128)(2,1)S(1)}, bf16[168,2048]{1,0:T(8,128)(2,1)S(1)}, u32[]{:S(2)}, u32[]{:S(2)}) collective-permute-start(bf16[168,2048]{1,0:T(8,128)(2,1)S(1)} %pad_maximum_fusion.4), channel_id=1, source_target_pairs={{0,1},{1,0},{2,3},{3,2},{4,5},{5,4},{6,7},{7,6},{8,9},{9,8},{10,11... | collective-permute-start | bytes 2064392 | tf_op jit(solution)/shard_map/ppermute | solution.py:47
  45.5 1.8 %copy-start.5 = (bf16[384,448]{1,0:T(8,128)(2,1)S(1)}, bf16[384,448]{1,0:T(8,128)(2,1)}, u32[]{:S(2)}) copy-start(bf16[384,448]{1,0:T(8,128)(2,1)} %get-tuple-element.14) | copy-start | bytes 1032196
  48.7 2.2 %copy-start.4 = (bf16[4,128,4096]{2,1,0:T(8,128)(2,1)S(1)}, bf16[4,128,4096]{2,1,0:T(8,128)(2,1)}, u32[]{:S(2)}) copy-start(bf16[4,128,4096]{2,1,0:T(8,128)(2,1)} %param.10) | copy-start | bytes 12582916
  49.2 5.3 %copy-start.3 = (bf16[4,128,4096]{2,1,0:T(8,128)(2,1)S(1)}, bf16[4,128,4096]{2,1,0:T(8,128)(2,1)}, u32[]{:S(2)}) copy-start(bf16[4,128,4096]{2,1,0:T(8,128)(2,1)} %param.11) | copy-start | bytes 12582916
  51.6 6.3 %collective-permute-start.13 = (f32[256,128]{1,0:T(8,128)S(1)}, f32[256,128]{1,0:T(8,128)S(1)}, u32[]{:S(2)}, u32[]{:S(2)}) collective-permute-start(f32[256,128]{1,0:T(8,128)S(1)} %fusion.2), channel_id=1, source_target_pairs={{0,4},{1,5},{2,6},{3,7},{4,0},{5,1},{6,2},{7,3},{8,12},{9,13},{10,... | collective-permute-start | bytes 393224 | tf_op jit(solution)/shard_map/ppermute | solution.py:47
  56.1 8.8 %collective-permute-start.14 = (f32[256,256]{1,0:T(8,128)S(1)}, f32[256,256]{1,0:T(8,128)S(1)}, u32[]{:S(2)}, u32[]{:S(2)}) collective-permute-start(f32[256,256]{1,0:T(8,128)S(1)} %fusion), channel_id=1, source_target_pairs={{0,4},{1,5},{2,6},{3,7},{4,0},{5,1},{6,2},{7,3},{8,12},{9,13},{10,... | collective-permute-start | bytes 786440 | tf_op jit(solution)/shard_map/ppermute | solution.py:47
  57.5 20.9 %copy-start.2 = (f32[8,128]{1,0:T(8,128)S(1)}, f32[8,128]{1,0:T(8,128)}, u32[]{:S(2)}) copy-start(f32[8,128]{1,0:T(8,128)} %get-tuple-element.18) | copy-start | bytes 12292
  57.9 31.0 %copy-start.1 = (bf16[128,2048]{1,0:T(8,128)(2,1)S(1)}, bf16[128,2048]{1,0:T(8,128)(2,1)}, u32[]{:S(2)}) copy-start(bf16[128,2048]{1,0:T(8,128)(2,1)} %queries_ref.1) | copy-start | bytes 1572868
  65.3 2.5 %collective-permute-start.15 = (f32[2,2,16,128]{3,2,1,0:T(8,128)S(1)}, f32[2,2,16,128]{3,2,1,0:T(8,128)S(1)}, u32[]{:S(2)}, u32[]{:S(2)}) collective-permute-start(f32[2,2,16,128]{3,2,1,0:T(8,128)S(1)} %pad_maximum_fusion.10), channel_id=1, source_target_pairs={{0,1},{1,0},{2,3},{3,2},{4,5},{5,4},{6,7},{7,6},{8,9},{9,8},{10,11... | collective-permute-start | bytes 98312 | tf_op jit(solution)/shard_map/ppermute | solution.py:47
  67.8 2.7 %collective-permute-start.16 = (f32[2,16,128]{2,1,0:T(8,128)S(1)}, f32[2,16,128]{2,1,0:T(8,128)S(1)}, u32[]{:S(2)}, u32[]{:S(2)}) collective-permute-start(f32[2,16,128]{2,1,0:T(8,128)S(1)} %slice_bitcast_fusion.2), channel_id=1, source_target_pairs={{0,2},{1,3},{2,0},{3,1},{4,6},{5,7},{6,4},{7,5},{8,10},{9,11},{10,... | collective-permute-start | bytes 49160 | tf_op jit(solution)/shard_map/ppermute | solution.py:47
  71.3 17.5 %all-to-all-start = ((bf16[32,2,2048]{2,1,0:T(2,128)(2,1)}), bf16[32,2,2048]{2,1,0:T(2,128)(2,1)S(1)}, u32[]{:S(2)}, u32[]{:S(2)}) async-start(bf16[32,2,2048]{2,1,0:T(2,128)(2,1)} %broadcast_in_dim.11), calls=%async_computation | async-start | bytes 524288 | tf_op jit(solution)/shard_map/all_to_all | solution.py:202
  89.7 4.7 %collective-permute-start.17 = (f32[2,24,256]{2,1,0:T(8,128)S(1)}, f32[2,24,256]{2,1,0:T(8,128)S(1)}, u32[]{:S(2)}, u32[]{:S(2)}) collective-permute-start(f32[2,24,256]{2,1,0:T(8,128)S(1)} %pad_maximum_fusion.9), channel_id=1, source_target_pairs={{0,1},{1,0},{2,3},{3,2},{4,5},{5,4},{6,7},{7,6},{8,9},{9,8},{10,11... | collective-permute-start | bytes 147464 | tf_op jit(solution)/shard_map/ppermute | solution.py:47
  94.5 3.3 %collective-permute-start.18 = (f32[24,256]{1,0:T(8,128)S(1)}, f32[24,256]{1,0:T(8,128)S(1)}, u32[]{:S(2)}, u32[]{:S(2)}) collective-permute-start(f32[24,256]{1,0:T(8,128)S(1)} %get-tuple-element.40), channel_id=1, source_target_pairs={{0,2},{1,3},{2,0},{3,1},{4,6},{5,7},{6,4},{7,5},{8,10},{9,11},{10,... | collective-permute-start | bytes 73736 | tf_op jit(solution)/shard_map/ppermute | solution.py:47
  95.0 5.3 %collective-permute-start.20 = (f32[24,256]{1,0:T(8,128)S(1)}, f32[24,256]{1,0:T(8,128)S(1)}, u32[]{:S(2)}, u32[]{:S(2)}) collective-permute-start(f32[24,256]{1,0:T(8,128)S(1)} %get-tuple-element.40), channel_id=1, source_target_pairs={{0,6},{1,7},{2,4},{3,5},{4,2},{5,3},{6,0},{7,1},{8,14},{9,15},{10,... | collective-permute-start | bytes 73736 | tf_op jit(solution)/shard_map/ppermute | solution.py:47
  96.1 4.2 %collective-permute-start.19 = (f32[24,256]{1,0:T(8,128)S(1)}, f32[24,256]{1,0:T(8,128)S(1)}, u32[]{:S(2)}, u32[]{:S(2)}) collective-permute-start(f32[24,256]{1,0:T(8,128)S(1)} %get-tuple-element.39), channel_id=1, source_target_pairs={{0,4},{1,5},{2,6},{3,7},{4,0},{5,1},{6,2},{7,3},{8,12},{9,13},{10,... | collective-permute-start | bytes 73736 | tf_op jit(solution)/shard_map/ppermute | solution.py:47

commit v8 on v7

--- a/solution.py
+++ b/solution.py
@@ -119,17 +119,17 @@
     s = lax.axis_index("sketch")
     core = s % 2
 
-    block = jnp.concatenate(
-        [
-            lax.dynamic_slice_in_dim(part.T, core * half, half, axis=1)
-            for part in (
-                lowrank_contract_matrix,
-                lowrank_expand_matrix,
-                output_feature_sketch,
-                input_feature_sketch,
-            )
-        ]
-    )
+    block, start = None, 0
+    for part in (
+        lowrank_contract_matrix,
+        lowrank_expand_matrix,
+        output_feature_sketch,
+        input_feature_sketch,
+    ):
+        rows = lax.dynamic_slice_in_dim(part.T, core * half, half, axis=1)
+        rows = jnp.pad(rows, ((start, ROWS - start - rows.shape[0]), (0, 0)))
+        block = rows if block is None else block + rows
+        start += part.shape[1]
     weights, query_squares = pl.pallas_call(
         weights_kernel,
         out_shape=[shape((LEFT + RIGHT, Z * X * ROWS), jnp.bfloat16), shape((8, 128))],
@@ -203,24 +203,24 @@
     inner = dot(every_demo, queries, LAST)
     every_f = every_demo.astype(jnp.float32)
     demo_squares = jnp.sum(every_f * every_f, axis=1, keepdims=True)
-    both = jnp.concatenate([inner, jnp.broadcast_to(demo_squares, inner.shape)], axis=1)
+    both = inner
     block_rows = Z * X * own // S
-    both = both.reshape(S, block_rows, 2 * nq)
-    extra = jnp.concatenate([query_squares, query_squares], axis=1)
-    both = jnp.concatenate([both, jnp.broadcast_to(extra[None], (S, 8, 2 * nq))], axis=1)
+    spread = jnp.broadcast_to(demo_squares, inner.shape).reshape(S, block_rows, nq)
+    both = both.reshape(S, block_rows, nq)
+    extra = jnp.broadcast_to(query_squares[None], (S, 8, nq))
+    both = jnp.concatenate([both, spread, extra], axis=1)
     keep = jnp.stack([pick(both, s), pick(both, s ^ 2)])
     give = jnp.stack([pick(both, s ^ 1), pick(both, s ^ 3)])
     pair = keep + send(give, CORE)
     here = pair[0] + send(pair[1], NEAR)
     there = send(pair[0], FAR) + send(pair[1], FAR_NEAR)
-    query_total = here[block_rows : block_rows + 1, :nq]
-    here, there = here[:block_rows], there[:block_rows]
+    query_total = here[2 * block_rows : 2 * block_rows + 1]
     total = jnp.stack([jnp.where(f == 0, here, there), jnp.where(f == 0, there, here)])
-    total = total.reshape(F, block_rows // own, own, 2 * nq).transpose(1, 0, 2, 3)
-    total = total.reshape(F * block_rows, 2 * nq)
-    demo_norm = jnp.sqrt(total[:, nq:] + 1e-06)
+    total = total[:, : 2 * block_rows].reshape(F, 2, block_rows // own, own, nq)
+    total = total.transpose(1, 2, 0, 3, 4).reshape(2, F * block_rows, nq)
+    demo_norm = jnp.sqrt(total[1] + 1e-06)
     query_norm = jnp.sqrt(query_total + 1e-06)
-    return math.sqrt(K) * total[:, :nq] / (demo_norm * query_norm)
+    return math.sqrt(K) * total[0] / (demo_norm * query_norm)
 
 
 def solution(mesh):

time: 101 us -> 100 us (0.990)
  blocking collectives: 0 us -> 17.3 us
  waiting for transfers between devices: 35.4 us -> 24.8 us
  starting transfers between devices: 48.8 us -> 42.4 us
  local copies, waits for them, and re-layouts: 6.4 us -> 4.96 us
    all_to_all x0 -> x1, blocking collectives: none -> 17.3 us  [shards(): lax.all_to_all(copies, 'demo', 0, 0).reshape(Z * X * own, K // S)]
    all_to_all x1 -> x0, waiting for transfers between devices: 10.4 us -> none  [shards(): lax.all_to_all(copies, 'demo', 0, 0).reshape(Z * X * own, K // S)]
    all_to_all x1 -> x0, starting transfers between devices: 7.06 us -> none  [shards(): lax.all_to_all(copies, 'demo', 0, 0).reshape(Z * X * own, K // S)]
  transfers between devices with their start and end apart: 22 -> 21, of which waited for: 12 -> 12; matrix products, arithmetic and copies ran while one was open for 4% -> 4% of each run, Pallas kernels for 2% -> 2%
where the time goes in v8:
time: 100 us
  starting transfers between devices  42.4 us (42%)
  waiting for transfers between devices  24.8 us (25%)
  blocking collectives  17.3 us (17%)
  matrix products  6.07 us (6%)
  local copies, waits for them, and re-layouts  4.96 us (5%)
  Pallas kernels  2.13 us (2%)
  other arithmetic  1.91 us (2%)
    ppermute x21, starting transfers between devices, send(): return lax.ppermute(value, AXES, moves)  42.4 us
    ppermute x21, waiting for transfers between devices, send(): return lax.ppermute(value, AXES, moves)  24.8 us
    all_to_all x1, blocking collectives, shards(): lax.all_to_all(copies, 'demo', 0, 0).reshape(Z * X * own, K // S)  17.3 us
    dot_general x5, matrix products, dot(): lax.dot_general(a, b, (contract, ((), ())), preferred_element_type=jnp.fl...  3.18 us
    dot_general x4, matrix products, build(): jnp.dot(part, side, preferred_element_type=jnp.float32).astype(jnp.bfloat16)  2.64 us
    pallas_call x1, Pallas kernels, shards(): pl.pallas_call(weights_kernel, out_shape=[shape((LEFT + RIGHT, Z * X * RO...  2.13 us
  transfers between devices with their start and end apart: 21, of which 12 were waited for; matrix products, arithmetic and copies ran while one was open for 4% of the time, Pallas kernels for 2%

profile of v8, /device:TPU:1, one launch (start us, length us, event | category | flops | bytes accessed | tf_op | source)
XLA Modules:
  0.0 100.0 jit_solution(1798944238869576327)
XLA Ops:
  0.0 0.8 copy-done
  1.5 0.7 dynamic-slice_bitcast_fusion.4
  2.3 2.1 %collective-permute-start = (bf16[14,2048]{1,0:T(8,128)(2,1)S(1)}, bf16[14,2048]{1,0:T(8,128)(2,1)S(1)}, u32[]{:S(2)}, u32[]{:S(2)}) collective-permute-start(bf16[14,2048]{1,0:T(8,128)(2,1)S(1)} %pad_add_fusion), channel_id=1, source_target_pairs={{0,8},{1,9},{2,10},{3,11},{4,12},{5,13},{6,14},{7,15},{8,16},{9,17... | collective-permute-start | bytes 172040 | tf_op jit(solution)/shard_map/ppermute | solution.py:47
  4.4 2.5 %collective-permute-start.1 = (bf16[14,2048]{1,0:T(8,128)(2,1)S(1)}, bf16[14,2048]{1,0:T(8,128)(2,1)S(1)}, u32[]{:S(2)}, u32[]{:S(2)}) collective-permute-start(bf16[14,2048]{1,0:T(8,128)(2,1)S(1)} %pad_add_fusion), channel_id=1, source_target_pairs={{0,16},{1,17},{2,18},{3,19},{4,20},{5,21},{6,22},{7,23},{8,24},{9,... | collective-permute-start | bytes 172040 | tf_op jit(solution)/shard_map/ppermute | solution.py:47
  6.9 1.2 %collective-permute-start.2 = (bf16[14,2048]{1,0:T(8,128)(2,1)S(1)}, bf16[14,2048]{1,0:T(8,128)(2,1)S(1)}, u32[]{:S(2)}, u32[]{:S(2)}) collective-permute-start(bf16[14,2048]{1,0:T(8,128)(2,1)S(1)} %pad_add_fusion), channel_id=1, source_target_pairs={{0,24},{1,25},{2,26},{3,27},{4,28},{5,29},{6,30},{7,31},{8,0},{9,1... | collective-permute-start | bytes 172040 | tf_op jit(solution)/shard_map/ppermute | solution.py:47
  9.4 2.1 %shard_map.100 = (bf16[384,448]{1,0:T(8,128)(2,1)}, f32[8,128]{1,0:T(8,128)}) custom-call(s32[2]{0:T(128)} %pad_add_fusion.1.info_ref, bf16[128,128]{1,0:T(8,128)(2,1)} %contracting_ref.1, bf16[64,128]{1,0:T(8,128)(2,1)} %bitcast.83, bf16[128,2048]{1,0:T(8,128)(2,1)} %queries_ref.1), custom_call_target="tpu_custom_call" | custom-call | flops 100000000 | bytes 1000000 | tf_op jit(solution)/shard_map/pallas_call | solution.py:133
  11.6 1.7 %collective-permute-start.3 = (bf16[56,2048]{1,0:T(8,128)(2,1)S(1)}, bf16[56,2048]{1,0:T(8,128)(2,1)S(1)}, u32[]{:S(2)}, u32[]{:S(2)}) collective-permute-start(bf16[56,2048]{1,0:T(8,128)(2,1)S(1)} %pad_maximum_fusion.7), channel_id=1, source_target_pairs={{0,32},{1,33},{2,34},{3,35},{4,36},{5,37},{6,38},{7,39},{8,40},{9,... | collective-permute-start | bytes 688136 | tf_op jit(solution)/shard_map/ppermute | solution.py:47
  13.3 4.0 %collective-permute-start.5 = (bf16[56,2048]{1,0:T(8,128)(2,1)S(1)}, bf16[56,2048]{1,0:T(8,128)(2,1)S(1)}, u32[]{:S(2)}, u32[]{:S(2)}) collective-permute-start(bf16[56,2048]{1,0:T(8,128)(2,1)S(1)} %pad_maximum_fusion.7), channel_id=1, source_target_pairs={{0,224},{1,225},{2,226},{3,227},{4,228},{5,229},{6,230},{7,231},{8... | collective-permute-start | bytes 688136 | tf_op jit(solution)/shard_map/ppermute | solution.py:47
  17.4 4.3 %collective-permute-done.3 = bf16[56,2048]{1,0:T(8,128)(2,1)S(1)} collective-permute-done((bf16[56,2048]{1,0:T(8,128)(2,1)S(1)}, bf16[56,2048]{1,0:T(8,128)(2,1)S(1)}, u32[]{:S(2)}, u32[]{:S(2)}) %collective-permute-start.3) | collective-permute-done | bytes 229408 | tf_op jit(solution)/shard_map/ppermute | solution.py:47
  21.7 2.7 %collective-permute-start.6 = (bf16[56,2048]{1,0:T(8,128)(2,1)S(1)}, bf16[56,2048]{1,0:T(8,128)(2,1)S(1)}, u32[]{:S(2)}, u32[]{:S(2)}) collective-permute-start(bf16[56,2048]{1,0:T(8,128)(2,1)S(1)} %collective-permute-done.5), channel_id=1, source_target_pairs={{0,224},{1,225},{2,226},{3,227},{4,228},{5,229},{6,230},{7,231},{8... | collective-permute-start | bytes 688136 | tf_op jit(solution)/shard_map/ppermute | solution.py:47
  24.4 3.4 %collective-permute-done.4 = bf16[56,2048]{1,0:T(8,128)(2,1)S(1)} collective-permute-done((bf16[56,2048]{1,0:T(8,128)(2,1)S(1)}, bf16[56,2048]{1,0:T(8,128)(2,1)S(1)}, u32[]{:S(2)}, u32[]{:S(2)}) %collective-permute-start.4) | collective-permute-done | bytes 229408 | tf_op jit(solution)/shard_map/ppermute | solution.py:47
  27.8 2.7 %collective-permute-start.8 = (bf16[56,2048]{1,0:T(8,128)(2,1)S(1)}, bf16[56,2048]{1,0:T(8,128)(2,1)S(1)}, u32[]{:S(2)}, u32[]{:S(2)}) collective-permute-start(bf16[56,2048]{1,0:T(8,128)(2,1)S(1)} %collective-permute-done.6), channel_id=1, source_target_pairs={{0,224},{1,225},{2,226},{3,227},{4,228},{5,229},{6,230},{7,231},{8... | collective-permute-start | bytes 688136 | tf_op jit(solution)/shard_map/ppermute | solution.py:47
  30.6 4.0 %collective-permute-start.11 = (bf16[280,2048]{1,0:T(8,128)(2,1)S(1)}, bf16[280,2048]{1,0:T(8,128)(2,1)S(1)}, u32[]{:S(2)}, u32[]{:S(2)}) collective-permute-start(bf16[280,2048]{1,0:T(8,128)(2,1)S(1)} %get-tuple-element.21), channel_id=1, source_target_pairs={{0,1},{1,0},{2,3},{3,2},{4,5},{5,4},{6,7},{7,6},{8,9},{9,8},{10,11... | collective-permute-start | bytes 3440648 | tf_op jit(solution)/shard_map/ppermute | solution.py:47
  34.7 2.7 %collective-permute-start.10 = (bf16[24,2048]{1,0:T(8,128)(2,1)S(1)}, bf16[24,2048]{1,0:T(8,128)(2,1)S(1)}, u32[]{:S(2)}, u32[]{:S(2)}) collective-permute-start(bf16[24,2048]{1,0:T(8,128)(2,1)S(1)} %slice.53), channel_id=1, source_target_pairs={{0,224},{1,225},{2,226},{3,227},{4,228},{5,229},{6,230},{7,231},{8... | collective-permute-start | bytes 294920 | tf_op jit(solution)/shard_map/ppermute | solution.py:47
  37.4 1.6 %collective-permute-done.10 = bf16[24,2048]{1,0:T(8,128)(2,1)S(1)} collective-permute-done((bf16[24,2048]{1,0:T(8,128)(2,1)S(1)}, bf16[24,2048]{1,0:T(8,128)(2,1)S(1)}, u32[]{:S(2)}, u32[]{:S(2)}) %collective-permute-start.10) | collective-permute-done | bytes 98336 | tf_op jit(solution)/shard_map/ppermute | solution.py:47
  39.7 5.2 %collective-permute-start.12 = (bf16[168,2048]{1,0:T(8,128)(2,1)S(1)}, bf16[168,2048]{1,0:T(8,128)(2,1)S(1)}, u32[]{:S(2)}, u32[]{:S(2)}) collective-permute-start(bf16[168,2048]{1,0:T(8,128)(2,1)S(1)} %pad_maximum_fusion.4), channel_id=1, source_target_pairs={{0,1},{1,0},{2,3},{3,2},{4,5},{5,4},{6,7},{7,6},{8,9},{9,8},{10,11... | collective-permute-start | bytes 2064392 | tf_op jit(solution)/shard_map/ppermute | solution.py:47
  45.1 1.6 %collective-permute-done.12 = bf16[168,2048]{1,0:T(8,128)(2,1)S(1)} collective-permute-done((bf16[168,2048]{1,0:T(8,128)(2,1)S(1)}, bf16[168,2048]{1,0:T(8,128)(2,1)S(1)}, u32[]{:S(2)}, u32[]{:S(2)}) %collective-permute-start.12) | collective-permute-done | bytes 688160 | tf_op jit(solution)/shard_map/ppermute | solution.py:47
  47.3 0.8 convolution_convert_fusion.1
  48.7 0.8 convolution_convert_fusion
  49.4 0.8 copy-done.4
  51.0 3.0 %collective-permute-start.13 = (f32[256,128]{1,0:T(8,128)S(1)}, f32[256,128]{1,0:T(8,128)S(1)}, u32[]{:S(2)}, u32[]{:S(2)}) collective-permute-start(f32[256,128]{1,0:T(8,128)S(1)} %fusion.2), channel_id=1, source_target_pairs={{0,4},{1,5},{2,6},{3,7},{4,0},{5,1},{6,2},{7,3},{8,12},{9,13},{10,... | collective-permute-start | bytes 393224 | tf_op jit(solution)/shard_map/ppermute | solution.py:47
  54.7 0.7 fusion
  57.4 6.8 %collective-permute-done.14 = f32[256,256]{1,0:T(8,128)S(1)} collective-permute-done((f32[256,256]{1,0:T(8,128)S(1)}, f32[256,256]{1,0:T(8,128)S(1)}, u32[]{:S(2)}, u32[]{:S(2)}) %collective-permute-start.14) | collective-permute-done | bytes 262176 | tf_op jit(solution)/shard_map/ppermute | solution.py:47
  64.8 1.6 %collective-permute-start.15 = (f32[2,2,16,128]{3,2,1,0:T(8,128)S(1)}, f32[2,2,16,128]{3,2,1,0:T(8,128)S(1)}, u32[]{:S(2)}, u32[]{:S(2)}) collective-permute-start(f32[2,2,16,128]{3,2,1,0:T(8,128)S(1)} %pad_maximum_fusion.11), channel_id=1, source_target_pairs={{0,1},{1,0},{2,3},{3,2},{4,5},{5,4},{6,7},{7,6},{8,9},{9,8},{10,11... | collective-permute-start | bytes 98312 | tf_op jit(solution)/shard_map/ppermute | solution.py:47
  66.4 0.9 collective-permute-done.15
  67.7 2.2 %collective-permute-done.16 = f32[2,16,128]{2,1,0:T(8,128)S(1)} collective-permute-done((f32[2,16,128]{2,1,0:T(8,128)S(1)}, f32[2,16,128]{2,1,0:T(8,128)S(1)}, u32[]{:S(2)}, u32[]{:S(2)}) %collective-permute-start.16) | collective-permute-done | bytes 16416 | tf_op jit(solution)/shard_map/ppermute | solution.py:47
  70.1 17.3 %all_to_all.5 = bf16[32,2,2048]{2,1,0:T(2,128)(2,1)S(1)} all-to-all(bf16[32,2,2048]{2,1,0:T(2,128)(2,1)S(1)} %broadcast_in_dim.11), channel_id=1, replica_groups=mesh['demo'=32,'fsdp'=2,'sketch'=4] {'demo'}, dimensions={0} | all-to-all | bytes 524288 | tf_op jit(solution)/shard_map/all_to_all | solution.py:202
  88.4 3.8 %collective-permute-start.17 = (f32[2,40,128]{2,1,0:T(8,128)S(1)}, f32[2,40,128]{2,1,0:T(8,128)S(1)}, u32[]{:S(2)}, u32[]{:S(2)}) collective-permute-start(f32[2,40,128]{2,1,0:T(8,128)S(1)} %pad_maximum_fusion.9), channel_id=1, source_target_pairs={{0,1},{1,0},{2,3},{3,2},{4,5},{5,4},{6,7},{7,6},{8,9},{9,8},{10,11... | collective-permute-start | bytes 122888 | tf_op jit(solution)/shard_map/ppermute | solution.py:47
  92.2 0.9 collective-permute-done.17
  93.6 1.8 %collective-permute-start.19 = (f32[40,128]{1,0:T(8,128)S(1)}, f32[40,128]{1,0:T(8,128)S(1)}, u32[]{:S(2)}, u32[]{:S(2)}) collective-permute-start(f32[40,128]{1,0:T(8,128)S(1)} %get-tuple-element.40), channel_id=1, source_target_pairs={{0,4},{1,5},{2,6},{3,7},{4,0},{5,1},{6,2},{7,3},{8,12},{9,13},{10,... | collective-permute-start | bytes 61448 | tf_op jit(solution)/shard_map/ppermute | solution.py:47
  95.4 1.6 %collective-permute-start.20 = (f32[40,128]{1,0:T(8,128)S(1)}, f32[40,128]{1,0:T(8,128)S(1)}, u32[]{:S(2)}, u32[]{:S(2)}) collective-permute-start(f32[40,128]{1,0:T(8,128)S(1)} %get-tuple-element.39), channel_id=1, source_target_pairs={{0,6},{1,7},{2,4},{3,5},{4,2},{5,3},{6,0},{7,1},{8,14},{9,15},{10,... | collective-permute-start | bytes 61448 | tf_op jit(solution)/shard_map/ppermute | solution.py:47
  97.7 1.5 %collective-permute-done.20 = f32[40,128]{1,0:T(8,128)S(1)} collective-permute-done((f32[40,128]{1,0:T(8,128)S(1)}, f32[40,128]{1,0:T(8,128)S(1)}, u32[]{:S(2)}, u32[]{:S(2)}) %collective-permute-start.20) | collective-permute-done | bytes 20512 | tf_op jit(solution)/shard_map/ppermute | solution.py:47
  (88 shorter events, 11.8 us)
Async XLA Ops:
  0.0 0.8 copy-start
  2.3 9.2 %collective-permute-start = (bf16[14,2048]{1,0:T(8,128)(2,1)S(1)}, bf16[14,2048]{1,0:T(8,128)(2,1)S(1)}, u32[]{:S(2)}, u32[]{:S(2)}) collective-permute-start(bf16[14,2048]{1,0:T(8,128)(2,1)S(1)} %pad_add_fusion), channel_id=1, source_target_pairs={{0,8},{1,9},{2,10},{3,11},{4,12},{5,13},{6,14},{7,15},{8,16},{9,17... | collective-permute-start | bytes 172040 | tf_op jit(solution)/shard_map/ppermute | solution.py:47
  4.4 7.1 %collective-permute-start.1 = (bf16[14,2048]{1,0:T(8,128)(2,1)S(1)}, bf16[14,2048]{1,0:T(8,128)(2,1)S(1)}, u32[]{:S(2)}, u32[]{:S(2)}) collective-permute-start(bf16[14,2048]{1,0:T(8,128)(2,1)S(1)} %pad_add_fusion), channel_id=1, source_target_pairs={{0,16},{1,17},{2,18},{3,19},{4,20},{5,21},{6,22},{7,23},{8,24},{9,... | collective-permute-start | bytes 172040 | tf_op jit(solution)/shard_map/ppermute | solution.py:47
  6.9 4.7 %collective-permute-start.2 = (bf16[14,2048]{1,0:T(8,128)(2,1)S(1)}, bf16[14,2048]{1,0:T(8,128)(2,1)S(1)}, u32[]{:S(2)}, u32[]{:S(2)}) collective-permute-start(bf16[14,2048]{1,0:T(8,128)(2,1)S(1)} %pad_add_fusion), channel_id=1, source_target_pairs={{0,24},{1,25},{2,26},{3,27},{4,28},{5,29},{6,30},{7,31},{8,0},{9,1... | collective-permute-start | bytes 172040 | tf_op jit(solution)/shard_map/ppermute | solution.py:47
  11.6 10.1 %collective-permute-start.3 = (bf16[56,2048]{1,0:T(8,128)(2,1)S(1)}, bf16[56,2048]{1,0:T(8,128)(2,1)S(1)}, u32[]{:S(2)}, u32[]{:S(2)}) collective-permute-start(bf16[56,2048]{1,0:T(8,128)(2,1)S(1)} %pad_maximum_fusion.7), channel_id=1, source_target_pairs={{0,32},{1,33},{2,34},{3,35},{4,36},{5,37},{6,38},{7,39},{8,40},{9,... | collective-permute-start | bytes 688136 | tf_op jit(solution)/shard_map/ppermute | solution.py:47
  13.3 8.3 %collective-permute-start.5 = (bf16[56,2048]{1,0:T(8,128)(2,1)S(1)}, bf16[56,2048]{1,0:T(8,128)(2,1)S(1)}, u32[]{:S(2)}, u32[]{:S(2)}) collective-permute-start(bf16[56,2048]{1,0:T(8,128)(2,1)S(1)} %pad_maximum_fusion.7), channel_id=1, source_target_pairs={{0,224},{1,225},{2,226},{3,227},{4,228},{5,229},{6,230},{7,231},{8... | collective-permute-start | bytes 688136 | tf_op jit(solution)/shard_map/ppermute | solution.py:47
  21.7 6.1 %collective-permute-start.4 = (bf16[56,2048]{1,0:T(8,128)(2,1)S(1)}, bf16[56,2048]{1,0:T(8,128)(2,1)S(1)}, u32[]{:S(2)}, u32[]{:S(2)}) collective-permute-start(bf16[56,2048]{1,0:T(8,128)(2,1)S(1)} %collective-permute-done.3), channel_id=1, source_target_pairs={{0,32},{1,33},{2,34},{3,35},{4,36},{5,37},{6,38},{7,39},{8,40},{9,... | collective-permute-start | bytes 688136 | tf_op jit(solution)/shard_map/ppermute | solution.py:47
  21.7 6.1 %collective-permute-start.6 = (bf16[56,2048]{1,0:T(8,128)(2,1)S(1)}, bf16[56,2048]{1,0:T(8,128)(2,1)S(1)}, u32[]{:S(2)}, u32[]{:S(2)}) collective-permute-start(bf16[56,2048]{1,0:T(8,128)(2,1)S(1)} %collective-permute-done.5), channel_id=1, source_target_pairs={{0,224},{1,225},{2,226},{3,227},{4,228},{5,229},{6,230},{7,231},{8... | collective-permute-start | bytes 688136 | tf_op jit(solution)/shard_map/ppermute | solution.py:47
  27.8 6.8 %collective-permute-start.7 = (bf16[56,2048]{1,0:T(8,128)(2,1)S(1)}, bf16[56,2048]{1,0:T(8,128)(2,1)S(1)}, u32[]{:S(2)}, u32[]{:S(2)}) collective-permute-start(bf16[56,2048]{1,0:T(8,128)(2,1)S(1)} %collective-permute-done.4), channel_id=1, source_target_pairs={{0,32},{1,33},{2,34},{3,35},{4,36},{5,37},{6,38},{7,39},{8,40},{9,... | collective-permute-start | bytes 688136 | tf_op jit(solution)/shard_map/ppermute | solution.py:47
  27.8 6.9 %collective-permute-start.8 = (bf16[56,2048]{1,0:T(8,128)(2,1)S(1)}, bf16[56,2048]{1,0:T(8,128)(2,1)S(1)}, u32[]{:S(2)}, u32[]{:S(2)}) collective-permute-start(bf16[56,2048]{1,0:T(8,128)(2,1)S(1)} %collective-permute-done.6), channel_id=1, source_target_pairs={{0,224},{1,225},{2,226},{3,227},{4,228},{5,229},{6,230},{7,231},{8... | collective-permute-start | bytes 688136 | tf_op jit(solution)/shard_map/ppermute | solution.py:47
  30.6 14.4 %collective-permute-start.11 = (bf16[280,2048]{1,0:T(8,128)(2,1)S(1)}, bf16[280,2048]{1,0:T(8,128)(2,1)S(1)}, u32[]{:S(2)}, u32[]{:S(2)}) collective-permute-start(bf16[280,2048]{1,0:T(8,128)(2,1)S(1)} %get-tuple-element.21), channel_id=1, source_target_pairs={{0,1},{1,0},{2,3},{3,2},{4,5},{5,4},{6,7},{7,6},{8,9},{9,8},{10,11... | collective-permute-start | bytes 3440648 | tf_op jit(solution)/shard_map/ppermute | solution.py:47
  34.5 5.1 %collective-permute-start.9 = (bf16[32,2048]{1,0:T(8,128)(2,1)S(1)}, bf16[32,2048]{1,0:T(8,128)(2,1)S(1)}, u32[]{:S(2)}, u32[]{:S(2)}) collective-permute-start(bf16[32,2048]{1,0:T(8,128)(2,1)S(1)} %slice.52), channel_id=1, source_target_pairs={{0,32},{1,33},{2,34},{3,35},{4,36},{5,37},{6,38},{7,39},{8,40},{9,... | collective-permute-start | bytes 393224 | tf_op jit(solution)/shard_map/ppermute | solution.py:47
  34.7 4.4 %collective-permute-start.10 = (bf16[24,2048]{1,0:T(8,128)(2,1)S(1)}, bf16[24,2048]{1,0:T(8,128)(2,1)S(1)}, u32[]{:S(2)}, u32[]{:S(2)}) collective-permute-start(bf16[24,2048]{1,0:T(8,128)(2,1)S(1)} %slice.53), channel_id=1, source_target_pairs={{0,224},{1,225},{2,226},{3,227},{4,228},{5,229},{6,230},{7,231},{8... | collective-permute-start | bytes 294920 | tf_op jit(solution)/shard_map/ppermute | solution.py:47
  39.7 7.0 %collective-permute-start.12 = (bf16[168,2048]{1,0:T(8,128)(2,1)S(1)}, bf16[168,2048]{1,0:T(8,128)(2,1)S(1)}, u32[]{:S(2)}, u32[]{:S(2)}) collective-permute-start(bf16[168,2048]{1,0:T(8,128)(2,1)S(1)} %pad_maximum_fusion.4), channel_id=1, source_target_pairs={{0,1},{1,0},{2,3},{3,2},{4,5},{5,4},{6,7},{7,6},{8,9},{9,8},{10,11... | collective-permute-start | bytes 2064392 | tf_op jit(solution)/shard_map/ppermute | solution.py:47
  44.9 1.8 %copy-start.5 = (bf16[384,448]{1,0:T(8,128)(2,1)S(1)}, bf16[384,448]{1,0:T(8,128)(2,1)}, u32[]{:S(2)}) copy-start(bf16[384,448]{1,0:T(8,128)(2,1)} %get-tuple-element.14) | copy-start | bytes 1032196
  48.1 2.2 %copy-start.4 = (bf16[4,128,4096]{2,1,0:T(8,128)(2,1)S(1)}, bf16[4,128,4096]{2,1,0:T(8,128)(2,1)}, u32[]{:S(2)}) copy-start(bf16[4,128,4096]{2,1,0:T(8,128)(2,1)} %param.10) | copy-start | bytes 12582916
  48.7 5.3 %copy-start.3 = (bf16[4,128,4096]{2,1,0:T(8,128)(2,1)S(1)}, bf16[4,128,4096]{2,1,0:T(8,128)(2,1)}, u32[]{:S(2)}) copy-start(bf16[4,128,4096]{2,1,0:T(8,128)(2,1)} %param.11) | copy-start | bytes 12582916
  51.0 6.3 %collective-permute-start.13 = (f32[256,128]{1,0:T(8,128)S(1)}, f32[256,128]{1,0:T(8,128)S(1)}, u32[]{:S(2)}, u32[]{:S(2)}) collective-permute-start(f32[256,128]{1,0:T(8,128)S(1)} %fusion.2), channel_id=1, source_target_pairs={{0,4},{1,5},{2,6},{3,7},{4,0},{5,1},{6,2},{7,3},{8,12},{9,13},{10,... | collective-permute-start | bytes 393224 | tf_op jit(solution)/shard_map/ppermute | solution.py:47
  55.5 8.8 %collective-permute-start.14 = (f32[256,256]{1,0:T(8,128)S(1)}, f32[256,256]{1,0:T(8,128)S(1)}, u32[]{:S(2)}, u32[]{:S(2)}) collective-permute-start(f32[256,256]{1,0:T(8,128)S(1)} %fusion), channel_id=1, source_target_pairs={{0,4},{1,5},{2,6},{3,7},{4,0},{5,1},{6,2},{7,3},{8,12},{9,13},{10,... | collective-permute-start | bytes 786440 | tf_op jit(solution)/shard_map/ppermute | solution.py:47
  57.3 30.2 %copy-start.1 = (bf16[128,2048]{1,0:T(8,128)(2,1)S(1)}, bf16[128,2048]{1,0:T(8,128)(2,1)}, u32[]{:S(2)}) copy-start(bf16[128,2048]{1,0:T(8,128)(2,1)} %queries_ref.1) | copy-start | bytes 1572868
  64.3 24.0 %copy-start.2 = (f32[8,128]{1,0:T(8,128)S(1)}, f32[8,128]{1,0:T(8,128)}, u32[]{:S(2)}) copy-start(f32[8,128]{1,0:T(8,128)} %get-tuple-element.18) | copy-start | bytes 12292
  64.8 2.5 %collective-permute-start.15 = (f32[2,2,16,128]{3,2,1,0:T(8,128)S(1)}, f32[2,2,16,128]{3,2,1,0:T(8,128)S(1)}, u32[]{:S(2)}, u32[]{:S(2)}) collective-permute-start(f32[2,2,16,128]{3,2,1,0:T(8,128)S(1)} %pad_maximum_fusion.11), channel_id=1, source_target_pairs={{0,1},{1,0},{2,3},{3,2},{4,5},{5,4},{6,7},{7,6},{8,9},{9,8},{10,11... | collective-permute-start | bytes 98312 | tf_op jit(solution)/shard_map/ppermute | solution.py:47
  67.2 2.7 %collective-permute-start.16 = (f32[2,16,128]{2,1,0:T(8,128)S(1)}, f32[2,16,128]{2,1,0:T(8,128)S(1)}, u32[]{:S(2)}, u32[]{:S(2)}) collective-permute-start(f32[2,16,128]{2,1,0:T(8,128)S(1)} %slice_bitcast_fusion.2), channel_id=1, source_target_pairs={{0,2},{1,3},{2,0},{3,1},{4,6},{5,7},{6,4},{7,5},{8,10},{9,11},{10,... | collective-permute-start | bytes 49160 | tf_op jit(solution)/shard_map/ppermute | solution.py:47
  88.4 4.7 %collective-permute-start.17 = (f32[2,40,128]{2,1,0:T(8,128)S(1)}, f32[2,40,128]{2,1,0:T(8,128)S(1)}, u32[]{:S(2)}, u32[]{:S(2)}) collective-permute-start(f32[2,40,128]{2,1,0:T(8,128)S(1)} %pad_maximum_fusion.9), channel_id=1, source_target_pairs={{0,1},{1,0},{2,3},{3,2},{4,5},{5,4},{6,7},{7,6},{8,9},{9,8},{10,11... | collective-permute-start | bytes 122888 | tf_op jit(solution)/shard_map/ppermute | solution.py:47
  93.1 3.9 %collective-permute-start.18 = (f32[40,128]{1,0:T(8,128)S(1)}, f32[40,128]{1,0:T(8,128)S(1)}, u32[]{:S(2)}, u32[]{:S(2)}) collective-permute-start(f32[40,128]{1,0:T(8,128)S(1)} %get-tuple-element.39), channel_id=1, source_target_pairs={{0,2},{1,3},{2,0},{3,1},{4,6},{5,7},{6,4},{7,5},{8,10},{9,11},{10,... | collective-permute-start | bytes 61448 | tf_op jit(solution)/shard_map/ppermute | solution.py:47
  93.6 4.1 %collective-permute-start.19 = (f32[40,128]{1,0:T(8,128)S(1)}, f32[40,128]{1,0:T(8,128)S(1)}, u32[]{:S(2)}, u32[]{:S(2)}) collective-permute-start(f32[40,128]{1,0:T(8,128)S(1)} %get-tuple-element.40), channel_id=1, source_target_pairs={{0,4},{1,5},{2,6},{3,7},{4,0},{5,1},{6,2},{7,3},{8,12},{9,13},{10,... | collective-permute-start | bytes 61448 | tf_op jit(solution)/shard_map/ppermute | solution.py:47
  95.4 3.8 %collective-permute-start.20 = (f32[40,128]{1,0:T(8,128)S(1)}, f32[40,128]{1,0:T(8,128)S(1)}, u32[]{:S(2)}, u32[]{:S(2)}) collective-permute-start(f32[40,128]{1,0:T(8,128)S(1)} %get-tuple-element.39), channel_id=1, source_target_pairs={{0,6},{1,7},{2,4},{3,5},{4,2},{5,3},{6,0},{7,1},{8,14},{9,15},{10,... | collective-permute-start | bytes 61448 | tf_op jit(solution)/shard_map/ppermute | solution.py:47
